TPU v7x, 32 devices: a whole 2x2x4 slice. The times are simulated.
32 devices in a mesh: sen: 16 (over z, y, x), par: 2 (over core).
Axes of the slice: x: 2, y: 2, z: 4, core: 2. Of those that a mesh axis runs over, the one named last changes fastest.
Arguments:
- vectors: float32 [2, 128, 256], P(None, 'sen'), may hold values from -6 to 6
- observed: float32 [2, 128, 256], P(None, 'sen'), may hold values from -6 to 6
- operator: bfloat16 [2, 128, 128, 768], P(None, None, 'sen', 'par'), may hold values from -0.4375 to 0.4375
- noise: float32 [128], P('sen'), may hold values from 0.3 to 3
- coefficient: float32 [2, 384], P('par'), may hold values from 0.05 to 0.24
- offsets: int32 [2, 384], P('par'), may hold values from -3 to 3
Outputs:
- residual: float32 [2, 128, 256], P(None, 'sen')
- applied: float32 [2, 128, 256], P(None, 'sen')
All inputs are finite; a program needn't handle non-finite values.
Results may differ from a plain program's by a relative error of at most 0.0018.
Values may be sent and summed in bfloat16 or wider, within the bound.
No kernel may reach another device: no remote copies, remote signals or barrier semaphores. Data moves between devices by JAX's collectives and lax.ppermute only.
A program may use at most 64 MiB of HBM per device.

v0:
```python
import math

import jax
import jax.numpy as jnp
from jax import lax
from jax.sharding import PartitionSpec as P

SWEEPS = 4


def padded_2(cells, sides, width):
    for axis, dim in sides:
        count = lax.axis_size(axis)
        ends = count - 1
        head = lax.slice_in_dim(cells, 0, width, axis=dim)
        tail = lax.slice_in_dim(cells, cells.shape[dim] - width, cells.shape[dim], axis=dim)
        cells = jnp.concatenate(
            [
                lax.ppermute(tail, axis, [(i, (i + 1) % count) for i in range(ends)]),
                cells,
                lax.ppermute(head, axis, [((i + 1) % count, i) for i in range(ends)]),
            ],
            axis=dim,
        )
    return cells


def make_basis(length):
    half = length // 2
    times = jnp.arange(length, dtype=jnp.int32)[:, None]
    freqs = jnp.arange(half, dtype=jnp.int32)[None, :]
    phase = (2 * freqs + 1) * times % (2 * length)
    angle = phase.astype(jnp.float32) * (math.pi / length)
    scale = math.sqrt(2.0 / length)
    return jnp.concatenate([jnp.cos(angle), jnp.sin(angle)], axis=1) * scale


def sweep_once(field, padded, coefficient, offsets):
    width = field.shape[-1]
    upper = padded[..., :-2, :]
    lower = padded[..., 2:, :]
    lower_pad = jnp.pad(lower, ((0, 0), (0, 0), (0, 0), (0, 0), (3, 3)))
    linked = jnp.zeros_like(field)
    for shift in range(-3, 4):
        linked = linked + jnp.where(
            offsets == shift, lower_pad[..., 3 + shift : 3 + shift + width], 0.0
        )
    sides = jnp.pad(field, ((0, 0), (0, 0), (0, 0), (0, 0), (1, 1)))
    return field + coefficient * (sides[..., :-2] + sides[..., 2:] + upper + linked - 4.0 * field)


def smooth(field, coefficient, offsets, extend):
    for sweep in range(SWEEPS):
        field = sweep_once(field, extend(field), coefficient, offsets)
    return field


def forward_part(operator, piece):
    count = piece.shape[1]
    rows = piece.shape[2]
    flat = piece.reshape(2, count, rows, piece.shape[3] * piece.shape[4])
    real = jnp.einsum(
        "fsp,frp->frs", operator[0], flat[0], preferred_element_type=jnp.float32
    ) - jnp.einsum("fsp,frp->frs", operator[1], flat[1], preferred_element_type=jnp.float32)
    imag = jnp.einsum(
        "fsp,frp->frs", operator[0], flat[1], preferred_element_type=jnp.float32
    ) + jnp.einsum("fsp,frp->frs", operator[1], flat[0], preferred_element_type=jnp.float32)
    return jnp.stack([real, imag])


def extend_whole(field):
    return padded_2(field, (("par", 3),), 1)


def hessian(record, operator, noise, coefficient, offsets, basis):
    rows, sensors, length = record.shape
    half = length // 2
    grid_rows, width = coefficient.shape
    spectrum = jnp.dot(
        record.reshape(rows * sensors, length), basis, precision=lax.Precision.HIGHEST
    )
    spectrum = spectrum.reshape(rows, sensors, 2, half).transpose(2, 3, 0, 1).astype(jnp.bfloat16)
    real = jnp.einsum(
        "frs,fsp->frp", spectrum[0], operator[0], preferred_element_type=jnp.float32
    ) + jnp.einsum("frs,fsp->frp", spectrum[1], operator[1], preferred_element_type=jnp.float32)
    imag = jnp.einsum(
        "frs,fsp->frp", spectrum[1], operator[0], preferred_element_type=jnp.float32
    ) - jnp.einsum("frs,fsp->frp", spectrum[0], operator[1], preferred_element_type=jnp.float32)
    partial_value = jnp.stack([real, imag]).reshape(2, half, rows, grid_rows, width)
    adjoint = lax.psum(partial_value, "sen")
    smoothed = smooth(adjoint, coefficient, offsets, extend_whole)
    prior = smoothed.astype(jnp.bfloat16)
    forward = forward_part(operator, prior)
    forward = lax.psum(forward, "par")
    forward = forward.transpose(2, 3, 0, 1).reshape(rows * sensors, length)
    back = jnp.dot(forward, basis.T, precision=lax.Precision.HIGHEST).reshape(rows, sensors, length)
    return back + noise[None, :, None] * record


def body(vectors, observed, operator, noise, coefficient, offsets):
    basis = make_basis(vectors.shape[-1])
    residual = observed - hessian(vectors, operator, noise, coefficient, offsets, basis)
    applied = hessian(residual, operator, noise, coefficient, offsets, basis)
    return (residual, applied)


def solution(mesh):
    placed = (
        P(None, "sen", None),
        P(None, "sen", None),
        P(None, None, "sen", "par"),
        P("sen"),
        P("par", None),
        P("par", None),
    )
    return jax.shard_map(
        body,
        mesh=mesh,
        in_specs=placed,
        out_specs=(P(None, "sen", None), P(None, "sen", None)),
        check_vma=False,
    )
```

profile of v0, /device:TPU:0, one launch (start us, length us, event | category | flops | bytes accessed | tf_op | source)
XLA Modules:
  0.0 368.6 jit_solution(9380100295818304024)
XLA Ops:
  13.1 113.1 %all-reduce.19.cloned.1.call-done = f32[2,128,2,1,384]{4,2,1,0,3:T(2,128)} async-done(((f32[2,128,2,1,384]{4,2,1,0,3:T(2,128)}), f32[2,128,2,1,384]{4,2,1,0,3:T(2,128)}) %all-reduce.19.cloned.1.call-update) | async-done | bytes 786448 | tf_op jit(solution)/shard_map/psum | solution.py:90
  129.6 2.3 collective-permute-done.1
  131.9 8.0 %multiply_add_fusion.5 = f32[2,128,2,1,384]{4,2,1,0,3:T(2,128)S(1)} fusion(f32[2,128,2,1,384]{4,2,1,0,3:T(2,128)} %all-reduce.19.cloned.1.call-done, f32[2,128,2,1,384]{4,2,1,0,3:T(2,128)S(1)} %collective-permute-done, f32[2,128,2,1,384]{4,2,1,0,3:T(2,128)S(1)} %collective-permute-done.1, pred[384]{0:T(512)(128)(4,1)S(1)} %get-tuple-element.7, ...), kind=kLoop, calls=%fused_computation.138 | loop fusion | flops 3932160 | bytes 3149952 | tf_op jit(solution)/shard_map/add | solution.py:49
  140.0 2.1 collective-permute-start.2
  143.9 2.3 collective-permute-done.3
  146.3 6.8 %multiply_add_fusion.4 = f32[2,128,2,1,384]{4,2,1,0,3:T(2,128)S(1)} fusion(f32[2,128,2,1,384]{4,2,1,0,3:T(2,128)S(1)} %multiply_add_fusion.5, f32[2,128,2,1,384]{4,2,1,0,3:T(2,128)S(1)} %collective-permute-done.2, f32[2,128,2,1,384]{4,2,1,0,3:T(2,128)S(1)} %collective-permute-done.3, pred[384]{0:T(512)(128)(4,1)S(1)} %get-tuple-element.7, ...), kind=kLoop, calls=%fused_computation.132 | loop fusion | flops 3932160 | bytes 3149952 | tf_op jit(solution)/shard_map/add | solution.py:49
  153.1 2.1 collective-permute-start.4
  157.0 2.3 collective-permute-done.5
  159.4 6.8 %multiply_add_fusion.3 = f32[2,128,2,1,384]{4,2,1,0,3:T(2,128)S(1)} fusion(f32[2,128,2,1,384]{4,2,1,0,3:T(2,128)S(1)} %multiply_add_fusion.4, f32[2,128,2,1,384]{4,2,1,0,3:T(2,128)S(1)} %collective-permute-done.4, f32[2,128,2,1,384]{4,2,1,0,3:T(2,128)S(1)} %collective-permute-done.5, pred[384]{0:T(512)(128)(4,1)S(1)} %get-tuple-element.7, ...), kind=kLoop, calls=%fused_computation.126 | loop fusion | flops 3932160 | bytes 3149952 | tf_op jit(solution)/shard_map/add | solution.py:49
  166.2 2.9 collective-permute-start.6
  170.7 2.7 collective-permute-done.7
  173.4 9.9 %add_convert_fusion.1 = bf16[2,128,2,1,384]{4,2,1,0,3:T(2,128)(2,1)S(1)} fusion(f32[2,128,2,1,384]{4,2,1,0,3:T(2,128)S(1)} %multiply_add_fusion.3, f32[2,128,2,1,384]{4,2,1,0,3:T(2,128)} %collective-permute-done.6, f32[2,128,2,1,384]{4,2,1,0,3:T(2,128)} %collective-permute-done.7, pred[384]{0:T(512)(128)(4,1)S(1)} %get-tuple-element.7, ...), kind=kLoop, calls=%fused_computation.120 | loop fusion | flops 4128768 | bytes 2756736 | tf_op jit(solution)/shard_map/convert_element_type | solution.py:92
  185.5 3.4 psum.29
  192.8 109.4 %all-reduce.21.cloned.1.call-done = f32[2,128,2,1,384]{4,2,1,0,3:T(2,128)} async-done(((f32[2,128,2,1,384]{4,2,1,0,3:T(2,128)}), f32[2,128,2,1,384]{4,2,1,0,3:T(2,128)}) %all-reduce.21.cloned.1.call-update) | async-done | bytes 786448 | tf_op jit(solution)/shard_map/psum | solution.py:90
  305.6 2.3 collective-permute-done.9
  307.9 8.0 %multiply_add_fusion.2 = f32[2,128,2,1,384]{4,2,1,0,3:T(2,128)S(1)} fusion(f32[2,128,2,1,384]{4,2,1,0,3:T(2,128)} %all-reduce.21.cloned.1.call-done, f32[2,128,2,1,384]{4,2,1,0,3:T(2,128)S(1)} %collective-permute-done.8, f32[2,128,2,1,384]{4,2,1,0,3:T(2,128)S(1)} %collective-permute-done.9, pred[384]{0:T(512)(128)(4,1)S(1)} %get-tuple-element.7, ...), kind=kLoop, calls=%fused_computation.114 | loop fusion | flops 3932160 | bytes 3149952 | tf_op jit(solution)/shard_map/add | solution.py:49
  316.0 2.1 collective-permute-start.10
  319.9 2.3 collective-permute-done.11
  322.3 6.8 %multiply_add_fusion.1 = f32[2,128,2,1,384]{4,2,1,0,3:T(2,128)S(1)} fusion(f32[2,128,2,1,384]{4,2,1,0,3:T(2,128)S(1)} %multiply_add_fusion.2, f32[2,128,2,1,384]{4,2,1,0,3:T(2,128)S(1)} %collective-permute-done.10, f32[2,128,2,1,384]{4,2,1,0,3:T(2,128)S(1)} %collective-permute-done.11, pred[384]{0:T(512)(128)(4,1)S(1)} %get-tuple-element.7, ...), kind=kLoop, calls=%fused_computation.108 | loop fusion | flops 3932160 | bytes 3149952 | tf_op jit(solution)/shard_map/add | solution.py:49
  333.0 2.3 collective-permute-done.13
  335.4 6.8 %multiply_add_fusion = f32[2,128,2,1,384]{4,2,1,0,3:T(2,128)S(1)} fusion(f32[2,128,2,1,384]{4,2,1,0,3:T(2,128)S(1)} %multiply_add_fusion.1, f32[2,128,2,1,384]{4,2,1,0,3:T(2,128)S(1)} %collective-permute-done.12, f32[2,128,2,1,384]{4,2,1,0,3:T(2,128)S(1)} %collective-permute-done.13, pred[384]{0:T(512)(128)(4,1)S(1)} %get-tuple-element.7, ...), kind=kLoop, calls=%fused_computation.102 | loop fusion | flops 3932160 | bytes 3149952 | tf_op jit(solution)/shard_map/add | solution.py:49
  346.1 2.3 collective-permute-done.15
  348.5 6.8 %add_convert_fusion = bf16[2,128,2,1,384]{4,2,1,0,3:T(2,128)(2,1)S(1)} fusion(f32[2,128,2,1,384]{4,2,1,0,3:T(2,128)S(1)} %multiply_add_fusion, f32[2,128,2,1,384]{4,2,1,0,3:T(2,128)S(1)} %collective-permute-done.14, f32[2,128,2,1,384]{4,2,1,0,3:T(2,128)S(1)} %collective-permute-done.15, pred[384]{0:T(512)(128)(4,1)S(1)} %get-tuple-element.7, ...), kind=kLoop, calls=%fused_computation.96 | loop fusion | flops 4128768 | bytes 2756736 | tf_op jit(solution)/shard_map/convert_element_type | solution.py:92
  357.5 3.4 psum.31
  (76 shorter events, 36.8 us)
Async XLA Ops:
  7.2 119.0 %all-reduce.19.cloned.1.call-start = ((), (), s32[]{:S(2)}) async-start(), calls=%async_computation | async-start | bytes 1572864 | tf_op jit(solution)/shard_map/psum | solution.py:90
  11.8 117.1 %copy-start.5 = (f32[1,384]{1,0:T(1,128)S(1)}, f32[1,384]{1,0:T(1,128)}, u32[]{:S(2)}) copy-start(f32[1,384]{1,0:T(1,128)} %param.10) | copy-start | bytes 4612
  11.8 117.1 %copy-start.6 = (s32[1,384]{1,0:T(1,128)S(1)}, s32[1,384]{1,0:T(1,128)}, u32[]{:S(2)}) copy-start(s32[1,384]{1,0:T(1,128)} %param.11) | copy-start | bytes 4612
  13.1 289.1 %all-reduce.21.cloned.1.call-start = ((), (), s32[]{:S(2)}) async-start(), calls=%async_computation.1 | async-start | bytes 1572864 | tf_op jit(solution)/shard_map/psum | solution.py:90
  126.2 3.4 collective-permute-start
  127.5 4.4 %collective-permute-start.1 = (f32[2,128,2,1,384]{4,2,1,0,3:T(2,128)}, f32[2,128,2,1,384]{4,2,1,0,3:T(2,128)S(1)}, u32[]{:S(2)}, u32[]{:S(2)}) collective-permute-start(f32[2,128,2,1,384]{4,2,1,0,3:T(2,128)} %all-reduce.19.cloned.1.call-done), channel_id=1, source_target_pairs={{1,0},{3,2},{5,4},{7,6},{9,8},{11,10},{13,12},{15,14},{17,16},{19,... | collective-permute-start | bytes 2359304 | tf_op jit(solution)/shard_map/ppermute | solution.py:21
  140.0 3.9 %collective-permute-start.2 = (f32[2,128,2,1,384]{4,2,1,0,3:T(2,128)S(1)}, f32[2,128,2,1,384]{4,2,1,0,3:T(2,128)S(1)}, u32[]{:S(2)}, u32[]{:S(2)}) collective-permute-start(f32[2,128,2,1,384]{4,2,1,0,3:T(2,128)S(1)} %multiply_add_fusion.5), channel_id=1, source_target_pairs={{0,1},{2,3},{4,5},{6,7},{8,9},{10,11},{12,13},{14,15},{16,17},{18,... | collective-permute-start | bytes 2359304 | tf_op jit(solution)/shard_map/ppermute | solution.py:19
  142.1 4.2 %collective-permute-start.3 = (f32[2,128,2,1,384]{4,2,1,0,3:T(2,128)S(1)}, f32[2,128,2,1,384]{4,2,1,0,3:T(2,128)S(1)}, u32[]{:S(2)}, u32[]{:S(2)}) collective-permute-start(f32[2,128,2,1,384]{4,2,1,0,3:T(2,128)S(1)} %multiply_add_fusion.5), channel_id=1, source_target_pairs={{1,0},{3,2},{5,4},{7,6},{9,8},{11,10},{13,12},{15,14},{17,16},{19,... | collective-permute-start | bytes 2359304 | tf_op jit(solution)/shard_map/ppermute | solution.py:21
  153.1 3.9 %collective-permute-start.4 = (f32[2,128,2,1,384]{4,2,1,0,3:T(2,128)S(1)}, f32[2,128,2,1,384]{4,2,1,0,3:T(2,128)S(1)}, u32[]{:S(2)}, u32[]{:S(2)}) collective-permute-start(f32[2,128,2,1,384]{4,2,1,0,3:T(2,128)S(1)} %multiply_add_fusion.4), channel_id=1, source_target_pairs={{0,1},{2,3},{4,5},{6,7},{8,9},{10,11},{12,13},{14,15},{16,17},{18,... | collective-permute-start | bytes 2359304 | tf_op jit(solution)/shard_map/ppermute | solution.py:19
  155.2 4.2 %collective-permute-start.5 = (f32[2,128,2,1,384]{4,2,1,0,3:T(2,128)S(1)}, f32[2,128,2,1,384]{4,2,1,0,3:T(2,128)S(1)}, u32[]{:S(2)}, u32[]{:S(2)}) collective-permute-start(f32[2,128,2,1,384]{4,2,1,0,3:T(2,128)S(1)} %multiply_add_fusion.4), channel_id=1, source_target_pairs={{1,0},{3,2},{5,4},{7,6},{9,8},{11,10},{13,12},{15,14},{17,16},{19,... | collective-permute-start | bytes 2359304 | tf_op jit(solution)/shard_map/ppermute | solution.py:21
  166.2 4.6 %collective-permute-start.6 = (f32[2,128,2,1,384]{4,2,1,0,3:T(2,128)S(1)}, f32[2,128,2,1,384]{4,2,1,0,3:T(2,128)}, u32[]{:S(2)}, u32[]{:S(2)}) collective-permute-start(f32[2,128,2,1,384]{4,2,1,0,3:T(2,128)S(1)} %multiply_add_fusion.3), channel_id=1, source_target_pairs={{0,1},{2,3},{4,5},{6,7},{8,9},{10,11},{12,13},{14,15},{16,17},{18,... | collective-permute-start | bytes 2359304 | tf_op jit(solution)/shard_map/ppermute | solution.py:19
  169.1 4.3 %collective-permute-start.7 = (f32[2,128,2,1,384]{4,2,1,0,3:T(2,128)S(1)}, f32[2,128,2,1,384]{4,2,1,0,3:T(2,128)}, u32[]{:S(2)}, u32[]{:S(2)}) collective-permute-start(f32[2,128,2,1,384]{4,2,1,0,3:T(2,128)S(1)} %multiply_add_fusion.3), channel_id=1, source_target_pairs={{1,0},{3,2},{5,4},{7,6},{9,8},{11,10},{13,12},{15,14},{17,16},{19,... | collective-permute-start | bytes 2359304 | tf_op jit(solution)/shard_map/ppermute | solution.py:21
  184.9 4.0 %copy-start.2 = (f32[2,8,256]{2,1,0:T(8,128)S(1)}, f32[2,8,256]{2,1,0:T(8,128)}, u32[]{:S(2)}) copy-start(f32[2,8,256]{2,1,0:T(8,128)} %param.6) | copy-start | bytes 49156
  184.9 4.0 %copy-start.3 = (f32[2,8,256]{2,1,0:T(8,128)S(1)}, f32[2,8,256]{2,1,0:T(8,128)}, u32[]{:S(2)}) copy-start(f32[2,8,256]{2,1,0:T(8,128)} %param.7) | copy-start | bytes 49156
  184.9 4.0 %copy-start.4 = (f32[8]{0:T(128)S(1)}, f32[8]{0:T(128)}, u32[]{:S(2)}) copy-start(f32[8]{0:T(128)} %param.9) | copy-start | bytes 100
  189.2 171.6 %copy-start.1 = (f32[2,8,256]{2,1,0:T(8,128)}, f32[2,8,256]{2,1,0:T(8,128)S(1)}, u32[]{:S(2)}) copy-start(f32[2,8,256]{2,1,0:T(8,128)S(1)} %fusion.8) | copy-start | bytes 49156
  302.2 3.4 collective-permute-start.8
  303.6 4.4 %collective-permute-start.9 = (f32[2,128,2,1,384]{4,2,1,0,3:T(2,128)}, f32[2,128,2,1,384]{4,2,1,0,3:T(2,128)S(1)}, u32[]{:S(2)}, u32[]{:S(2)}) collective-permute-start(f32[2,128,2,1,384]{4,2,1,0,3:T(2,128)} %all-reduce.21.cloned.1.call-done), channel_id=1, source_target_pairs={{1,0},{3,2},{5,4},{7,6},{9,8},{11,10},{13,12},{15,14},{17,16},{19,... | collective-permute-start | bytes 2359304 | tf_op jit(solution)/shard_map/ppermute | solution.py:21
  316.0 3.9 %collective-permute-start.10 = (f32[2,128,2,1,384]{4,2,1,0,3:T(2,128)S(1)}, f32[2,128,2,1,384]{4,2,1,0,3:T(2,128)S(1)}, u32[]{:S(2)}, u32[]{:S(2)}) collective-permute-start(f32[2,128,2,1,384]{4,2,1,0,3:T(2,128)S(1)} %multiply_add_fusion.2), channel_id=1, source_target_pairs={{0,1},{2,3},{4,5},{6,7},{8,9},{10,11},{12,13},{14,15},{16,17},{18,... | collective-permute-start | bytes 2359304 | tf_op jit(solution)/shard_map/ppermute | solution.py:19
  318.1 4.2 %collective-permute-start.11 = (f32[2,128,2,1,384]{4,2,1,0,3:T(2,128)S(1)}, f32[2,128,2,1,384]{4,2,1,0,3:T(2,128)S(1)}, u32[]{:S(2)}, u32[]{:S(2)}) collective-permute-start(f32[2,128,2,1,384]{4,2,1,0,3:T(2,128)S(1)} %multiply_add_fusion.2), channel_id=1, source_target_pairs={{1,0},{3,2},{5,4},{7,6},{9,8},{11,10},{13,12},{15,14},{17,16},{19,... | collective-permute-start | bytes 2359304 | tf_op jit(solution)/shard_map/ppermute | solution.py:21
  329.1 3.9 %collective-permute-start.12 = (f32[2,128,2,1,384]{4,2,1,0,3:T(2,128)S(1)}, f32[2,128,2,1,384]{4,2,1,0,3:T(2,128)S(1)}, u32[]{:S(2)}, u32[]{:S(2)}) collective-permute-start(f32[2,128,2,1,384]{4,2,1,0,3:T(2,128)S(1)} %multiply_add_fusion.1), channel_id=1, source_target_pairs={{0,1},{2,3},{4,5},{6,7},{8,9},{10,11},{12,13},{14,15},{16,17},{18,... | collective-permute-start | bytes 2359304 | tf_op jit(solution)/shard_map/ppermute | solution.py:19
  331.2 4.2 %collective-permute-start.13 = (f32[2,128,2,1,384]{4,2,1,0,3:T(2,128)S(1)}, f32[2,128,2,1,384]{4,2,1,0,3:T(2,128)S(1)}, u32[]{:S(2)}, u32[]{:S(2)}) collective-permute-start(f32[2,128,2,1,384]{4,2,1,0,3:T(2,128)S(1)} %multiply_add_fusion.1), channel_id=1, source_target_pairs={{1,0},{3,2},{5,4},{7,6},{9,8},{11,10},{13,12},{15,14},{17,16},{19,... | collective-permute-start | bytes 2359304 | tf_op jit(solution)/shard_map/ppermute | solution.py:21
  342.2 3.9 %collective-permute-start.14 = (f32[2,128,2,1,384]{4,2,1,0,3:T(2,128)S(1)}, f32[2,128,2,1,384]{4,2,1,0,3:T(2,128)S(1)}, u32[]{:S(2)}, u32[]{:S(2)}) collective-permute-start(f32[2,128,2,1,384]{4,2,1,0,3:T(2,128)S(1)} %multiply_add_fusion), channel_id=1, source_target_pairs={{0,1},{2,3},{4,5},{6,7},{8,9},{10,11},{12,13},{14,15},{16,17},{18,... | collective-permute-start | bytes 2359304 | tf_op jit(solution)/shard_map/ppermute | solution.py:19
  344.3 4.2 %collective-permute-start.15 = (f32[2,128,2,1,384]{4,2,1,0,3:T(2,128)S(1)}, f32[2,128,2,1,384]{4,2,1,0,3:T(2,128)S(1)}, u32[]{:S(2)}, u32[]{:S(2)}) collective-permute-start(f32[2,128,2,1,384]{4,2,1,0,3:T(2,128)S(1)} %multiply_add_fusion), channel_id=1, source_target_pairs={{1,0},{3,2},{5,4},{7,6},{9,8},{11,10},{13,12},{15,14},{17,16},{19,... | collective-permute-start | bytes 2359304 | tf_op jit(solution)/shard_map/ppermute | solution.py:21
  (1 other events, 3.3 us)
Sparse Core Ops, SparseCore 0:
  13.2 112.9 all-reduce.18
  192.9 109.2 all-reduce.20
where the time goes:
time: 369 us
  waiting for transfers between devices  245 us (66%)
  other arithmetic  63.2 us (17%)
  starting transfers between devices  26.8 us (7%)
  between operations  14.5 us (4%)
  matrix products  11.1 us (3%)
  blocking collectives  6.73 us (2%)
    psum x2, waiting for transfers between devices, hessian(): adjoint = lax.psum(partial_value, 'sen')  222 us
    add x6, other arithmetic, sweep_once(): field + coefficient * (sides[..., :-2] + sides[..., 2:] + upper + linked...  43.3 us
    ppermute x8, waiting for transfers between devices, padded_2(): lax.ppermute(head, axis, [((i + 1) % count, i) for i in range(ends)])  19 us
    convert_element_type x2, other arithmetic, hessian(): prior = smoothed.astype(jnp.bfloat16)  16.7 us
    ppermute x8, starting transfers between devices, padded_2(): lax.ppermute(tail, axis, [(i, (i + 1) % count) for i in range(ends)])  16 us
    ppermute x8, starting transfers between devices, padded_2(): lax.ppermute(head, axis, [((i + 1) % count, i) for i in range(ends)])  10.7 us
  transfers between devices with their start and end apart: 18, of which 17 were waited for; matrix products, arithmetic and copies ran while one was open for 0% of the time, Pallas kernels for 0%

commit v1 on v0

v1 whole, which is shorter than its diff:
```python
import math

import jax
import jax.numpy as jnp
import numpy as np
from jax import lax
from jax.sharding import PartitionSpec as P

SWEEPS = 4
REACH = 3


def make_basis(length):
    half = length // 2
    times = np.arange(length)[:, None]
    freqs = np.arange(half)[None, :]
    phase = (2 * freqs + 1) * times % (2 * length)
    angle = phase.astype(np.float64) * (math.pi / length)
    scale = math.sqrt(2.0 / length)
    return (np.concatenate([np.cos(angle), np.sin(angle)], axis=1) * scale).astype(np.float32)


def halo(field, axis, dim):
    count = lax.axis_size(axis)
    if count == 1:
        edge = jnp.zeros_like(lax.slice_in_dim(field, 0, 1, axis=dim))
        return jnp.concatenate([edge, field, edge], axis=dim)
    ends = count - 1
    head = lax.slice_in_dim(field, 0, 1, axis=dim)
    tail = lax.slice_in_dim(field, field.shape[dim] - 1, field.shape[dim], axis=dim)
    return jnp.concatenate(
        [
            lax.ppermute(tail, axis, [(i, i + 1) for i in range(ends)]),
            field,
            lax.ppermute(head, axis, [(i + 1, i) for i in range(ends)]),
        ],
        axis=dim,
    )


def zero_halo(field):
    return jnp.pad(field, [(0, 0)] * (field.ndim - 2) + [(1, 1), (0, 0)])


def smooth(field, coefficient, offsets, extend):
    width = field.shape[-1]
    lead = [(0, 0)] * (field.ndim - 1)
    for _ in range(SWEEPS):
        padded = extend(field)
        upper = padded[..., :-2, :]
        lower = jnp.pad(padded[..., 2:, :], lead + [(REACH, REACH)])
        linked = jnp.zeros_like(field)
        for shift in range(-REACH, REACH + 1):
            start = REACH + shift
            linked = linked + jnp.where(offsets == shift, lower[..., start : start + width], 0.0)
        sides = jnp.pad(field, lead + [(1, 1)])
        field = field + coefficient * (
            sides[..., :-2] + sides[..., 2:] + upper + linked - 4.0 * field
        )
    return field


def apply_part(spectrum, operator, coefficient, offsets, extend):
    low = spectrum.astype(jnp.bfloat16)

    def adjoint_of(spec, resp):
        return jnp.einsum("frs,fsp->frp", spec, resp, preferred_element_type=jnp.float32)

    def forward_of(par, resp):
        return jnp.einsum("frp,fsp->frs", par, resp, preferred_element_type=jnp.float32)

    real = adjoint_of(low[0], operator[0]) + adjoint_of(low[1], operator[1])
    imag = adjoint_of(low[1], operator[0]) - adjoint_of(low[0], operator[1])
    adjoint = jnp.stack([real, imag])
    grid = adjoint.reshape(adjoint.shape[:3] + coefficient.shape)
    prior = smooth(grid, coefficient, offsets, extend).astype(jnp.bfloat16)
    prior = prior.reshape(adjoint.shape)
    real = forward_of(prior[0], operator[0]) - forward_of(prior[1], operator[1])
    imag = forward_of(prior[1], operator[0]) + forward_of(prior[0], operator[1])
    return jnp.stack([real, imag])


def body(vectors, observed, operator, noise, coefficient, offsets):
    sen, par = lax.axis_size("sen"), lax.axis_size("par")
    rows, sensors, length = vectors.shape
    half = length // 2
    grid_rows, width = coefficient.shape
    basis = jnp.asarray(make_basis(length))
    both = jnp.stack([vectors, observed])
    spectra = jnp.dot(
        both.reshape(2 * rows * sensors, length), basis, precision=lax.Precision.HIGHEST
    )
    spectra = spectra.reshape(2, rows, sensors, 2, half)
    whole_cells = half % (sen * par) == 0
    axes = ("sen", "par") if whole_cells else "sen"
    shares = sen * par if whole_cells else sen
    each = half // shares

    cut = operator.reshape(2, shares, each, sensors, grid_rows, width)
    cut = lax.all_to_all(cut, axes, 1, 1, tiled=True)
    if whole_cells:
        resp = cut.reshape(2, sen, par, each, sensors, grid_rows, width)
        resp = resp.transpose(0, 3, 1, 4, 2, 5, 6)
        resp = resp.reshape(2, each, sen * sensors, par * grid_rows * width)
        coefficient = lax.all_gather(coefficient, "par", tiled=True)
        offsets = lax.all_gather(offsets, "par", tiled=True)
        extend = zero_halo
    else:
        resp = cut.transpose(0, 2, 1, 3, 4, 5)
        resp = resp.reshape(2, each, sen * sensors, grid_rows * width)
        extend = lambda field: halo(field, "par", field.ndim - 2)

    def to_frequencies(spec):
        parts = spec.shape[0]
        cut = spec.reshape(parts, rows, sensors, 2, shares, each)
        cut = lax.all_to_all(cut.transpose(4, 0, 3, 5, 1, 2), axes, 0, 0, tiled=True)
        if whole_cells:
            cut = cut.reshape((sen, par) + cut.shape[1:])[:, 0]
        return cut.transpose(1, 2, 3, 4, 0, 5).reshape(parts, 2, each, rows, sen * sensors)

    def to_sensors(spec):
        parts = spec.shape[0]
        cut = spec.reshape(parts, 2, each, rows, sen, sensors).transpose(4, 0, 3, 5, 1, 2)
        if whole_cells:
            cut = jnp.repeat(cut, par, axis=0)
        cut = lax.all_to_all(cut, axes, 0, 0, tiled=True)
        return cut.transpose(1, 2, 3, 4, 0, 5).reshape(parts, rows, sensors, 2 * half)

    def hessian(spectrum):
        forward = apply_part(spectrum, resp, coefficient, offsets, extend)
        return forward if whole_cells else lax.psum(forward, "par")

    rest = spectra[1] - noise[None, :, None, None] * spectra[0]
    own, rest = to_frequencies(jnp.stack([spectra[0], rest]))
    left = rest - hessian(own)
    again = hessian(left)
    home = to_sensors(jnp.stack([left, again]))
    back = jnp.dot(
        home.reshape(2 * rows * sensors, length), basis.T, precision=lax.Precision.HIGHEST
    ).reshape(2, rows, sensors, length)
    residual = back[0]
    applied = back[1] + noise[None, :, None] * residual
    return (residual, applied)


def solution(mesh):
    placed = (
        P(None, "sen", None),
        P(None, "sen", None),
        P(None, None, "sen", "par"),
        P("sen"),
        P("par", None),
        P("par", None),
    )
    return jax.shard_map(
        body,
        mesh=mesh,
        in_specs=placed,
        out_specs=(P(None, "sen", None), P(None, "sen", None)),
        check_vma=False,
    )
```

time: 369 us -> 86.4 us (0.23)
  waiting for transfers between devices: 245 us -> 37.1 us
  other arithmetic: 63.2 us -> 7.98 us
  starting transfers between devices: 26.8 us -> 9.98 us
  between operations: 14.5 us -> 1.19 us
  local copies, waits for them, and re-layouts: 0.89 us -> 9.84 us
  blocking collectives: 6.73 us -> 14.2 us
  matrix products: 11.1 us -> 5.67 us
    psum x2 -> x0, waiting for transfers between devices: 222 us -> none  [hessian(): adjoint = lax.psum(partial_value, 'sen')]
    add x7, other arithmetic: 43.3 us -> 3.55 us  [the longest x6 2.88 us: smooth(): field + coefficient * (sides[..., :-2] + sides[..., 2:] + upper + linked...]
    all_to_all x0 -> x2, waiting for transfers between devices: none -> 37.1 us  [the longest x1 31.4 us: body(): cut = lax.all_to_all(cut, axes, 1, 1, tiled=True)]
    ppermute x16 -> x0, starting transfers between devices: 26.8 us -> none  [the longest x8 16 us: padded_2(): lax.ppermute(tail, axis, [(i, (i + 1) % count) for i in range(ends)])]
    ppermute x16 -> x0, waiting for transfers between devices: 22.9 us -> none  [the longest x8 19 us: padded_2(): lax.ppermute(head, axis, [((i + 1) % count, i) for i in range(ends)])]
    convert_element_type x2 -> x3, other arithmetic: 16.7 us -> 0.97 us  [the longest x2 0.96 us: apply_part(): prior = smooth(grid, coefficient, offsets, extend).astype(jnp.bfloat16)]
    all_to_all x0 -> x1, blocking collectives: none -> 10.6 us  [to_sensors(): cut = lax.all_to_all(cut, axes, 0, 0, tiled=True)]
    all_to_all x0 -> x2, starting transfers between devices: none -> 9.98 us  [the longest x1 7.3 us: to_frequencies(): lax.all_to_all(cut.transpose(4, 0, 3, 5, 1, 2), axes, 0, 0, tiled=True)]
  transfers between devices with their start and end apart: 18 -> 2, of which waited for: 17 -> 2; matrix products, arithmetic and copies ran while one was open for 0% -> 5% of each run, Pallas kernels for 0% -> 0%
where the time goes in v1:
time: 86.4 us; the launch traced here: 85.9 us
  waiting for transfers between devices  37.1 us (43%)
  blocking collectives  14.2 us (16%)
  starting transfers between devices  9.98 us (12%)
  local copies, waits for them, and re-layouts  9.84 us (11%)
  other arithmetic  7.98 us (9%)
  matrix products  5.67 us (7%)
  between operations  1.19 us (1%)
    all_to_all x1, waiting for transfers between devices, body(): cut = lax.all_to_all(cut, axes, 1, 1, tiled=True)  31.4 us
    all_to_all x1, blocking collectives, to_sensors(): cut = lax.all_to_all(cut, axes, 0, 0, tiled=True)  10.6 us
    all_to_all x1, starting transfers between devices, to_frequencies(): lax.all_to_all(cut.transpose(4, 0, 3, 5, 1, 2), axes, 0, 0, tiled=True)  7.3 us
    all_to_all x1, waiting for transfers between devices, to_frequencies(): lax.all_to_all(cut.transpose(4, 0, 3, 5, 1, 2), axes, 0, 0, tiled=True)  5.75 us
    unnamed x21, local copies, waits for them, and re-layouts  3.87 us
    add x6, other arithmetic, smooth(): field + coefficient * (sides[..., :-2] + sides[..., 2:] + upper + linked...  2.88 us
    all_to_all x1, starting transfers between devices, body(): cut = lax.all_to_all(cut, axes, 1, 1, tiled=True)  2.69 us
    dot_general x8, matrix products, forward_of(): jnp.einsum('frp,fsp->frs', par, resp, preferred_element_type=jnp.float32)  2.44 us
  transfers between devices with their start and end apart: 2, of which 2 were waited for; matrix products, arithmetic and copies ran while one was open for 5% of the time, Pallas kernels for 0%

profile of v1, /device:TPU:0, one launch (start us, length us, event | category | flops | bytes accessed | tf_op | source)
XLA Modules:
  0.0 85.9 jit_solution(10340937426642190041)
XLA Ops:
  0.6 0.7 pad_maximum_fusion
  1.4 1.2 %fusion.65 = f32[32,256]{1,0:T(8,128)S(1)} fusion(f32[32,256]{1,0:T(8,128)S(1)} %bitcast.136, f32[256,256]{1,0:T(8,128)} %constant.22.clone), kind=kOutput, calls=%fused_computation.160 | convolution fusion | flops 25165824 | bytes 327680 | tf_op jit(solution)/shard_map/dot_general | solution.py:90
  3.2 0.9 %multiply_subtract_fusion = f32[1,2,8,2,32,4]{2,1,5,4,3,0:T(2,128)S(1)} fusion(f32[1,2,8,2,32,4]{2,1,5,4,3,0:T(2,128)S(1)} %squeeze.28, f32[1,2,8,2,32,4]{2,1,5,4,3,0:T(2,128)S(1)} %stack.65, f32[8]{0:T(128)} %param.10), kind=kLoop, calls=%fused_computation.11 | loop fusion | flops 8192 | bytes 49184 | tf_op jit(solution)/shard_map/sub | solution.py:133
  4.4 1.4 %reshape.133 = f32[32,1,256]{2,1,0:T(1,128)} reshape(f32[32,2,2,4,2,8]{5,4,3,2,1,0:T(2,128)S(1)} %copy.37) | data formatting | bytes 65536
  5.8 7.3 %all-to-all-start = ((f32[32,1,256]{2,1,0:T(1,128)}), f32[32,1,256]{2,1,0:T(1,128)S(1)}, u32[]{:S(2)}, u32[]{:S(2)}) async-start(f32[32,1,256]{2,1,0:T(1,128)} %reshape.133), calls=%async_computation | async-start | bytes 65536 | tf_op jit(solution)/shard_map/all_to_all | solution.py:116
  13.1 1.5 %copy.39 = bf16[2,32,4,8,1,384]{5,3,2,0,4,1:T(8,128)(2,1)} copy(bf16[2,32,4,8,1,384]{5,3,2,1,0,4:T(8,128)(2,1)S(1)} %bitcast.126) | data formatting | bytes 3145728 | tf_op jit(solution)/shard_map/reshape | solution.py:99
  14.6 5.8 %all-to-all-done = f32[32,1,256]{2,1,0:T(1,128)S(1)} async-done(((f32[32,1,256]{2,1,0:T(1,128)}), f32[32,1,256]{2,1,0:T(1,128)S(1)}, u32[]{:S(2)}, u32[]{:S(2)}) %all-to-all-start) | async-done | bytes 32800 | tf_op jit(solution)/shard_map/all_to_all | solution.py:116
  20.4 2.7 %all-to-all-start.1 = ((bf16[2,32,4,8,1,384]{5,3,2,0,4,1:T(8,128)(2,1)}), bf16[2,32,4,8,1,384]{5,3,2,0,4,1:T(8,128)(2,1)S(1)}, u32[]{:S(2)}, u32[]{:S(2)}) async-start(bf16[2,32,4,8,1,384]{5,3,2,0,4,1:T(8,128)(2,1)} %copy.39), calls=%async_computation.1 | async-start | bytes 3145728 | tf_op jit(solution)/shard_map/all_to_all | solution.py:100
  23.1 1.8 %all-gather.1 = s32[2,1,384]{2,1,0:T(1,128)S(1)} all-gather(s32[1,1,384]{2,1,0:T(1,128)S(1)} %bitcast.149), channel_id=1, replica_groups=mesh['sen'=16,'par'=2] {'par'}, dimensions={0}, use_global_device_ids=true | all-gather | bytes 4608 | tf_op jit(solution)/shard_map/all_gather | solution.py:106
  24.9 1.8 %all-gather = f32[2,1,384]{2,1,0:T(1,128)S(1)} all-gather(f32[1,1,384]{2,1,0:T(1,128)S(1)} %bitcast.150), channel_id=1, replica_groups=mesh['sen'=16,'par'=2] {'par'}, dimensions={0}, use_global_device_ids=true | all-gather | bytes 4608 | tf_op jit(solution)/shard_map/all_gather | solution.py:105
  26.8 0.5 broadcast.120
  27.3 0.7 reduce
  28.0 0.8 reshape.134
  29.6 31.4 %all-to-all-done.1 = bf16[2,32,4,8,1,384]{5,3,2,0,4,1:T(8,128)(2,1)S(1)} async-done(((bf16[2,32,4,8,1,384]{5,3,2,0,4,1:T(8,128)(2,1)}), bf16[2,32,4,8,1,384]{5,3,2,0,4,1:T(8,128)(2,1)S(1)}, u32[]{:S(2)}, u32[]{:S(2)}) %all-to-all-start.1) | async-done | bytes 1572896 | tf_op jit(solution)/shard_map/all_to_all | solution.py:100
  62.3 0.5 multiply_add_fusion.5
  63.3 0.5 multiply_add_fusion.3
  63.9 0.5 add_convert_fusion.1
  67.1 0.5 multiply_add_fusion.2
  68.6 0.5 add_convert_fusion
  71.1 0.8 reshape.135
  71.9 10.6 %all_to_all.15 = f32[32,1,256]{2,1,0:T(1,128)S(1)} all-to-all(f32[32,1,256]{2,1,0:T(1,128)S(1)} %reshape.135), channel_id=1, replica_groups=mesh['sen'=16,'par'=2] {'sen','par'}, dimensions={0} | all-to-all | bytes 65536 | tf_op jit(solution)/shard_map/all_to_all | solution.py:126
  82.5 0.7 reduce.1
  83.2 0.8 reshape.136
  85.3 0.7 fusion.56
  (86 shorter events, 10.4 us)
Async XLA Ops:
  3.2 10.0 %copy-start = (bf16[2,128,8,384]{3,2,1,0:T(8,128)(2,1)S(1)}, bf16[2,128,8,384]{3,2,1,0:T(8,128)(2,1)}, u32[]{:S(2)}) copy-start(bf16[2,128,8,384]{3,2,1,0:T(8,128)(2,1)} %param.9) | copy-start | bytes 4718596
  5.8 14.6 %all-to-all-start = ((f32[32,1,256]{2,1,0:T(1,128)}), f32[32,1,256]{2,1,0:T(1,128)S(1)}, u32[]{:S(2)}, u32[]{:S(2)}) async-start(f32[32,1,256]{2,1,0:T(1,128)} %reshape.133), calls=%async_computation | async-start | bytes 65536 | tf_op jit(solution)/shard_map/all_to_all | solution.py:116
  14.6 8.5 %copy-start.3 = (s32[1,384]{1,0:T(1,128)S(1)}, s32[1,384]{1,0:T(1,128)}, u32[]{:S(2)}) copy-start(s32[1,384]{1,0:T(1,128)} %param.12) | copy-start | bytes 4612
  14.6 10.3 %copy-start.4 = (f32[1,384]{1,0:T(1,128)S(1)}, f32[1,384]{1,0:T(1,128)}, u32[]{:S(2)}) copy-start(f32[1,384]{1,0:T(1,128)} %param.11) | copy-start | bytes 4612
  20.4 40.5 %all-to-all-start.1 = ((bf16[2,32,4,8,1,384]{5,3,2,0,4,1:T(8,128)(2,1)}), bf16[2,32,4,8,1,384]{5,3,2,0,4,1:T(8,128)(2,1)S(1)}, u32[]{:S(2)}, u32[]{:S(2)}) async-start(bf16[2,32,4,8,1,384]{5,3,2,0,4,1:T(8,128)(2,1)} %copy.39), calls=%async_computation.1 | async-start | bytes 3145728 | tf_op jit(solution)/shard_map/all_to_all | solution.py:100
  83.2 1.7 %copy-start.1 = (f32[256,256]{1,0:T(8,128)S(1)}, f32[256,256]{1,0:T(8,128)}, u32[]{:S(2)}) copy-start(f32[256,256]{1,0:T(8,128)} %constant.22.clone) | copy-start | bytes 786436
  84.1 1.2 %copy-start.2 = (f32[8]{0:T(128)S(1)}, f32[8]{0:T(128)}, u32[]{:S(2)}) copy-start(f32[8]{0:T(128)} %param.10) | copy-start | bytes 100

commit v2 on v1

--- a/solution.py
+++ b/solution.py
@@ -4,6 +4,8 @@
 import jax.numpy as jnp
 import numpy as np
 from jax import lax
+from jax.experimental import pallas as pl
+from jax.experimental.pallas import tpu as pltpu
 from jax.sharding import PartitionSpec as P
 
 SWEEPS = 4
@@ -80,7 +82,7 @@
     return jnp.stack([real, imag])
 
 
-def body(vectors, observed, operator, noise, coefficient, offsets):
+def body_plain(vectors, observed, operator, noise, coefficient, offsets):
     sen, par = lax.axis_size("sen"), lax.axis_size("par")
     rows, sensors, length = vectors.shape
     half = length // 2
@@ -143,6 +145,184 @@
     return (residual, applied)
 
 
+def roll(x, shift, axis):
+    size = x.shape[axis]
+    return x if shift % size == 0 else pltpu.roll(x, shift % size, axis)
+
+
+def iota(shape, axis):
+    return lax.broadcasted_iota(jnp.int32, shape, axis)
+
+
+def local_kernel(resp_ref, own_ref, rest_ref, coef_ref, link_ref, out_ref):
+    sen, par, each, pair, width = resp_ref.shape
+    sensors = pair // 2
+    lines, lanes = own_ref.shape
+    row, lane = iota((lines, lanes), 0), iota((lines, lanes), 1)
+    real_row = row % 2 == 0
+    real_lane = lane // sensors % 2 == 0
+    freq = row // 2 % each
+
+    def swapped(x):
+        return jnp.where(real_row, roll(x, -1, 0), roll(x, 1, 0))
+
+    shape = (lines, width)
+    column = iota(shape, 1)
+    coefs, links = [], []
+    for x in range(par):
+        coefs.append(jnp.broadcast_to(coef_ref[x : x + 1, :], shape))
+        offset = jnp.broadcast_to(link_ref[x : x + 1, :], shape)
+        masks = []
+        for shift in range(-REACH, REACH + 1):
+            inside = (column + shift >= 0) & (column + shift < width)
+            masks.append(jnp.where((offset == shift) & inside, 1.0, 0.0))
+        links.append(masks)
+    after_first = jnp.where(column > 0, 1.0, 0.0)
+    before_last = jnp.where(column < width - 1, 1.0, 0.0)
+
+    def block(f, p):
+        return resp_ref[:, p, f].reshape(sen * pair, width)
+
+    def hessian(left):
+        field = []
+        for p in range(par):
+            total = jnp.zeros(shape, jnp.float32)
+            for f in range(each):
+                part = jnp.where(freq == f, left, 0.0).astype(jnp.bfloat16)
+                total += jnp.dot(part, block(f, p), preferred_element_type=jnp.float32)
+            field.append(total)
+        for _ in range(SWEEPS):
+            after = []
+            for x, u in enumerate(field):
+                around = roll(u, 1, 1) * after_first + roll(u, -1, 1) * before_last
+                if x > 0:
+                    around += field[x - 1]
+                if x < par - 1:
+                    linked = jnp.zeros(shape, jnp.float32)
+                    for mask, shift in zip(links[x], range(-REACH, REACH + 1)):
+                        linked += mask * roll(field[x + 1], -shift, 1)
+                    around += linked
+                after.append(u + coefs[x] * (around - 4.0 * u))
+            field = after
+        prior = [u.astype(jnp.bfloat16) for u in field]
+        out = jnp.zeros((lines, lanes), jnp.float32)
+        for f in range(each):
+            part = jnp.zeros((lines, lanes), jnp.float32)
+            for p in range(par):
+                part += lax.dot_general(
+                    prior[p], block(f, p), (((1,), (1,)), ((), ())), preferred_element_type=jnp.float32
+                )
+            out = jnp.where(freq == f, part, out)
+        crossed = swapped(roll(out, -sensors, 1))
+        return out + jnp.where(real_row, -crossed, crossed)
+
+    left = rest_ref[...] - hessian(own_ref[...])
+    crossed = swapped(left)
+    crossed = roll(jnp.where(real_row, crossed, -crossed), sensors, 1)
+    again = hessian(jnp.where(real_lane, left, crossed))
+    both = jnp.where(real_lane, left, roll(again, sensors, 1))
+
+    count = 2 * each
+    wide = count * pair
+    to, group = iota((count, wide), 0), iota((count, wide), 1) // pair
+    for r in range(lines // count):
+        for h in range(lanes // wide):
+            tile = both[r * count : (r + 1) * count, h * wide : (h + 1) * wide]
+            moved = tile
+            for turn in range(1, count):
+                turned = roll(roll(tile, -turn, 0), turn * pair, 1)
+                moved = jnp.where((group - to + count) % count == turn, turned, moved)
+            for i in range(count):
+                for p in range(par):
+                    out_ref[(h * count + i) * par + p, r : r + 1, :] = moved[i : i + 1, :]
+
+
+def home_kernel(got_ref, basis_ref, noise_ref, residual_ref, applied_ref):
+    sources, rows, wide = got_ref.shape
+    sensors = noise_ref.shape[0]
+    pair = 2 * sensors
+    lines = []
+    for r in range(rows):
+        turned = got_ref[:, r, :].T
+        lines.append(
+            jnp.concatenate([turned[i : i + pair, :] for i in range(0, wide, pair)], axis=1)
+        )
+    back = jnp.dot(
+        jnp.concatenate(lines, axis=0),
+        basis_ref[...],
+        precision=lax.Precision.HIGHEST,
+        preferred_element_type=jnp.float32,
+    )
+    for r in range(rows):
+        residual = back[r * pair : r * pair + sensors]
+        residual_ref[r] = residual
+        applied_ref[r] = back[r * pair + sensors : (r + 1) * pair] + noise_ref[...] * residual
+
+
+def body_fast(vectors, observed, operator, noise, coefficient, offsets):
+    sen, par = lax.axis_size("sen"), lax.axis_size("par")
+    rows, sensors, length = vectors.shape
+    half = length // 2
+    width = coefficient.shape[1]
+    shares = sen * par
+    each = half // shares
+    pair = 2 * sensors
+    axes = ("sen", "par")
+    basis = make_basis(length)
+
+    cut = operator.reshape(2, shares, each, sensors, width).transpose(1, 2, 0, 3, 4)
+    cut = cut.reshape(shares, each, pair, width)
+    cut, vectors, observed, coefficient, offsets = lax.optimization_barrier(
+        (cut, vectors, observed, coefficient, offsets)
+    )
+    resp = lax.all_to_all(cut, axes, 0, 0, tiled=True)
+    resp = resp.reshape(sen, par, each, pair, width)
+
+    both = jnp.stack([vectors, observed])
+    spectra = jnp.dot(
+        both.reshape(2 * rows * sensors, length), basis, precision=lax.Precision.HIGHEST
+    )
+    spectra = spectra.reshape(2, rows, sensors, 2, shares, each)
+    rest = spectra[1] - noise[None, :, None, None, None] * spectra[0]
+    spectra = jnp.stack([spectra[0], rest]).transpose(4, 0, 1, 5, 3, 2)
+    spectra = lax.all_to_all(
+        spectra.reshape(shares, 1, 4 * rows * each * sensors), axes, 0, 0, tiled=True
+    )
+    spectra = spectra.reshape(sen, par, 2, rows, each, 2, sensors)[:, 0]
+    own, rest = spectra.transpose(1, 2, 3, 4, 0, 5)
+    other = jnp.stack([own[:, :, 1], -own[:, :, 0]], axis=2)
+    lines, lanes = rows * each * 2, sen * pair
+    own = jnp.stack([own, other], axis=4).reshape(lines, lanes)
+    rest = jnp.stack([rest, jnp.zeros_like(rest)], axis=4).reshape(lines, lanes)
+    grid = jnp.concatenate([coefficient, offsets.astype(jnp.float32)])
+    grid = lax.all_gather(grid, "par").transpose(1, 0, 2)
+
+    message = pl.pallas_call(
+        local_kernel,
+        out_shape=jax.ShapeDtypeStruct((shares, rows, 2 * each * pair), jnp.float32),
+        compiler_params=pltpu.CompilerParams(vmem_limit_bytes=32 * 2**20),
+        name="local_hessians",
+    )(resp, own, rest, grid[0], grid[1].astype(jnp.int32))
+    got = lax.all_to_all(message, axes, 0, 0, tiled=True)
+    turned = basis.reshape(length, 2, shares, each).transpose(3, 1, 2, 0).reshape(length, length)
+    return pl.pallas_call(
+        home_kernel,
+        out_shape=[jax.ShapeDtypeStruct((rows, sensors, length), jnp.float32)] * 2,
+        name="to_time",
+    )(got, jnp.asarray(turned), noise[:, None])
+
+
+def fits(mesh, args):
+    vectors, _, _, _, coefficient, _ = args
+    sen, par = mesh.shape["sen"], mesh.shape["par"]
+    rows, sensors, length = vectors.shape
+    half = length // 2
+    if half % (sen * par) or sensors % sen or coefficient.shape[0] != par:
+        return False
+    each, pair = half // (sen * par), 2 * (sensors // sen)
+    return 2 * each * pair == 128 and 2 * each == 8 and sen * pair % 128 == 0 and coefficient.shape[1] % 128 == 0
+
+
 def solution(mesh):
     placed = (
         P(None, "sen", None),
@@ -152,10 +332,14 @@
         P("par", None),
         P("par", None),
     )
-    return jax.shard_map(
-        body,
-        mesh=mesh,
-        in_specs=placed,
-        out_specs=(P(None, "sen", None), P(None, "sen", None)),
-        check_vma=False,
-    )
+
+    def whole(*args):
+        return jax.shard_map(
+            body_fast if fits(mesh, args) else body_plain,
+            mesh=mesh,
+            in_specs=placed,
+            out_specs=(P(None, "sen", None), P(None, "sen", None)),
+            check_vma=False,
+        )(*args)
+
+    return whole

time: 86.4 us -> 76.9 us (0.89)
  other arithmetic: 7.98 us -> 0.65 us
  matrix products: 5.67 us -> 0.23 us
  Pallas kernels: 0 us -> 5.2 us
  starting transfers between devices: 9.98 us -> 6.37 us
  waiting for transfers between devices: 37.1 us -> 39.9 us
  local copies, waits for them, and re-layouts: 9.84 us -> 7.25 us
  blocking collectives: 14.2 us -> 16.1 us
    dot_general x18 -> x1, matrix products: 5.67 us -> 0.23 us  [body_fast(): jnp.dot(both.reshape(2 * rows * sensors, length), basis, precision=lax.Pr...]
    pallas_call x0 -> x2, Pallas kernels: none -> 5.2 us  [the longest x1 3.27 us: body_fast(): pl.pallas_call(local_kernel, out_shape=jax.ShapeDtypeStruct((shares, rows...]
    all_to_all x1, blocking collectives: 10.6 us -> 14.4 us  [body_fast(): lax.all_to_all(spectra.reshape(shares, 1, 4 * rows * each * sensors), axe...]
    all_to_all x2, starting transfers between devices: 9.98 us -> 6.37 us  [the longest x1 3.56 us: body_fast(): got = lax.all_to_all(message, axes, 0, 0, tiled=True)]
    add x7 -> x0, other arithmetic: 3.55 us -> none  [the longest x6 2.88 us: smooth(): field + coefficient * (sides[..., :-2] + sides[..., 2:] + upper + linked...]
    unnamed x21 -> x15, local copies, waits for them, and re-layouts: 3.87 us -> 0.77 us
    all_to_all x2, waiting for transfers between devices: 37.1 us -> 39.9 us  [the longest x1 33.3 us: body_fast(): resp = lax.all_to_all(cut, axes, 0, 0, tiled=True)]
    transpose x4 -> x3, local copies, waits for them, and re-layouts: 0.56 us -> 2.93 us  [the longest x1 2.9 us: body_fast(): operator.reshape(2, shares, each, sensors, width).transpose(1, 2, 0, 3, 4)]
  transfers between devices with their start and end apart: 2 -> 2, of which waited for: 2 -> 2; matrix products, arithmetic and copies ran while one was open for 5% -> 4% of each run, Pallas kernels for 0% -> 0%
where the time goes in v2:
time: 76.9 us; the launch traced here: 76.6 us
  waiting for transfers between devices  39.9 us (52%)
  blocking collectives  16.1 us (21%)
  local copies, waits for them, and re-layouts  7.25 us (9%)
  starting transfers between devices  6.37 us (8%)
  Pallas kernels  5.2 us (7%)
  between operations  0.86 us (1%)
    all_to_all x1, waiting for transfers between devices, body_fast(): resp = lax.all_to_all(cut, axes, 0, 0, tiled=True)  33.3 us
    all_to_all x1, blocking collectives, body_fast(): lax.all_to_all(spectra.reshape(shares, 1, 4 * rows * each * sensors), axe...  14.4 us
    all_to_all x1, waiting for transfers between devices, body_fast(): got = lax.all_to_all(message, axes, 0, 0, tiled=True)  6.58 us
    all_to_all x1, starting transfers between devices, body_fast(): got = lax.all_to_all(message, axes, 0, 0, tiled=True)  3.56 us
    pallas_call x1, Pallas kernels, body_fast(): pl.pallas_call(local_kernel, out_shape=jax.ShapeDtypeStruct((shares, rows...  3.27 us
    transpose x1, local copies, waits for them, and re-layouts, body_fast(): operator.reshape(2, shares, each, sensors, width).transpose(1, 2, 0, 3, 4)  2.9 us
    all_to_all x1, starting transfers between devices, body_fast(): resp = lax.all_to_all(cut, axes, 0, 0, tiled=True)  2.82 us
    pallas_call x1, Pallas kernels, body_fast(): pl.pallas_call(home_kernel, out_shape=[jax.ShapeDtypeStruct((rows, sensor...  1.92 us
  transfers between devices with their start and end apart: 2, of which 2 were waited for; matrix products, arithmetic and copies ran while one was open for 4% of the time, Pallas kernels for 0%

profile of v2, /device:TPU:0, one launch (start us, length us, event | category | flops | bytes accessed | tf_op | source)
XLA Modules:
  0.0 76.6 jit_solution(18146065095442487267)
XLA Ops:
  0.7 2.9 %copy.35 = bf16[32,4,2,8,384]{4,3,2,1,0:T(8,128)(2,1)} copy(bf16[32,4,2,8,384]{4,3,1,0,2:T(8,128)(2,1)} %bitcast.42) | data formatting | bytes 3145728 | tf_op jit(solution)/shard_map/transpose | solution.py:273
  3.6 0.2 fusion.3
  3.9 0.2 squeeze.12
  4.2 0.2 slice.27
  4.4 0.1 copy.24
  4.6 0.1 multiply_subtract_fusion
  4.7 0.1 copy.25
  5.0 14.4 %all_to_all.15 = f32[32,1,256]{2,1,0:T(1,128)S(1)} all-to-all(f32[32,1,256]{2,1,0:T(1,128)S(1)} %copy.27), channel_id=1, replica_groups=mesh['sen'=16,'par'=2] {'sen','par'}, dimensions={0} | all-to-all | bytes 65536 | tf_op jit(solution)/shard_map/all_to_all | solution.py:288
  19.3 2.8 %all-to-all-start = ((bf16[32,4,16,384]{3,2,1,0:T(8,128)(2,1)}), bf16[32,4,16,384]{3,2,1,0:T(8,128)(2,1)S(1)}, u32[]{:S(2)}, u32[]{:S(2)}) async-start(bf16[32,4,16,384]{3,2,1,0:T(8,128)(2,1)} %bitcast.39), calls=%async_computation | async-start | bytes 3145728 | tf_op jit(solution)/shard_map/all_to_all | solution.py:278
  22.2 1.8 %all-gather.1 = f32[2,2,384]{2,1,0:T(2,128)S(1)} all-gather(f32[1,2,384]{2,1,0:T(2,128)S(1)} %maximum_bitcast_fusion.2), channel_id=2, replica_groups=mesh['sen'=16,'par'=2] {'par'}, dimensions={0}, use_global_device_ids=true | all-gather | bytes 9216 | tf_op jit(solution)/shard_map/all_gather | solution.py:298
  24.1 0.8 %reshape.60 = f32[16,2,2,2,4,2,8]{6,5,4,3,2,1,0:T(2,128)S(1)} reshape(f32[32,256]{1,0:T(8,128)S(1)} %reduce) | data formatting | bytes 65536 | tf_op jit(solution)/shard_map/reshape | solution.py:291
  25.1 0.2 maximum_bitcast_fusion.1
  25.3 0.1 pad_maximum_fusion
  25.4 0.2 copy.28
  25.7 0.4 reshape.61.own_ref
  26.0 0.1 copy.32
  26.3 0.4 reshape.62.rest_ref
  26.7 33.3 %all-to-all-done = bf16[32,4,16,384]{3,2,1,0:T(8,128)(2,1)S(1)} async-done(((bf16[32,4,16,384]{3,2,1,0:T(8,128)(2,1)}), bf16[32,4,16,384]{3,2,1,0:T(8,128)(2,1)S(1)}, u32[]{:S(2)}, u32[]{:S(2)}) %all-to-all-start) | async-done | bytes 1572896 | tf_op jit(solution)/shard_map/all_to_all | solution.py:278
  60.0 3.3 %local_hessians.1 = f32[32,2,128]{2,1,0:T(2,128)} custom-call(bf16[16,2,4,16,384]{4,3,2,1,0:T(8,128)(2,1)S(1)} %bitcast.41, f32[16,256]{1,0:T(8,128)S(1)} %reshape.61.own_ref, f32[16,256]{1,0:T(8,128)S(1)} %reshape.62.rest_ref, f32[2,384]{1,0:T(2,128)S(1)} %get-tuple-element.20.coef_ref, s32[2,384]{1,0:T(2,128)S(1)} %get-tuple-element.19.link_ref), custom_call_target="tpu_custom_call" | custom-call | tf_op jit(solution)/shard_map/local_hessians/pallas_call | solution.py:300
  63.3 3.6 %all-to-all-start.2 = ((f32[32,2,128]{2,1,0:T(2,128)}), f32[32,2,128]{2,1,0:T(2,128)S(1)}, u32[]{:S(2)}, u32[]{:S(2)}) async-start(f32[32,2,128]{2,1,0:T(2,128)} %local_hessians.1), calls=%async_computation.2 | async-start | bytes 65536 | tf_op jit(solution)/shard_map/all_to_all | solution.py:306
  66.8 0.7 copy.31.noise_ref
  67.5 6.6 %all-to-all-done.2.got_ref = f32[32,2,128]{2,1,0:T(2,128)S(1)} async-done(((f32[32,2,128]{2,1,0:T(2,128)}), f32[32,2,128]{2,1,0:T(2,128)S(1)}, u32[]{:S(2)}, u32[]{:S(2)}) %all-to-all-start.2) | async-done | bytes 32800 | tf_op jit(solution)/shard_map/all_to_all | solution.py:306
  74.1 0.6 copy-done.1
  74.7 1.9 %to_time.1 = (f32[2,8,256]{2,1,0:T(8,128)}, f32[2,8,256]{2,1,0:T(8,128)}) custom-call(f32[32,2,128]{2,1,0:T(2,128)} %copy-done.1, f32[256,256]{1,0:T(8,128)} %constant.7.clone.basis_ref, f32[8,1]{1,0:T(8,128)} %copy.31.noise_ref), custom_call_target="tpu_custom_call" | custom-call | tf_op jit(solution)/shard_map/to_time/pallas_call | solution.py:308
  (29 shorter events, 0.8 us)
Async XLA Ops:
  0.6 2.9 %copy-start.2 = (f32[2,8,256]{2,1,0:T(8,128)S(1)}, f32[2,8,256]{2,1,0:T(8,128)}, u32[]{:S(2)}) copy-start(f32[2,8,256]{2,1,0:T(8,128)} %param.9) | copy-start | bytes 49156
  0.6 2.9 %copy-start.3 = (f32[2,8,256]{2,1,0:T(8,128)S(1)}, f32[2,8,256]{2,1,0:T(8,128)}, u32[]{:S(2)}) copy-start(f32[2,8,256]{2,1,0:T(8,128)} %param.8) | copy-start | bytes 49156
  0.6 2.9 %copy-start = (f32[256,256]{1,0:T(8,128)S(1)}, f32[256,256]{1,0:T(8,128)}, u32[]{:S(2)}) copy-start(f32[256,256]{1,0:T(8,128)} %constant.6.clone) | copy-start | bytes 786436
  3.6 1.0 %copy-start.4 = (f32[8]{0:T(128)S(1)}, f32[8]{0:T(128)}, u32[]{:S(2)}) copy-start(f32[8]{0:T(128)} %param.11) | copy-start | bytes 100
  19.3 2.8 %copy-start.5 = (s32[1,384]{1,0:T(1,128)S(1)}, s32[1,384]{1,0:T(1,128)}, u32[]{:S(2)}) copy-start(s32[1,384]{1,0:T(1,128)} %param.13) | copy-start | bytes 4612
  19.3 2.9 %copy-start.6 = (f32[1,384]{1,0:T(1,128)S(1)}, f32[1,384]{1,0:T(1,128)}, u32[]{:S(2)}) copy-start(f32[1,384]{1,0:T(1,128)} %param.12) | copy-start | bytes 4612
  19.3 40.7 %all-to-all-start = ((bf16[32,4,16,384]{3,2,1,0:T(8,128)(2,1)}), bf16[32,4,16,384]{3,2,1,0:T(8,128)(2,1)S(1)}, u32[]{:S(2)}, u32[]{:S(2)}) async-start(bf16[32,4,16,384]{3,2,1,0:T(8,128)(2,1)} %bitcast.39), calls=%async_computation | async-start | bytes 3145728 | tf_op jit(solution)/shard_map/all_to_all | solution.py:278
  63.3 10.8 %all-to-all-start.2 = ((f32[32,2,128]{2,1,0:T(2,128)}), f32[32,2,128]{2,1,0:T(2,128)S(1)}, u32[]{:S(2)}, u32[]{:S(2)}) async-start(f32[32,2,128]{2,1,0:T(2,128)} %local_hessians.1), calls=%async_computation.2 | async-start | bytes 65536 | tf_op jit(solution)/shard_map/all_to_all | solution.py:306
  74.1 0.6 copy-start.1

commit v3 on v2

--- a/solution.py
+++ b/solution.py
@@ -1,3 +1,4 @@
+import functools
 import math
 
 import jax
@@ -154,11 +155,73 @@
     return lax.broadcasted_iota(jnp.int32, shape, axis)
 
 
-def local_kernel(resp_ref, own_ref, rest_ref, coef_ref, link_ref, out_ref):
-    sen, par, each, pair, width = resp_ref.shape
+def outbound_kernel(resp_ref, vectors_ref, observed_ref, noise_ref, basis_ref, out_ref, spectra_ref):
+    _, devices, each, sensors, width = resp_ref.shape
+    pair, lines = 2 * sensors, 2 * each
+    wide = out_ref.shape[2]
+    tiles = width // wide
+
+    @pl.when(pl.program_id(0) == 0)
+    def _():
+        rows = vectors_ref.shape[0]
+        records = []
+        for r in range(rows):
+            record = vectors_ref[r]
+            records += [record, observed_ref[r] - noise_ref[...] * record]
+        filled = rows * pair
+        records.append(jnp.zeros((wide - filled, records[0].shape[1]), jnp.float32))
+        spectra = lax.dot_general(
+            basis_ref[...],
+            jnp.concatenate(records, axis=0),
+            (((1,), (1,)), ((), ())),
+            precision=lax.Precision.HIGHEST,
+            preferred_element_type=jnp.float32,
+        )
+        exact = iota(spectra.shape, 1) // sensors % 2 == 1
+        high = spectra.astype(jnp.bfloat16).astype(jnp.float32)
+        rest = jnp.where(exact, spectra - high, 0.0)
+        middle = rest.astype(jnp.bfloat16).astype(jnp.float32)
+        low = (rest - middle).astype(jnp.bfloat16).astype(jnp.float32)
+        packed = high + roll(middle, filled, 1) + roll(low, 2 * filled, 1)
+        spectra_ref[...] = packed.reshape(spectra_ref.shape)
+
+    for f in range(each):
+        for j in range(tiles):
+            lanes = pl.ds(j * wide, wide)
+            part = jnp.concatenate([resp_ref[0, :, f, :, lanes], resp_ref[1, :, f, :, lanes]], axis=1)
+            out_ref[:, pl.ds((f * tiles + j) * pair, pair), :] = part
+    first = pl.multiple_of(pl.program_id(0) * devices, devices)
+    out_ref[:, pl.ds(each * tiles * pair, lines), :] = spectra_ref[pl.ds(first, devices)].astype(
+        jnp.bfloat16
+    )
+
+
+def local_kernel(each, got_ref, coef_ref, link_ref, out_ref):
+    sen, par, _, wide = got_ref.shape
+    width = coef_ref.shape[1]
+    tiles = width // wide
+    rows = out_ref.shape[1]
+    lines = 2 * each
+    pair = wide // lines
     sensors = pair // 2
-    lines, lanes = own_ref.shape
-    row, lane = iota((lines, lanes), 0), iota((lines, lanes), 1)
+    held, lanes = rows * lines, sen * pair
+    per = wide // pair
+    body_rows = each * tiles * pair
+
+    tail = got_ref[:, 0, pl.ds(body_rows, lines), :].astype(jnp.float32)
+    parts = rows * pair
+    at = iota((lines, wide), 1) // pair
+    spectra = [[jnp.zeros((lines, wide), jnp.float32) for _ in range(lanes // wide)] for _ in range(rows)]
+    for i in range(sen):
+        packed = tail[i]
+        packed = packed + roll(packed, -parts, 1) + roll(packed, -2 * parts, 1)
+        h, place = divmod(i, per)
+        for r in range(rows):
+            moved = roll(packed, (place - r) * pair, 1)
+            spectra[r][h] = jnp.where(at == place, moved, spectra[r][h])
+    spectra = jnp.concatenate([jnp.concatenate(line, axis=1) for line in spectra], axis=0)
+
+    row, lane = iota((held, lanes), 0), iota((held, lanes), 1)
     real_row = row % 2 == 0
     real_lane = lane // sensors % 2 == 0
     freq = row // 2 % each
@@ -166,7 +229,7 @@
     def swapped(x):
         return jnp.where(real_row, roll(x, -1, 0), roll(x, 1, 0))
 
-    shape = (lines, width)
+    shape = (held, width)
     column = iota(shape, 1)
     coefs, links = [], []
     for x in range(par):
@@ -181,9 +244,18 @@
     before_last = jnp.where(column < width - 1, 1.0, 0.0)
 
     def block(f, p):
-        return resp_ref[:, p, f].reshape(sen * pair, width)
-
-    def hessian(left):
+        return jnp.concatenate(
+            [
+                got_ref[:, p, pl.ds((f * tiles + j) * pair, pair), :].reshape(lanes, wide)
+                for j in range(tiles)
+            ],
+            axis=1,
+        )
+
+    def hessian(record):
+        crossed = swapped(record)
+        crossed = roll(jnp.where(real_row, crossed, -crossed), sensors, 1)
+        left = jnp.where(real_lane, record, crossed)
         field = []
         for p in range(par):
             total = jnp.zeros(shape, jnp.float32)
@@ -205,9 +277,9 @@
                 after.append(u + coefs[x] * (around - 4.0 * u))
             field = after
         prior = [u.astype(jnp.bfloat16) for u in field]
-        out = jnp.zeros((lines, lanes), jnp.float32)
+        out = jnp.zeros((held, lanes), jnp.float32)
         for f in range(each):
-            part = jnp.zeros((lines, lanes), jnp.float32)
+            part = jnp.zeros((held, lanes), jnp.float32)
             for p in range(par):
                 part += lax.dot_general(
                     prior[p], block(f, p), (((1,), (1,)), ((), ())), preferred_element_type=jnp.float32
@@ -216,25 +288,21 @@
         crossed = swapped(roll(out, -sensors, 1))
         return out + jnp.where(real_row, -crossed, crossed)
 
-    left = rest_ref[...] - hessian(own_ref[...])
-    crossed = swapped(left)
-    crossed = roll(jnp.where(real_row, crossed, -crossed), sensors, 1)
-    again = hessian(jnp.where(real_lane, left, crossed))
-    both = jnp.where(real_lane, left, roll(again, sensors, 1))
-
-    count = 2 * each
-    wide = count * pair
-    to, group = iota((count, wide), 0), iota((count, wide), 1) // pair
-    for r in range(lines // count):
+    residual = roll(spectra, -sensors, 1) - hessian(spectra)
+    applied = hessian(residual)
+    both = jnp.where(real_lane, residual, roll(applied, sensors, 1))
+
+    to, group = iota((lines, wide), 0), iota((lines, wide), 1) // pair
+    for r in range(rows):
         for h in range(lanes // wide):
-            tile = both[r * count : (r + 1) * count, h * wide : (h + 1) * wide]
+            tile = both[r * lines : (r + 1) * lines, h * wide : (h + 1) * wide]
             moved = tile
-            for turn in range(1, count):
+            for turn in range(1, lines):
                 turned = roll(roll(tile, -turn, 0), turn * pair, 1)
-                moved = jnp.where((group - to + count) % count == turn, turned, moved)
-            for i in range(count):
+                moved = jnp.where((group - to + lines) % lines == turn, turned, moved)
+            for i in range(lines):
                 for p in range(par):
-                    out_ref[(h * count + i) * par + p, r : r + 1, :] = moved[i : i + 1, :]
+                    out_ref[(h * lines + i) * par + p, r : r + 1, :] = moved[i : i + 1, :]
 
 
 def home_kernel(got_ref, basis_ref, noise_ref, residual_ref, applied_ref):
@@ -262,54 +330,58 @@
 def body_fast(vectors, observed, operator, noise, coefficient, offsets):
     sen, par = lax.axis_size("sen"), lax.axis_size("par")
     rows, sensors, length = vectors.shape
-    half = length // 2
     width = coefficient.shape[1]
     shares = sen * par
-    each = half // shares
+    each = length // 2 // shares
     pair = 2 * sensors
+    wide = 2 * each * pair
     axes = ("sen", "par")
-    basis = make_basis(length)
-
-    cut = operator.reshape(2, shares, each, sensors, width).transpose(1, 2, 0, 3, 4)
-    cut = cut.reshape(shares, each, pair, width)
-    cut, vectors, observed, coefficient, offsets = lax.optimization_barrier(
-        (cut, vectors, observed, coefficient, offsets)
-    )
-    resp = lax.all_to_all(cut, axes, 0, 0, tiled=True)
-    resp = resp.reshape(sen, par, each, pair, width)
-
-    both = jnp.stack([vectors, observed])
-    spectra = jnp.dot(
-        both.reshape(2 * rows * sensors, length), basis, precision=lax.Precision.HIGHEST
-    )
-    spectra = spectra.reshape(2, rows, sensors, 2, shares, each)
-    rest = spectra[1] - noise[None, :, None, None, None] * spectra[0]
-    spectra = jnp.stack([spectra[0], rest]).transpose(4, 0, 1, 5, 3, 2)
-    spectra = lax.all_to_all(
-        spectra.reshape(shares, 1, 4 * rows * each * sensors), axes, 0, 0, tiled=True
-    )
-    spectra = spectra.reshape(sen, par, 2, rows, each, 2, sensors)[:, 0]
-    own, rest = spectra.transpose(1, 2, 3, 4, 0, 5)
-    other = jnp.stack([own[:, :, 1], -own[:, :, 0]], axis=2)
-    lines, lanes = rows * each * 2, sen * pair
-    own = jnp.stack([own, other], axis=4).reshape(lines, lanes)
-    rest = jnp.stack([rest, jnp.zeros_like(rest)], axis=4).reshape(lines, lanes)
+    basis = make_basis(length).reshape(length, 2, shares, each)
+    noise = noise[:, None]
+    whole = lambda shape: pl.BlockSpec(shape, lambda i: (0,) * len(shape))
+
+    steps = 4 if shares % 4 == 0 else 1
+    some = shares // steps
+    tall = each * width // wide * pair + 2 * each
+    message = pl.pallas_call(
+        outbound_kernel,
+        grid=(steps,),
+        in_specs=[
+            pl.BlockSpec((2, some, each, sensors, width), lambda i: (0, i, 0, 0, 0)),
+            whole(vectors.shape),
+            whole(observed.shape),
+            whole(noise.shape),
+            whole((length, length)),
+        ],
+        out_specs=pl.BlockSpec((some, tall, wide), lambda i: (i, 0, 0)),
+        out_shape=jax.ShapeDtypeStruct((shares, tall, wide), jnp.bfloat16),
+        scratch_shapes=[pltpu.VMEM((shares, 2 * each, wide), jnp.float32)],
+        compiler_params=pltpu.CompilerParams(vmem_limit_bytes=32 * 2**20),
+        name="outbound",
+    )(
+        operator.reshape(2, shares, each, sensors, width),
+        vectors,
+        observed,
+        noise,
+        jnp.asarray(basis.transpose(2, 3, 1, 0).reshape(length, length)),
+    )
+    got = lax.all_to_all(message, axes, 0, 0, tiled=True).reshape(sen, par, tall, wide)
+
     grid = jnp.concatenate([coefficient, offsets.astype(jnp.float32)])
     grid = lax.all_gather(grid, "par").transpose(1, 0, 2)
-
     message = pl.pallas_call(
-        local_kernel,
-        out_shape=jax.ShapeDtypeStruct((shares, rows, 2 * each * pair), jnp.float32),
+        functools.partial(local_kernel, each),
+        out_shape=jax.ShapeDtypeStruct((shares, rows, wide), jnp.float32),
         compiler_params=pltpu.CompilerParams(vmem_limit_bytes=32 * 2**20),
         name="local_hessians",
-    )(resp, own, rest, grid[0], grid[1].astype(jnp.int32))
+    )(got, grid[0], grid[1].astype(jnp.int32))
     got = lax.all_to_all(message, axes, 0, 0, tiled=True)
-    turned = basis.reshape(length, 2, shares, each).transpose(3, 1, 2, 0).reshape(length, length)
     return pl.pallas_call(
         home_kernel,
         out_shape=[jax.ShapeDtypeStruct((rows, sensors, length), jnp.float32)] * 2,
+        compiler_params=pltpu.CompilerParams(vmem_limit_bytes=16 * 2**20),
         name="to_time",
-    )(got, jnp.asarray(turned), noise[:, None])
+    )(got, jnp.asarray(basis.transpose(3, 1, 2, 0).reshape(length, length)), noise)
 
 
 def fits(mesh, args):
@@ -320,7 +392,7 @@
     if half % (sen * par) or sensors % sen or coefficient.shape[0] != par:
         return False
     each, pair = half // (sen * par), 2 * (sensors // sen)
-    return 2 * each * pair == 128 and 2 * each == 8 and sen * pair % 128 == 0 and coefficient.shape[1] % 128 == 0
+    return 2 * each * pair == 128 and 2 * each == 8 and 3 * rows * pair <= 128 and sen * pair % 128 == 0 and coefficient.shape[1] % 128 == 0
 
 
 def solution(mesh):

time: 76.9 us -> 69.2 us (0.90)
  blocking collectives: 16.1 us -> 12.9 us
  waiting for transfers between devices: 39.9 us -> 37 us
  local copies, waits for them, and re-layouts: 7.25 us -> 4.54 us
  Pallas kernels: 5.2 us -> 6.32 us
  starting transfers between devices: 6.37 us -> 7.3 us
    all_to_all x1, blocking collectives: 14.4 us -> 11 us  [body_fast(): got = lax.all_to_all(message, axes, 0, 0, tiled=True)]
    unnamed x15 -> x14, local copies, waits for them, and re-layouts: 0.77 us -> 3.8 us
    transpose x3 -> x0, local copies, waits for them, and re-layouts: 2.93 us -> none  [the longest x1 2.9 us: body_fast(): operator.reshape(2, shares, each, sensors, width).transpose(1, 2, 0, 3, 4)]
    all_to_all x2 -> x1, waiting for transfers between devices: 39.9 us -> 37 us  [body_fast(): lax.all_to_all(message, axes, 0, 0, tiled=True)]
    pallas_call x1 -> x2, Pallas kernels: 3.27 us -> 5.34 us  [the longest x1 2.87 us: body_fast(): pl.pallas_call(functools.partial(local_kernel, each), out_shape=jax.Shape...]
    reshape x4 -> x0, local copies, waits for them, and re-layouts: 1.61 us -> none  [the longest x1 0.8 us: body_fast(): spectra = spectra.reshape(sen, par, 2, rows, each, 2, sensors)[:, 0]]
    pallas_call x1, Pallas kernels: 1.92 us -> 0.97 us  [body_fast(): pl.pallas_call(home_kernel, out_shape=[jax.ShapeDtypeStruct((rows, sensor...]
    all_to_all x2 -> x1, starting transfers between devices: 6.37 us -> 7.3 us  [body_fast(): lax.all_to_all(message, axes, 0, 0, tiled=True)]
  transfers between devices with their start and end apart: 2 -> 1, of which waited for: 2 -> 1; matrix products, arithmetic and copies ran while one was open for 4% -> 0% of each run, Pallas kernels for 0% -> 0%
where the time goes in v3:
time: 69.2 us; the launch traced here: 68.8 us
  waiting for transfers between devices  37 us (53%)
  blocking collectives  12.9 us (19%)
  starting transfers between devices  7.3 us (11%)
  Pallas kernels  6.32 us (9%)
  local copies, waits for them, and re-layouts  4.54 us (7%)
  between operations  0.7 us (1%)
    all_to_all x1, waiting for transfers between devices, body_fast(): lax.all_to_all(message, axes, 0, 0, tiled=True)  37 us
    all_to_all x1, blocking collectives, body_fast(): got = lax.all_to_all(message, axes, 0, 0, tiled=True)  11 us
    all_to_all x1, starting transfers between devices, body_fast(): lax.all_to_all(message, axes, 0, 0, tiled=True)  7.3 us
    unnamed x14, local copies, waits for them, and re-layouts  3.8 us
    pallas_call x1, Pallas kernels, body_fast(): pl.pallas_call(functools.partial(local_kernel, each), out_shape=jax.Shape...  2.87 us
    pallas_call x1, Pallas kernels, body_fast(): pl.pallas_call(outbound_kernel, grid=(steps,), in_specs=[pl.BlockSpec((2,...  2.47 us
    all_gather x1, blocking collectives, body_fast(): grid = lax.all_gather(grid, 'par').transpose(1, 0, 2)  1.92 us
  transfers between devices with their start and end apart: 1, of which 1 were waited for; matrix products, arithmetic and copies ran while one was open for 0% of the time, Pallas kernels for 0%

profile of v3, /device:TPU:0, one launch (start us, length us, event | category | flops | bytes accessed | tf_op | source)
XLA Modules:
  0.0 68.8 jit_solution(14743251648583262615)
XLA Ops:
  0.6 0.7 %copy.12.noise_ref = f32[8,1]{1,0:T(8,128)S(1)} copy(f32[8,1]{0,1:T(1,128)} %bitcast.15) | data formatting | bytes 64 | tf_op jit(solution)/shard_map/broadcast_in_dim | solution.py:340
  1.4 0.0 copy-start
  1.4 1.4 %copy-done = bf16[2,128,8,384]{3,2,1,0:T(8,128)(2,1)S(1)} copy-done((bf16[2,128,8,384]{3,2,1,0:T(8,128)(2,1)S(1)}, bf16[2,128,8,384]{3,2,1,0:T(8,128)(2,1)}, u32[]{:S(2)}) %copy-start) | copy-done | bytes 1572888
  2.8 0.0 copy-start.2
  2.8 0.9 %copy-done.2 = f32[256,256]{1,0:T(8,128)S(1)} copy-done((f32[256,256]{1,0:T(8,128)S(1)}, f32[256,256]{1,0:T(8,128)}, u32[]{:S(2)}) %copy-start.2) | copy-done | bytes 262168
  3.7 0.0 copy-start.3
  3.7 0.7 %copy-done.3 = f32[2,8,256]{2,1,0:T(8,128)S(1)} copy-done((f32[2,8,256]{2,1,0:T(8,128)S(1)}, f32[2,8,256]{2,1,0:T(8,128)}, u32[]{:S(2)}) %copy-start.3) | copy-done | bytes 16408
  4.4 0.0 copy-start.4
  4.4 0.7 %copy-done.4 = f32[2,8,256]{2,1,0:T(8,128)S(1)} copy-done((f32[2,8,256]{2,1,0:T(8,128)S(1)}, f32[2,8,256]{2,1,0:T(8,128)}, u32[]{:S(2)}) %copy-start.4) | copy-done | bytes 16408
  5.2 2.5 %outbound.1 = bf16[32,200,128]{2,1,0:T(8,128)(2,1)} custom-call(bf16[2,32,4,8,384]{4,3,2,1,0:T(8,128)(2,1)S(1)} %bitcast.13, f32[2,8,256]{2,1,0:T(8,128)S(1)} %copy-done.3, f32[2,8,256]{2,1,0:T(8,128)S(1)} %copy-done.4, f32[8,1]{1,0:T(8,128)S(1)} %copy.12.noise_ref, f32[256,256]{1,0:T(8,128)S(1)} %copy-done.2), custom_call_target="tpu_custom_call" | custom-call | tf_op jit(solution)/shard_map/outbound/pallas_call | solution.py:346
  7.6 0.0 copy-start.5
  7.6 0.0 copy-start.6
  7.6 7.3 %all-to-all-start = ((bf16[32,200,128]{2,1,0:T(8,128)(2,1)}), bf16[32,200,128]{2,1,0:T(8,128)(2,1)S(1)}, u32[]{:S(2)}, u32[]{:S(2)}) async-start(bf16[32,200,128]{2,1,0:T(8,128)(2,1)} %outbound.1), calls=%async_computation | async-start | bytes 3276800 | tf_op jit(solution)/shard_map/all_to_all | solution.py:368
  14.9 0.0 copy-done.5
  14.9 0.0 copy-start.1
  15.0 0.0 copy-done.6
  15.0 1.9 %all-gather.1 = f32[2,2,384]{2,1,0:T(2,128)S(1)} all-gather(f32[1,2,384]{2,1,0:T(2,128)S(1)} %maximum_bitcast_fusion), channel_id=2, replica_groups=mesh['sen'=16,'par'=2] {'par'}, dimensions={0}, use_global_device_ids=true | all-gather | bytes 9216 | tf_op jit(solution)/shard_map/all_gather | solution.py:371
  16.9 37.0 %all-to-all-done = bf16[32,200,128]{2,1,0:T(8,128)(2,1)S(1)} async-done(((bf16[32,200,128]{2,1,0:T(8,128)(2,1)}), bf16[32,200,128]{2,1,0:T(8,128)(2,1)S(1)}, u32[]{:S(2)}, u32[]{:S(2)}) %all-to-all-start) | async-done | bytes 1638432 | tf_op jit(solution)/shard_map/all_to_all | solution.py:368
  54.0 2.9 %local_hessians.1 = f32[32,2,128]{2,1,0:T(2,128)S(1)} custom-call(bf16[16,2,200,128]{3,2,1,0:T(8,128)(2,1)S(1)} %bitcast.12, f32[2,384]{1,0:T(2,128)S(1)} %get-tuple-element.3.coef_ref, s32[2,384]{1,0:T(2,128)S(1)} %get-tuple-element.2.link_ref), custom_call_target="tpu_custom_call" | custom-call | tf_op jit(solution)/shard_map/local_hessians/pallas_call | solution.py:372
  56.8 11.0 %all_to_all.10.got_ref = f32[32,2,128]{2,1,0:T(2,128)S(1)} all-to-all(f32[32,2,128]{2,1,0:T(2,128)S(1)} %local_hessians.1), channel_id=1, replica_groups=mesh['sen'=16,'par'=2] {'sen','par'}, dimensions={0} | all-to-all | bytes 65536 | tf_op jit(solution)/shard_map/all_to_all | solution.py:378
  67.8 0.0 copy-done.1
  67.8 1.0 %to_time.1 = (f32[2,8,256]{2,1,0:T(8,128)}, f32[2,8,256]{2,1,0:T(8,128)}) custom-call(f32[32,2,128]{2,1,0:T(2,128)S(1)} %all_to_all.10.got_ref, f32[256,256]{1,0:T(8,128)S(1)} %copy-done.1, f32[8,1]{1,0:T(8,128)S(1)} %copy.12.noise_ref), custom_call_target="tpu_custom_call" | custom-call | tf_op jit(solution)/shard_map/to_time/pallas_call | solution.py:379
  (4 shorter events, 0.0 us)
Async XLA Ops:
  1.4 1.4 %copy-start = (bf16[2,128,8,384]{3,2,1,0:T(8,128)(2,1)S(1)}, bf16[2,128,8,384]{3,2,1,0:T(8,128)(2,1)}, u32[]{:S(2)}) copy-start(bf16[2,128,8,384]{3,2,1,0:T(8,128)(2,1)} %param.10) | copy-start | bytes 4718596
  2.8 0.9 %copy-start.2 = (f32[256,256]{1,0:T(8,128)S(1)}, f32[256,256]{1,0:T(8,128)}, u32[]{:S(2)}) copy-start(f32[256,256]{1,0:T(8,128)} %constant.4.clone.basis_ref) | copy-start | bytes 786436
  3.7 0.7 %copy-start.3 = (f32[2,8,256]{2,1,0:T(8,128)S(1)}, f32[2,8,256]{2,1,0:T(8,128)}, u32[]{:S(2)}) copy-start(f32[2,8,256]{2,1,0:T(8,128)} %vectors_ref.1) | copy-start | bytes 49156
  4.4 0.7 %copy-start.4 = (f32[2,8,256]{2,1,0:T(8,128)S(1)}, f32[2,8,256]{2,1,0:T(8,128)}, u32[]{:S(2)}) copy-start(f32[2,8,256]{2,1,0:T(8,128)} %observed_ref.1) | copy-start | bytes 49156
  7.6 7.3 %copy-start.5 = (s32[1,384]{1,0:T(1,128)S(1)}, s32[1,384]{1,0:T(1,128)}, u32[]{:S(2)}) copy-start(s32[1,384]{1,0:T(1,128)} %param.13) | copy-start | bytes 4612
  7.6 7.3 %copy-start.6 = (f32[1,384]{1,0:T(1,128)S(1)}, f32[1,384]{1,0:T(1,128)}, u32[]{:S(2)}) copy-start(f32[1,384]{1,0:T(1,128)} %param.12) | copy-start | bytes 4612
  7.6 46.3 %all-to-all-start = ((bf16[32,200,128]{2,1,0:T(8,128)(2,1)}), bf16[32,200,128]{2,1,0:T(8,128)(2,1)S(1)}, u32[]{:S(2)}, u32[]{:S(2)}) async-start(bf16[32,200,128]{2,1,0:T(8,128)(2,1)} %outbound.1), calls=%async_computation | async-start | bytes 3276800 | tf_op jit(solution)/shard_map/all_to_all | solution.py:368
  14.9 52.9 %copy-start.1 = (f32[256,256]{1,0:T(8,128)S(1)}, f32[256,256]{1,0:T(8,128)}, u32[]{:S(2)}) copy-start(f32[256,256]{1,0:T(8,128)} %constant.5.clone.basis_ref) | copy-start | bytes 786436

commit v4 on v3

--- a/solution.py
+++ b/solution.py
@@ -155,6 +155,13 @@
     return lax.broadcasted_iota(jnp.int32, shape, axis)
 
 
+def upright(line):
+    count = line.shape[1]
+    square = jnp.broadcast_to(line, (count, count))
+    square = jnp.where(iota((count, count), 0) == iota((count, count), 1), square, 0.0)
+    return jnp.sum(square, axis=1, keepdims=True)
+
+
 def outbound_kernel(resp_ref, vectors_ref, observed_ref, noise_ref, basis_ref, out_ref, spectra_ref):
     _, devices, each, sensors, width = resp_ref.shape
     pair, lines = 2 * sensors, 2 * each
@@ -164,10 +171,11 @@
     @pl.when(pl.program_id(0) == 0)
     def _():
         rows = vectors_ref.shape[0]
+        noise = upright(noise_ref[...])
         records = []
         for r in range(rows):
             record = vectors_ref[r]
-            records += [record, observed_ref[r] - noise_ref[...] * record]
+            records += [record, observed_ref[r] - noise * record]
         filled = rows * pair
         records.append(jnp.zeros((wide - filled, records[0].shape[1]), jnp.float32))
         spectra = lax.dot_general(
@@ -307,8 +315,9 @@
 
 def home_kernel(got_ref, basis_ref, noise_ref, residual_ref, applied_ref):
     sources, rows, wide = got_ref.shape
-    sensors = noise_ref.shape[0]
+    sensors = noise_ref.shape[1]
     pair = 2 * sensors
+    noise = upright(noise_ref[...])
     lines = []
     for r in range(rows):
         turned = got_ref[:, r, :].T
@@ -324,7 +333,7 @@
     for r in range(rows):
         residual = back[r * pair : r * pair + sensors]
         residual_ref[r] = residual
-        applied_ref[r] = back[r * pair + sensors : (r + 1) * pair] + noise_ref[...] * residual
+        applied_ref[r] = back[r * pair + sensors : (r + 1) * pair] + noise * residual
 
 
 def body_fast(vectors, observed, operator, noise, coefficient, offsets):
@@ -337,7 +346,7 @@
     wide = 2 * each * pair
     axes = ("sen", "par")
     basis = make_basis(length).reshape(length, 2, shares, each)
-    noise = noise[:, None]
+    noise = noise[None, :]
     whole = lambda shape: pl.BlockSpec(shape, lambda i: (0,) * len(shape))
 
     steps = 4 if shares % 4 == 0 else 1
@@ -356,7 +365,7 @@
         out_specs=pl.BlockSpec((some, tall, wide), lambda i: (i, 0, 0)),
         out_shape=jax.ShapeDtypeStruct((shares, tall, wide), jnp.bfloat16),
         scratch_shapes=[pltpu.VMEM((shares, 2 * each, wide), jnp.float32)],
-        compiler_params=pltpu.CompilerParams(vmem_limit_bytes=32 * 2**20),
+        compiler_params=pltpu.CompilerParams(vmem_limit_bytes=60 * 2**20),
         name="outbound",
     )(
         operator.reshape(2, shares, each, sensors, width),

time: 69.2 us -> 66.5 us (0.961)
  local copies, waits for them, and re-layouts: 4.54 us -> 0.02 us
  Pallas kernels: 6.32 us -> 8.22 us
    unnamed x14 -> x8, local copies, waits for them, and re-layouts: 3.8 us -> 0.02 us
    pallas_call x1, Pallas kernels: 2.47 us -> 4.37 us  [body_fast(): pl.pallas_call(outbound_kernel, grid=(steps,), in_specs=[pl.BlockSpec((2,...]
    broadcast_in_dim x1 -> x0, local copies, waits for them, and re-layouts: 0.73 us -> none  [body_fast(): noise = noise[:, None]]
where the time goes in v4:
time: 66.5 us; the launch traced here: 66.2 us
  waiting for transfers between devices  37 us (56%)
  blocking collectives  12.9 us (19%)
  Pallas kernels  8.22 us (12%)
  starting transfers between devices  7.3 us (11%)
  between operations  0.7 us (1%)
    all_to_all x1, waiting for transfers between devices, body_fast(): lax.all_to_all(message, axes, 0, 0, tiled=True)  37 us
    all_to_all x1, blocking collectives, body_fast(): got = lax.all_to_all(message, axes, 0, 0, tiled=True)  11 us
    all_to_all x1, starting transfers between devices, body_fast(): lax.all_to_all(message, axes, 0, 0, tiled=True)  7.3 us
    pallas_call x1, Pallas kernels, body_fast(): pl.pallas_call(outbound_kernel, grid=(steps,), in_specs=[pl.BlockSpec((2,...  4.37 us
    pallas_call x1, Pallas kernels, body_fast(): pl.pallas_call(functools.partial(local_kernel, each), out_shape=jax.Shape...  2.88 us
    all_gather x1, blocking collectives, body_fast(): grid = lax.all_gather(grid, 'par').transpose(1, 0, 2)  1.92 us
  transfers between devices with their start and end apart: 1, of which 1 were waited for; matrix products, arithmetic and copies ran while one was open for 0% of the time, Pallas kernels for 0%

profile of v4, /device:TPU:0, one launch (start us, length us, event | category | flops | bytes accessed | tf_op | source)
XLA Modules:
  0.0 66.2 jit_solution(18312960159981771150)
XLA Ops:
  0.6 4.4 %outbound.1 = bf16[32,200,128]{2,1,0:T(8,128)(2,1)} custom-call(bf16[2,32,4,8,384]{4,3,2,1,0:T(8,128)(2,1)} %bitcast.15, f32[2,8,256]{2,1,0:T(8,128)} %vectors_ref.1, f32[2,8,256]{2,1,0:T(8,128)} %observed_ref.1, f32[1,8]{1,0:T(1,128)} %bitcast.13, f32[256,256]{1,0:T(8,128)} %constant.4.clone.basis_ref), custom_call_target="tpu_custom_call" | custom-call | tf_op jit(solution)/shard_map/outbound/pallas_call | solution.py:355
  5.0 0.0 copy-start.2
  5.0 0.0 copy-start.3
  5.0 7.3 %all-to-all-start = ((bf16[32,200,128]{2,1,0:T(8,128)(2,1)}), bf16[32,200,128]{2,1,0:T(8,128)(2,1)S(1)}, u32[]{:S(2)}, u32[]{:S(2)}) async-start(bf16[32,200,128]{2,1,0:T(8,128)(2,1)} %outbound.1), calls=%async_computation | async-start | bytes 3276800 | tf_op jit(solution)/shard_map/all_to_all | solution.py:377
  12.3 0.0 copy-done.2
  12.3 0.0 copy-start
  12.3 0.0 copy-start.1
  12.4 0.0 copy-done.3
  12.4 1.9 %all-gather.1 = f32[2,2,384]{2,1,0:T(2,128)S(1)} all-gather(f32[1,2,384]{2,1,0:T(2,128)S(1)} %maximum_bitcast_fusion), channel_id=2, replica_groups=mesh['sen'=16,'par'=2] {'par'}, dimensions={0}, use_global_device_ids=true | all-gather | bytes 9216 | tf_op jit(solution)/shard_map/all_gather | solution.py:380
  14.3 37.0 %all-to-all-done = bf16[32,200,128]{2,1,0:T(8,128)(2,1)S(1)} async-done(((bf16[32,200,128]{2,1,0:T(8,128)(2,1)}), bf16[32,200,128]{2,1,0:T(8,128)(2,1)S(1)}, u32[]{:S(2)}, u32[]{:S(2)}) %all-to-all-start) | async-done | bytes 1638432 | tf_op jit(solution)/shard_map/all_to_all | solution.py:377
  51.3 2.9 %local_hessians.1 = f32[32,2,128]{2,1,0:T(2,128)S(1)} custom-call(bf16[16,2,200,128]{3,2,1,0:T(8,128)(2,1)S(1)} %bitcast.12, f32[2,384]{1,0:T(2,128)S(1)} %get-tuple-element.3.coef_ref, s32[2,384]{1,0:T(2,128)S(1)} %get-tuple-element.2.link_ref), custom_call_target="tpu_custom_call" | custom-call | tf_op jit(solution)/shard_map/local_hessians/pallas_call | solution.py:381
  54.2 11.0 %all_to_all.10.got_ref = f32[32,2,128]{2,1,0:T(2,128)S(1)} all-to-all(f32[32,2,128]{2,1,0:T(2,128)S(1)} %local_hessians.1), channel_id=1, replica_groups=mesh['sen'=16,'par'=2] {'sen','par'}, dimensions={0} | all-to-all | bytes 65536 | tf_op jit(solution)/shard_map/all_to_all | solution.py:387
  65.2 0.0 copy-done
  65.2 0.0 copy-done.1
  65.2 1.0 %to_time.1 = (f32[2,8,256]{2,1,0:T(8,128)}, f32[2,8,256]{2,1,0:T(8,128)}) custom-call(f32[32,2,128]{2,1,0:T(2,128)S(1)} %all_to_all.10.got_ref, f32[256,256]{1,0:T(8,128)S(1)} %copy-done, f32[1,8]{1,0:T(1,128)S(1)} %bitcast.14), custom_call_target="tpu_custom_call" | custom-call | tf_op jit(solution)/shard_map/to_time/pallas_call | solution.py:388
  (4 shorter events, 0.0 us)
Async XLA Ops:
  5.0 7.3 %copy-start.2 = (s32[1,384]{1,0:T(1,128)S(1)}, s32[1,384]{1,0:T(1,128)}, u32[]{:S(2)}) copy-start(s32[1,384]{1,0:T(1,128)} %param.13) | copy-start | bytes 4612
  5.0 7.4 %copy-start.3 = (f32[1,384]{1,0:T(1,128)S(1)}, f32[1,384]{1,0:T(1,128)}, u32[]{:S(2)}) copy-start(f32[1,384]{1,0:T(1,128)} %param.12) | copy-start | bytes 4612
  5.0 46.3 %all-to-all-start = ((bf16[32,200,128]{2,1,0:T(8,128)(2,1)}), bf16[32,200,128]{2,1,0:T(8,128)(2,1)S(1)}, u32[]{:S(2)}, u32[]{:S(2)}) async-start(bf16[32,200,128]{2,1,0:T(8,128)(2,1)} %outbound.1), calls=%async_computation | async-start | bytes 3276800 | tf_op jit(solution)/shard_map/all_to_all | solution.py:377
  12.3 52.9 %copy-start = (f32[256,256]{1,0:T(8,128)S(1)}, f32[256,256]{1,0:T(8,128)}, u32[]{:S(2)}) copy-start(f32[256,256]{1,0:T(8,128)} %constant.5.clone.basis_ref) | copy-start | bytes 786436
  12.3 52.9 %copy-start.1 = (f32[8]{0:T(128)S(1)}, f32[8]{0:T(128)}, u32[]{:S(2)}) copy-start(f32[8]{0:T(128)} %param.11) | copy-start | bytes 100

commit v5 on v4

--- a/solution.py
+++ b/solution.py
@@ -7,10 +7,13 @@
 from jax import lax
 from jax.experimental import pallas as pl
 from jax.experimental.pallas import tpu as pltpu
+from jax.sharding import Mesh
 from jax.sharding import PartitionSpec as P
 
 SWEEPS = 4
 REACH = 3
+LANES = 128
+DEPTH = 256
 
 
 def make_basis(length):
@@ -204,126 +207,187 @@
     )
 
 
-def local_kernel(each, got_ref, coef_ref, link_ref, out_ref):
-    sen, par, _, wide = got_ref.shape
-    width = coef_ref.shape[1]
-    tiles = width // wide
-    rows = out_ref.shape[1]
-    lines = 2 * each
-    pair = wide // lines
-    sensors = pair // 2
-    held, lanes = rows * lines, sen * pair
-    per = wide // pair
-    body_rows = each * tiles * pair
-
-    tail = got_ref[:, 0, pl.ds(body_rows, lines), :].astype(jnp.float32)
-    parts = rows * pair
-    at = iota((lines, wide), 1) // pair
-    spectra = [[jnp.zeros((lines, wide), jnp.float32) for _ in range(lanes // wide)] for _ in range(rows)]
-    for i in range(sen):
-        packed = tail[i]
-        packed = packed + roll(packed, -parts, 1) + roll(packed, -2 * parts, 1)
-        h, place = divmod(i, per)
-        for r in range(rows):
-            moved = roll(packed, (place - r) * pair, 1)
-            spectra[r][h] = jnp.where(at == place, moved, spectra[r][h])
-    spectra = jnp.concatenate([jnp.concatenate(line, axis=1) for line in spectra], axis=0)
-
-    row, lane = iota((held, lanes), 0), iota((held, lanes), 1)
-    real_row = row % 2 == 0
-    real_lane = lane // sensors % 2 == 0
-    freq = row // 2 % each
-
-    def swapped(x):
-        return jnp.where(real_row, roll(x, -1, 0), roll(x, 1, 0))
-
-    shape = (held, width)
-    column = iota(shape, 1)
-    coefs, links = [], []
-    for x in range(par):
-        coefs.append(jnp.broadcast_to(coef_ref[x : x + 1, :], shape))
-        offset = jnp.broadcast_to(link_ref[x : x + 1, :], shape)
-        masks = []
-        for shift in range(-REACH, REACH + 1):
-            inside = (column + shift >= 0) & (column + shift < width)
-            masks.append(jnp.where((offset == shift) & inside, 1.0, 0.0))
-        links.append(masks)
-    after_first = jnp.where(column > 0, 1.0, 0.0)
-    before_last = jnp.where(column < width - 1, 1.0, 0.0)
-
-    def block(f, p):
+class Share:
+    def __init__(self, got_ref, rows, each, width):
+        self.got = got_ref
+        self.low, self.par = got_ref.shape[:2]
+        self.rows, self.each, self.width = rows, each, width
+        self.lines = 2 * each
+        self.tiles = width // LANES
+        self.pair = (got_ref.shape[2] - self.lines) // (each * self.tiles)
+        self.sensors = self.pair // 2
+        self.lanes = self.low * self.pair
+        self.held = rows * self.lines
+        shape = (self.held, self.lanes)
+        row = iota(shape, 0)
+        self.real_row = row % 2 == 0
+        self.real_lane = iota(shape, 1) // self.sensors % 2 == 0
+        self.freq = row // 2 % each
+        self.joint = max(1, min(each, DEPTH // self.lanes))
+
+    def swapped(self, x):
+        return jnp.where(self.real_row, roll(x, -1, 0), roll(x, 1, 0))
+
+    def block(self, first, p):
         return jnp.concatenate(
             [
-                got_ref[:, p, pl.ds((f * tiles + j) * pair, pair), :].reshape(lanes, wide)
-                for j in range(tiles)
+                jnp.concatenate(
+                    [
+                        self.got[
+                            :, p, pl.ds((f * self.tiles + j) * self.pair, self.pair), :
+                        ].reshape(self.lanes, LANES)
+                        for j in range(self.tiles)
+                    ],
+                    axis=1,
+                )
+                for f in range(first, first + self.joint)
             ],
-            axis=1,
+            axis=0,
         )
 
-    def hessian(record):
-        crossed = swapped(record)
-        crossed = roll(jnp.where(real_row, crossed, -crossed), sensors, 1)
-        left = jnp.where(real_lane, record, crossed)
-        field = []
-        for p in range(par):
-            total = jnp.zeros(shape, jnp.float32)
-            for f in range(each):
-                part = jnp.where(freq == f, left, 0.0).astype(jnp.bfloat16)
-                total += jnp.dot(part, block(f, p), preferred_element_type=jnp.float32)
-            field.append(total)
+    def spectra(self):
+        tail = self.got[:, 0, pl.ds(self.got.shape[2] - self.lines, self.lines), :]
+        tail = tail.astype(jnp.float32)
+        filled = self.rows * self.pair
+        shape = (self.lines, LANES)
+        at = iota(shape, 1) // self.pair
+        per = LANES // self.pair
+        found = [
+            [jnp.zeros(shape, jnp.float32) for _ in range(self.lanes // LANES)]
+            for _ in range(self.rows)
+        ]
+        for i in range(self.low):
+            packed = tail[i]
+            packed = packed + roll(packed, -filled, 1) + roll(packed, -2 * filled, 1)
+            h, place = divmod(i, per)
+            for r in range(self.rows):
+                moved = roll(packed, (place - r) * self.pair, 1)
+                found[r][h] = jnp.where(at == place, moved, found[r][h])
+        return jnp.concatenate([jnp.concatenate(line, axis=1) for line in found], axis=0)
+
+    def adjoint(self, record):
+        crossed = self.swapped(record)
+        crossed = roll(jnp.where(self.real_row, crossed, -crossed), self.sensors, 1)
+        left = jnp.where(self.real_lane, record, crossed)
+        sums = [jnp.zeros((self.held, self.width), jnp.float32) for _ in range(self.par)]
+        for first in range(0, self.each, self.joint):
+            part = [
+                jnp.where(self.freq == f, left, 0.0) for f in range(first, first + self.joint)
+            ]
+            part = jnp.concatenate(part, axis=1).astype(jnp.bfloat16)
+            for p in range(self.par):
+                sums[p] += jnp.dot(
+                    part, self.block(first, p), preferred_element_type=jnp.float32
+                )
+        return sums
+
+    def smoothed(self, field, coef_ref, link_ref):
+        shape = (self.held, self.width)
+        column = iota((1, self.width), 1)
+        coefs, links = [], []
+        for x in range(self.par):
+            coefs.append(jnp.broadcast_to(coef_ref[x : x + 1, :], shape))
+            offset = link_ref[x : x + 1, :]
+            masks = []
+            for shift in range(-REACH, REACH + 1):
+                inside = (column + shift >= 0) & (column + shift < self.width)
+                mask = jnp.where((offset == shift) & inside, 1.0, 0.0)
+                masks.append(jnp.broadcast_to(mask, shape))
+            links.append(masks)
+        after_first = jnp.broadcast_to(jnp.where(column > 0, 1.0, 0.0), shape)
+        before_last = jnp.broadcast_to(jnp.where(column < self.width - 1, 1.0, 0.0), shape)
         for _ in range(SWEEPS):
             after = []
             for x, u in enumerate(field):
                 around = roll(u, 1, 1) * after_first + roll(u, -1, 1) * before_last
                 if x > 0:
                     around += field[x - 1]
-                if x < par - 1:
+                if x < self.par - 1:
                     linked = jnp.zeros(shape, jnp.float32)
                     for mask, shift in zip(links[x], range(-REACH, REACH + 1)):
                         linked += mask * roll(field[x + 1], -shift, 1)
                     around += linked
                 after.append(u + coefs[x] * (around - 4.0 * u))
             field = after
+        return field
+
+    def forward(self, field):
         prior = [u.astype(jnp.bfloat16) for u in field]
-        out = jnp.zeros((held, lanes), jnp.float32)
-        for f in range(each):
-            part = jnp.zeros((held, lanes), jnp.float32)
-            for p in range(par):
+        out = jnp.zeros((self.held, self.lanes), jnp.float32)
+        for first in range(0, self.each, self.joint):
+            part = jnp.zeros((self.held, self.joint * self.lanes), jnp.float32)
+            for p in range(self.par):
                 part += lax.dot_general(
-                    prior[p], block(f, p), (((1,), (1,)), ((), ())), preferred_element_type=jnp.float32
+                    prior[p],
+                    self.block(first, p),
+                    (((1,), (1,)), ((), ())),
+                    preferred_element_type=jnp.float32,
                 )
-            out = jnp.where(freq == f, part, out)
-        crossed = swapped(roll(out, -sensors, 1))
-        return out + jnp.where(real_row, -crossed, crossed)
-
-    residual = roll(spectra, -sensors, 1) - hessian(spectra)
-    applied = hessian(residual)
-    both = jnp.where(real_lane, residual, roll(applied, sensors, 1))
-
-    to, group = iota((lines, wide), 0), iota((lines, wide), 1) // pair
-    for r in range(rows):
-        for h in range(lanes // wide):
-            tile = both[r * lines : (r + 1) * lines, h * wide : (h + 1) * wide]
-            moved = tile
-            for turn in range(1, lines):
-                turned = roll(roll(tile, -turn, 0), turn * pair, 1)
-                moved = jnp.where((group - to + lines) % lines == turn, turned, moved)
-            for i in range(lines):
-                for p in range(par):
-                    out_ref[(h * lines + i) * par + p, r : r + 1, :] = moved[i : i + 1, :]
+            for i in range(self.joint):
+                own = part[:, i * self.lanes : (i + 1) * self.lanes]
+                out = jnp.where(self.freq == first + i, own, out)
+        crossed = self.swapped(roll(out, -self.sensors, 1))
+        return out + jnp.where(self.real_row, -crossed, crossed)
+
+    def messages(self, residual, applied, out_ref):
+        both = jnp.where(self.real_lane, residual, roll(applied, self.sensors, 1))
+        per = LANES // self.pair
+        to, group = iota((per, LANES), 0), iota((per, LANES), 1) // self.pair
+        for g in range(self.held // per):
+            for h in range(self.lanes // LANES):
+                tile = both[g * per : (g + 1) * per, h * LANES : (h + 1) * LANES]
+                moved = tile
+                for turn in range(1, per):
+                    turned = roll(roll(tile, -turn, 0), turn * self.pair, 1)
+                    moved = jnp.where((group - to + per) % per == turn, turned, moved)
+                for i in range(per):
+                    for p in range(self.par):
+                        out_ref[(h * per + i) * self.par + p, g : g + 1, :] = moved[i : i + 1, :]
+
+
+def first_kernel(share, got_ref, spectra_ref, sums_ref):
+    share = share(got_ref)
+    spectra = share.spectra()
+    spectra_ref[...] = spectra
+    for p, part in enumerate(share.adjoint(spectra)):
+        sums_ref[p] = part
+
+
+def summed(one_ref, other_ref):
+    return [one_ref[x] + other_ref[x] for x in range(one_ref.shape[0])]
+
+
+def middle_kernel(
+    share, got_ref, one_ref, other_ref, spectra_ref, coef_ref, link_ref, residual_ref, sums_ref
+):
+    share = share(got_ref)
+    rest = roll(spectra_ref[...], -share.sensors, 1)
+    field = share.smoothed(summed(one_ref, other_ref), coef_ref, link_ref)
+    residual = rest - share.forward(field)
+    residual_ref[...] = residual
+    for p, part in enumerate(share.adjoint(residual)):
+        sums_ref[p] = part
+
+
+def last_kernel(share, got_ref, one_ref, other_ref, residual_ref, coef_ref, link_ref, out_ref):
+    share = share(got_ref)
+    field = share.smoothed(summed(one_ref, other_ref), coef_ref, link_ref)
+    share.messages(residual_ref[...], share.forward(field), out_ref)
 
 
 def home_kernel(got_ref, basis_ref, noise_ref, residual_ref, applied_ref):
-    sources, rows, wide = got_ref.shape
     sensors = noise_ref.shape[1]
+    rows = residual_ref.shape[0]
     pair = 2 * sensors
     noise = upright(noise_ref[...])
+    groups = got_ref.shape[1] // rows
     lines = []
     for r in range(rows):
-        turned = got_ref[:, r, :].T
-        lines.append(
-            jnp.concatenate([turned[i : i + pair, :] for i in range(0, wide, pair)], axis=1)
-        )
+        parts = []
+        for g in range(groups):
+            turned = got_ref[:, r * groups + g, :].T
+            parts += [turned[i : i + pair, :] for i in range(0, LANES, pair)]
+        lines.append(jnp.concatenate(parts, axis=1))
     back = jnp.dot(
         jnp.concatenate(lines, axis=0),
         basis_ref[...],
@@ -337,21 +401,22 @@
 
 
 def body_fast(vectors, observed, operator, noise, coefficient, offsets):
-    sen, par = lax.axis_size("sen"), lax.axis_size("par")
+    top, low, par = (lax.axis_size(axis) for axis in ("top", "low", "par"))
     rows, sensors, length = vectors.shape
     width = coefficient.shape[1]
-    shares = sen * par
+    shares = low * par
     each = length // 2 // shares
     pair = 2 * sensors
-    wide = 2 * each * pair
-    axes = ("sen", "par")
+    axes = ("low", "par")
     basis = make_basis(length).reshape(length, 2, shares, each)
     noise = noise[None, :]
     whole = lambda shape: pl.BlockSpec(shape, lambda i: (0,) * len(shape))
+    f32 = lambda *shape: jax.ShapeDtypeStruct(shape, jnp.float32)
+    room = lambda mib: pltpu.CompilerParams(vmem_limit_bytes=mib * 2**20)
 
     steps = 4 if shares % 4 == 0 else 1
     some = shares // steps
-    tall = each * width // wide * pair + 2 * each
+    tall = each * width // LANES * pair + 2 * each
     message = pl.pallas_call(
         outbound_kernel,
         grid=(steps,),
@@ -362,10 +427,10 @@
             whole(noise.shape),
             whole((length, length)),
         ],
-        out_specs=pl.BlockSpec((some, tall, wide), lambda i: (i, 0, 0)),
-        out_shape=jax.ShapeDtypeStruct((shares, tall, wide), jnp.bfloat16),
-        scratch_shapes=[pltpu.VMEM((shares, 2 * each, wide), jnp.float32)],
-        compiler_params=pltpu.CompilerParams(vmem_limit_bytes=60 * 2**20),
+        out_specs=pl.BlockSpec((some, tall, LANES), lambda i: (i, 0, 0)),
+        out_shape=jax.ShapeDtypeStruct((shares, tall, LANES), jnp.bfloat16),
+        scratch_shapes=[pltpu.VMEM((shares, 2 * each, LANES), jnp.float32)],
+        compiler_params=room(60),
         name="outbound",
     )(
         operator.reshape(2, shares, each, sensors, width),
@@ -374,21 +439,41 @@
         noise,
         jnp.asarray(basis.transpose(2, 3, 1, 0).reshape(length, length)),
     )
-    got = lax.all_to_all(message, axes, 0, 0, tiled=True).reshape(sen, par, tall, wide)
+    got = lax.all_to_all(message, axes, 0, 0, tiled=True).reshape(low, par, tall, LANES)
 
     grid = jnp.concatenate([coefficient, offsets.astype(jnp.float32)])
     grid = lax.all_gather(grid, "par").transpose(1, 0, 2)
+    coefs, links = grid[0], grid[1].astype(jnp.int32)
+
+    def across(sums):
+        return lax.ppermute(sums, "top", [(i, (i + 1) % top) for i in range(top)])
+
+    share = functools.partial(Share, rows=rows, each=each, width=width)
+    held, lanes = rows * 2 * each, low * pair
+    sums = f32(par, held, width)
+    spectra, one = pl.pallas_call(
+        functools.partial(first_kernel, share),
+        out_shape=[f32(held, lanes), sums],
+        compiler_params=room(32),
+        name="first_adjoint",
+    )(got)
+    residual, two = pl.pallas_call(
+        functools.partial(middle_kernel, share),
+        out_shape=[f32(held, lanes), sums],
+        compiler_params=room(32),
+        name="forward_adjoint",
+    )(got, one, across(one), spectra, coefs, links)
     message = pl.pallas_call(
-        functools.partial(local_kernel, each),
-        out_shape=jax.ShapeDtypeStruct((shares, rows, wide), jnp.float32),
-        compiler_params=pltpu.CompilerParams(vmem_limit_bytes=32 * 2**20),
-        name="local_hessians",
-    )(got, grid[0], grid[1].astype(jnp.int32))
+        functools.partial(last_kernel, share),
+        out_shape=f32(shares, held * pair // LANES, LANES),
+        compiler_params=room(32),
+        name="last_forward",
+    )(got, two, across(two), residual, coefs, links)
     got = lax.all_to_all(message, axes, 0, 0, tiled=True)
     return pl.pallas_call(
         home_kernel,
-        out_shape=[jax.ShapeDtypeStruct((rows, sensors, length), jnp.float32)] * 2,
-        compiler_params=pltpu.CompilerParams(vmem_limit_bytes=16 * 2**20),
+        out_shape=[f32(rows, sensors, length)] * 2,
+        compiler_params=room(16),
         name="to_time",
     )(got, jnp.asarray(basis.transpose(3, 1, 2, 0).reshape(length, length)), noise)
 
@@ -397,29 +482,40 @@
     vectors, _, _, _, coefficient, _ = args
     sen, par = mesh.shape["sen"], mesh.shape["par"]
     rows, sensors, length = vectors.shape
-    half = length // 2
-    if half % (sen * par) or sensors % sen or coefficient.shape[0] != par:
+    half, low = length // 2, sen // 2
+    if sen % 2 or half % (low * par) or sensors % sen or coefficient.shape[0] != par:
         return False
-    each, pair = half // (sen * par), 2 * (sensors // sen)
-    return 2 * each * pair == 128 and 2 * each == 8 and 3 * rows * pair <= 128 and sen * pair % 128 == 0 and coefficient.shape[1] % 128 == 0
+    each, pair = half // (low * par), 2 * (sensors // sen)
+    return (
+        pair == 16
+        and each % 8 == 0
+        and 3 * rows * pair <= LANES
+        and low * pair % LANES == 0
+        and coefficient.shape[1] % LANES == 0
+    )
 
 
 def solution(mesh):
-    placed = (
-        P(None, "sen", None),
-        P(None, "sen", None),
-        P(None, None, "sen", "par"),
-        P("sen"),
-        P("par", None),
-        P("par", None),
-    )
-
     def whole(*args):
+        if fits(mesh, args):
+            body, sen = body_fast, ("top", "low")
+            shape = (2, mesh.shape["sen"] // 2, mesh.shape["par"])
+            within = Mesh(mesh.devices.reshape(shape), sen + ("par",))
+        else:
+            body, sen, within = body_plain, "sen", mesh
+        record = P(None, sen, None)
         return jax.shard_map(
-            body_fast if fits(mesh, args) else body_plain,
-            mesh=mesh,
-            in_specs=placed,
-            out_specs=(P(None, "sen", None), P(None, "sen", None)),
+            body,
+            mesh=within,
+            in_specs=(
+                record,
+                record,
+                P(None, None, sen, "par"),
+                P(sen),
+                P("par", None),
+                P("par", None),
+            ),
+            out_specs=(record, record),
             check_vma=False,
         )(*args)
 

time: 66.5 us -> 63.3 us (0.952)
  waiting for transfers between devices: 37 us -> 31.8 us
  starting transfers between devices: 7.3 us -> 10.1 us
  blocking collectives: 12.9 us -> 12 us
    all_to_all x1, waiting for transfers between devices: 37 us -> 21.7 us  [body_fast(): lax.all_to_all(message, axes, 0, 0, tiled=True)]
    ppermute x0 -> x2, waiting for transfers between devices: none -> 10.1 us  [across(): return lax.ppermute(sums, 'top', [(i, (i + 1) % top) for i in range(top)])]
    ppermute x0 -> x2, starting transfers between devices: none -> 3.64 us  [across(): return lax.ppermute(sums, 'top', [(i, (i + 1) % top) for i in range(top)])]
    all_to_all x1, starting transfers between devices: 7.3 us -> 6.42 us  [body_fast(): lax.all_to_all(message, axes, 0, 0, tiled=True)]
    all_to_all x1, blocking collectives: 11 us -> 10.1 us  [body_fast(): got = lax.all_to_all(message, axes, 0, 0, tiled=True)]
    pallas_call x2 -> x4, Pallas kernels: 3.86 us -> 4.09 us  [the longest x1 1.36 us: body_fast(): pl.pallas_call(functools.partial(middle_kernel, share), out_shape=[f32(he...]
  transfers between devices with their start and end apart: 1 -> 3, of which waited for: 1 -> 3; matrix products, arithmetic and copies ran while one was open for 0% -> 0% of each run, Pallas kernels for 0% -> 0%
where the time goes in v5:
time: 63.3 us; the launch traced here: 63 us
  waiting for transfers between devices  31.8 us (50%)
  blocking collectives  12 us (19%)
  starting transfers between devices  10.1 us (16%)
  Pallas kernels  8.44 us (13%)
  between operations  0.7 us (1%)
    all_to_all x1, waiting for transfers between devices, body_fast(): lax.all_to_all(message, axes, 0, 0, tiled=True)  21.7 us
    all_to_all x1, blocking collectives, body_fast(): got = lax.all_to_all(message, axes, 0, 0, tiled=True)  10.1 us
    ppermute x2, waiting for transfers between devices, across(): return lax.ppermute(sums, 'top', [(i, (i + 1) % top) for i in range(top)])  10.1 us
    all_to_all x1, starting transfers between devices, body_fast(): lax.all_to_all(message, axes, 0, 0, tiled=True)  6.42 us
    pallas_call x1, Pallas kernels, body_fast(): pl.pallas_call(outbound_kernel, grid=(steps,), in_specs=[pl.BlockSpec((2,...  4.36 us
    ppermute x2, starting transfers between devices, across(): return lax.ppermute(sums, 'top', [(i, (i + 1) % top) for i in range(top)])  3.64 us
    all_gather x1, blocking collectives, body_fast(): grid = lax.all_gather(grid, 'par').transpose(1, 0, 2)  1.89 us
    pallas_call x1, Pallas kernels, body_fast(): pl.pallas_call(functools.partial(middle_kernel, share), out_shape=[f32(he...  1.36 us
  transfers between devices with their start and end apart: 3, of which 3 were waited for; matrix products, arithmetic and copies ran while one was open for 0% of the time, Pallas kernels for 0%

profile of v5, /device:TPU:0, one launch (start us, length us, event | category | flops | bytes accessed | tf_op | source)
XLA Modules:
  0.0 63.0 jit_solution(10301096507040057557)
XLA Ops:
  0.6 4.4 %outbound.1 = bf16[16,400,128]{2,1,0:T(8,128)(2,1)} custom-call(bf16[2,16,8,8,384]{4,3,2,1,0:T(8,128)(2,1)} %bitcast.17, f32[2,8,256]{2,1,0:T(8,128)} %vectors_ref.1, f32[2,8,256]{2,1,0:T(8,128)} %observed_ref.1, f32[1,8]{1,0:T(1,128)} %bitcast.15, f32[256,256]{1,0:T(8,128)} %constant.4.clone.basis_ref), custom_call_target="tpu_custom_call" | custom-call | tf_op jit(solution)/shard_map/outbound/pallas_call | solution.py:420
  5.0 0.0 copy-start.2
  5.0 0.0 copy-start.3
  5.0 6.4 %all-to-all-start = ((bf16[16,400,128]{2,1,0:T(8,128)(2,1)}), bf16[16,400,128]{2,1,0:T(8,128)(2,1)S(1)}, u32[]{:S(2)}, u32[]{:S(2)}) async-start(bf16[16,400,128]{2,1,0:T(8,128)(2,1)} %outbound.1), calls=%async_computation | async-start | bytes 3276800 | tf_op jit(solution)/shard_map/all_to_all | solution.py:442
  11.4 0.0 copy-done.2
  11.4 0.0 copy-done.3
  11.5 1.9 %all-gather.1 = f32[2,2,384]{2,1,0:T(2,128)S(1)} all-gather(f32[1,2,384]{2,1,0:T(2,128)S(1)} %maximum_bitcast_fusion), channel_id=2, replica_groups=mesh['top'=2,'low'=8,'par'=2] {'par'}, dimensions={0}, use_global_device_ids=true | all-gather | bytes 9216 | tf_op jit(solution)/shard_map/all_gather | solution.py:445
  13.4 21.7 %all-to-all-done = bf16[16,400,128]{2,1,0:T(8,128)(2,1)S(1)} async-done(((bf16[16,400,128]{2,1,0:T(8,128)(2,1)}), bf16[16,400,128]{2,1,0:T(8,128)(2,1)S(1)}, u32[]{:S(2)}, u32[]{:S(2)}) %all-to-all-start) | async-done | bytes 1638432 | tf_op jit(solution)/shard_map/all_to_all | solution.py:442
  35.0 0.5 first_adjoint.1
  35.6 2.7 %collective-permute-start = (f32[2,32,384]{2,1,0:T(8,128)S(1)}, f32[2,32,384]{2,1,0:T(8,128)S(1)}, u32[]{:S(2)}, u32[]{:S(2)}) collective-permute-start(f32[2,32,384]{2,1,0:T(8,128)S(1)} %get-tuple-element.6.one_ref), channel_id=1, source_target_pairs={{0,16},{16,0},{1,17},{17,1},{2,18},{18,2},{3,19},{19,3},{4,20},{20... | collective-permute-start | bytes 294920 | tf_op jit(solution)/shard_map/ppermute | solution.py:449
  38.2 4.6 %collective-permute-done.other_ref = f32[2,32,384]{2,1,0:T(8,128)S(1)} collective-permute-done((f32[2,32,384]{2,1,0:T(8,128)S(1)}, f32[2,32,384]{2,1,0:T(8,128)S(1)}, u32[]{:S(2)}, u32[]{:S(2)}) %collective-permute-start) | collective-permute-done | bytes 98336 | tf_op jit(solution)/shard_map/ppermute | solution.py:449
  42.8 0.0 copy-start
  42.8 0.0 copy-start.1
  42.8 1.4 %forward_adjoint.1 = (f32[32,128]{1,0:T(8,128)S(1)}, f32[2,32,384]{2,1,0:T(8,128)S(1)}) custom-call(bf16[8,2,400,128]{3,2,1,0:T(8,128)(2,1)S(1)} %bitcast.13, f32[2,32,384]{2,1,0:T(8,128)S(1)} %get-tuple-element.6.one_ref, f32[2,32,384]{2,1,0:T(8,128)S(1)} %collective-permute-done.other_ref, f32[32,128]{1,0:T(8,128)S(1)} %get-tuple-element.7.spectra_ref, ...), custom_call_target="tpu_custom_call" | custom-call | tf_op jit(solution)/shard_map/forward_adjoint/pallas_call | solution.py:460
  44.2 1.0 %collective-permute-start.1 = (f32[2,32,384]{2,1,0:T(8,128)S(1)}, f32[2,32,384]{2,1,0:T(8,128)S(1)}, u32[]{:S(2)}, u32[]{:S(2)}) collective-permute-start(f32[2,32,384]{2,1,0:T(8,128)S(1)} %get-tuple-element.8.one_ref), channel_id=1, source_target_pairs={{0,16},{16,0},{1,17},{17,1},{2,18},{18,2},{3,19},{19,3},{4,20},{20... | collective-permute-start | bytes 294920 | tf_op jit(solution)/shard_map/ppermute | solution.py:449
  45.2 5.5 %collective-permute-done.1.other_ref = f32[2,32,384]{2,1,0:T(8,128)S(1)} collective-permute-done((f32[2,32,384]{2,1,0:T(8,128)S(1)}, f32[2,32,384]{2,1,0:T(8,128)S(1)}, u32[]{:S(2)}, u32[]{:S(2)}) %collective-permute-start.1) | collective-permute-done | bytes 98336 | tf_op jit(solution)/shard_map/ppermute | solution.py:449
  50.7 1.1 %last_forward.1 = f32[16,4,128]{2,1,0:T(4,128)S(1)} custom-call(bf16[8,2,400,128]{3,2,1,0:T(8,128)(2,1)S(1)} %bitcast.14, f32[2,32,384]{2,1,0:T(8,128)S(1)} %get-tuple-element.8.one_ref, f32[2,32,384]{2,1,0:T(8,128)S(1)} %collective-permute-done.1.other_ref, f32[32,128]{1,0:T(8,128)S(1)} %get-tuple-element.9.residual_ref, ...), custom_call_target="tpu_custom_call" | custom-call | tf_op jit(solution)/shard_map/last_forward/pallas_call | solution.py:466
  51.9 10.1 %all_to_all.10.got_ref = f32[16,4,128]{2,1,0:T(4,128)S(1)} all-to-all(f32[16,4,128]{2,1,0:T(4,128)S(1)} %last_forward.1), channel_id=1, replica_groups=mesh['top'=2,'low'=8,'par'=2] {'low','par'}, dimensions={0} | all-to-all | bytes 65536 | tf_op jit(solution)/shard_map/all_to_all | solution.py:472
  62.0 0.0 copy-done
  62.0 0.0 copy-done.1
  62.0 1.0 %to_time.1 = (f32[2,8,256]{2,1,0:T(8,128)}, f32[2,8,256]{2,1,0:T(8,128)}) custom-call(f32[16,4,128]{2,1,0:T(4,128)S(1)} %all_to_all.10.got_ref, f32[256,256]{1,0:T(8,128)S(1)} %copy-done, f32[1,8]{1,0:T(1,128)S(1)} %bitcast.16), custom_call_target="tpu_custom_call" | custom-call | tf_op jit(solution)/shard_map/to_time/pallas_call | solution.py:473
  (4 shorter events, 0.0 us)
Async XLA Ops:
  5.0 6.4 %copy-start.2 = (s32[1,384]{1,0:T(1,128)S(1)}, s32[1,384]{1,0:T(1,128)}, u32[]{:S(2)}) copy-start(s32[1,384]{1,0:T(1,128)} %param.13) | copy-start | bytes 4612
  5.0 6.5 %copy-start.3 = (f32[1,384]{1,0:T(1,128)S(1)}, f32[1,384]{1,0:T(1,128)}, u32[]{:S(2)}) copy-start(f32[1,384]{1,0:T(1,128)} %param.12) | copy-start | bytes 4612
  5.0 30.0 %all-to-all-start = ((bf16[16,400,128]{2,1,0:T(8,128)(2,1)}), bf16[16,400,128]{2,1,0:T(8,128)(2,1)S(1)}, u32[]{:S(2)}, u32[]{:S(2)}) async-start(bf16[16,400,128]{2,1,0:T(8,128)(2,1)} %outbound.1), calls=%async_computation | async-start | bytes 3276800 | tf_op jit(solution)/shard_map/all_to_all | solution.py:442
  35.6 7.3 %collective-permute-start = (f32[2,32,384]{2,1,0:T(8,128)S(1)}, f32[2,32,384]{2,1,0:T(8,128)S(1)}, u32[]{:S(2)}, u32[]{:S(2)}) collective-permute-start(f32[2,32,384]{2,1,0:T(8,128)S(1)} %get-tuple-element.6.one_ref), channel_id=1, source_target_pairs={{0,16},{16,0},{1,17},{17,1},{2,18},{18,2},{3,19},{19,3},{4,20},{20... | collective-permute-start | bytes 294920 | tf_op jit(solution)/shard_map/ppermute | solution.py:449
  42.8 19.2 %copy-start = (f32[256,256]{1,0:T(8,128)S(1)}, f32[256,256]{1,0:T(8,128)}, u32[]{:S(2)}) copy-start(f32[256,256]{1,0:T(8,128)} %constant.5.clone.basis_ref) | copy-start | bytes 786436
  42.8 19.2 %copy-start.1 = (f32[8]{0:T(128)S(1)}, f32[8]{0:T(128)}, u32[]{:S(2)}) copy-start(f32[8]{0:T(128)} %param.11) | copy-start | bytes 100
  44.2 6.5 %collective-permute-start.1 = (f32[2,32,384]{2,1,0:T(8,128)S(1)}, f32[2,32,384]{2,1,0:T(8,128)S(1)}, u32[]{:S(2)}, u32[]{:S(2)}) collective-permute-start(f32[2,32,384]{2,1,0:T(8,128)S(1)} %get-tuple-element.8.one_ref), channel_id=1, source_target_pairs={{0,16},{16,0},{1,17},{17,1},{2,18},{18,2},{3,19},{19,3},{4,20},{20... | collective-permute-start | bytes 294920 | tf_op jit(solution)/shard_map/ppermute | solution.py:449

commit v6 on v5

--- a/solution.py
+++ b/solution.py
@@ -165,46 +165,78 @@
     return jnp.sum(square, axis=1, keepdims=True)
 
 
-def outbound_kernel(resp_ref, vectors_ref, observed_ref, noise_ref, basis_ref, out_ref, spectra_ref):
+def outbound_kernel(
+    resp_hbm, vectors_hbm, observed_hbm, noise_hbm, basis_hbm, out_hbm,
+    resp_ref, vectors_ref, observed_ref, noise_ref, basis_ref, out_ref, small_sems, in_sems, out_sems,
+):
     _, devices, each, sensors, width = resp_ref.shape
     pair, lines = 2 * sensors, 2 * each
-    wide = out_ref.shape[2]
-    tiles = width // wide
-
-    @pl.when(pl.program_id(0) == 0)
-    def _():
-        rows = vectors_ref.shape[0]
-        noise = upright(noise_ref[...])
-        records = []
-        for r in range(rows):
-            record = vectors_ref[r]
-            records += [record, observed_ref[r] - noise * record]
-        filled = rows * pair
-        records.append(jnp.zeros((wide - filled, records[0].shape[1]), jnp.float32))
-        spectra = lax.dot_general(
-            basis_ref[...],
-            jnp.concatenate(records, axis=0),
-            (((1,), (1,)), ((), ())),
-            precision=lax.Precision.HIGHEST,
-            preferred_element_type=jnp.float32,
+    tiles = width // LANES
+    steps = in_sems.shape[0]
+    some = devices // steps
+    pieces = [pl.ds(i * some, some) for i in range(steps)]
+    small = [
+        pltpu.make_async_copy(src, dst, small_sems.at[i])
+        for i, (src, dst) in enumerate(
+            [
+                (basis_hbm, basis_ref),
+                (vectors_hbm, vectors_ref),
+                (observed_hbm, observed_ref),
+                (noise_hbm, noise_ref),
+            ]
         )
-        exact = iota(spectra.shape, 1) // sensors % 2 == 1
-        high = spectra.astype(jnp.bfloat16).astype(jnp.float32)
-        rest = jnp.where(exact, spectra - high, 0.0)
-        middle = rest.astype(jnp.bfloat16).astype(jnp.float32)
-        low = (rest - middle).astype(jnp.bfloat16).astype(jnp.float32)
-        packed = high + roll(middle, filled, 1) + roll(low, 2 * filled, 1)
-        spectra_ref[...] = packed.reshape(spectra_ref.shape)
-
-    for f in range(each):
-        for j in range(tiles):
-            lanes = pl.ds(j * wide, wide)
-            part = jnp.concatenate([resp_ref[0, :, f, :, lanes], resp_ref[1, :, f, :, lanes]], axis=1)
-            out_ref[:, pl.ds((f * tiles + j) * pair, pair), :] = part
-    first = pl.multiple_of(pl.program_id(0) * devices, devices)
-    out_ref[:, pl.ds(each * tiles * pair, lines), :] = spectra_ref[pl.ds(first, devices)].astype(
-        jnp.bfloat16
+    ]
+    loads = [
+        pltpu.make_async_copy(resp_hbm.at[:, piece], resp_ref.at[:, piece], in_sems.at[i])
+        for i, piece in enumerate(pieces)
+    ]
+    body = each * tiles * pair
+    parts = [(piece, pl.ds(0, body)) for piece in pieces] + [(pl.ds(0, devices), pl.ds(body, lines))]
+    stores = [
+        pltpu.make_async_copy(out_ref.at[part], out_hbm.at[part], out_sems.at[i])
+        for i, part in enumerate(parts)
+    ]
+    for copy in loads + small:
+        copy.start()
+
+    for i, piece in enumerate(pieces):
+        loads[i].wait()
+        for f in range(each):
+            for j in range(tiles):
+                lanes = pl.ds(j * LANES, LANES)
+                both = [resp_ref[c, piece, f, :, lanes] for c in range(2)]
+                lane_rows = pl.ds((f * tiles + j) * pair, pair)
+                out_ref[piece, lane_rows, :] = jnp.concatenate(both, axis=1)
+        stores[i].start()
+
+    for copy in small:
+        copy.wait()
+    rows = vectors_ref.shape[0]
+    noise = upright(noise_ref[...])
+    records = []
+    for r in range(rows):
+        record = vectors_ref[r]
+        records += [record, observed_ref[r] - noise * record]
+    filled = rows * pair
+    records.append(jnp.zeros((LANES - filled, records[0].shape[1]), jnp.float32))
+    spectra = lax.dot_general(
+        basis_ref[...],
+        jnp.concatenate(records, axis=0),
+        (((1,), (1,)), ((), ())),
+        precision=lax.Precision.HIGHEST,
+        preferred_element_type=jnp.float32,
     )
+    exact = iota(spectra.shape, 1) // sensors % 2 == 1
+    high = spectra.astype(jnp.bfloat16).astype(jnp.float32)
+    rest = jnp.where(exact, spectra - high, 0.0)
+    middle = rest.astype(jnp.bfloat16).astype(jnp.float32)
+    low = (rest - middle).astype(jnp.bfloat16).astype(jnp.float32)
+    packed = high + roll(middle, filled, 1) + roll(low, 2 * filled, 1)
+    packed = packed.reshape(devices, lines, LANES).astype(jnp.bfloat16)
+    out_ref[:, pl.ds(body, lines), :] = packed
+    stores[-1].start()
+    for copy in stores:
+        copy.wait()
 
 
 class Share:
@@ -410,30 +442,32 @@
     axes = ("low", "par")
     basis = make_basis(length).reshape(length, 2, shares, each)
     noise = noise[None, :]
-    whole = lambda shape: pl.BlockSpec(shape, lambda i: (0,) * len(shape))
     f32 = lambda *shape: jax.ShapeDtypeStruct(shape, jnp.float32)
     room = lambda mib: pltpu.CompilerParams(vmem_limit_bytes=mib * 2**20)
 
     steps = 4 if shares % 4 == 0 else 1
-    some = shares // steps
     tall = each * width // LANES * pair + 2 * each
+    operator = operator.reshape(2, shares, each, sensors, width)
+    scratch = [
+        pltpu.VMEM(array.shape, array.dtype) for array in (operator, vectors, observed, noise)
+    ]
     message = pl.pallas_call(
         outbound_kernel,
-        grid=(steps,),
-        in_specs=[
-            pl.BlockSpec((2, some, each, sensors, width), lambda i: (0, i, 0, 0, 0)),
-            whole(vectors.shape),
-            whole(observed.shape),
-            whole(noise.shape),
-            whole((length, length)),
+        in_specs=[pl.BlockSpec(memory_space=pl.ANY)] * 5,
+        out_specs=pl.BlockSpec(memory_space=pl.ANY),
+        out_shape=jax.ShapeDtypeStruct((shares, tall, LANES), jnp.bfloat16),
+        scratch_shapes=scratch
+        + [
+            pltpu.VMEM((length, length), jnp.float32),
+            pltpu.VMEM((shares, tall, LANES), jnp.bfloat16),
+            pltpu.SemaphoreType.DMA((4,)),
+            pltpu.SemaphoreType.DMA((steps,)),
+            pltpu.SemaphoreType.DMA((steps + 1,)),
         ],
-        out_specs=pl.BlockSpec((some, tall, LANES), lambda i: (i, 0, 0)),
-        out_shape=jax.ShapeDtypeStruct((shares, tall, LANES), jnp.bfloat16),
-        scratch_shapes=[pltpu.VMEM((shares, 2 * each, LANES), jnp.float32)],
         compiler_params=room(60),
         name="outbound",
     )(
-        operator.reshape(2, shares, each, sensors, width),
+        operator,
         vectors,
         observed,
         noise,

time: 63.3 us -> 61.7 us (0.975)
  Pallas kernels: 8.44 us -> 6.89 us
    pallas_call x1, Pallas kernels: 4.36 us -> 2.8 us  [body_fast(): pl.pallas_call(outbound_kernel, in_specs=[pl.BlockSpec(memory_space=pl.AN...]
where the time goes in v6:
time: 61.7 us; the launch traced here: 61.4 us
  waiting for transfers between devices  31.8 us (52%)
  blocking collectives  12 us (19%)
  starting transfers between devices  9.93 us (16%)
  Pallas kernels  6.89 us (11%)
  between operations  0.72 us (1%)
    all_to_all x1, waiting for transfers between devices, body_fast(): lax.all_to_all(message, axes, 0, 0, tiled=True)  21.7 us
    all_to_all x1, blocking collectives, body_fast(): got = lax.all_to_all(message, axes, 0, 0, tiled=True)  10.1 us
    ppermute x2, waiting for transfers between devices, across(): return lax.ppermute(sums, 'top', [(i, (i + 1) % top) for i in range(top)])  10.1 us
    all_to_all x1, starting transfers between devices, body_fast(): lax.all_to_all(message, axes, 0, 0, tiled=True)  6.3 us
    ppermute x2, starting transfers between devices, across(): return lax.ppermute(sums, 'top', [(i, (i + 1) % top) for i in range(top)])  3.63 us
    pallas_call x1, Pallas kernels, body_fast(): pl.pallas_call(outbound_kernel, in_specs=[pl.BlockSpec(memory_space=pl.AN...  2.8 us
    all_gather x1, blocking collectives, body_fast(): grid = lax.all_gather(grid, 'par').transpose(1, 0, 2)  1.89 us
    pallas_call x1, Pallas kernels, body_fast(): pl.pallas_call(functools.partial(middle_kernel, share), out_shape=[f32(he...  1.36 us
  transfers between devices with their start and end apart: 3, of which 3 were waited for; matrix products, arithmetic and copies ran while one was open for 0% of the time, Pallas kernels for 0%

profile of v6, /device:TPU:0, one launch (start us, length us, event | category | flops | bytes accessed | tf_op | source)
XLA Modules:
  0.0 61.4 jit_solution(3762534545772616004)
XLA Ops:
  0.6 2.8 %outbound.1 = bf16[16,400,128]{2,1,0:T(8,128)(2,1)} custom-call(bf16[2,16,8,8,384]{4,3,2,1,0:T(8,128)(2,1)} %bitcast.17, f32[2,8,256]{2,1,0:T(8,128)} %vectors_hbm.1, f32[2,8,256]{2,1,0:T(8,128)} %observed_hbm.1, f32[1,8]{1,0:T(1,128)} %bitcast.15, f32[256,256]{1,0:T(8,128)} %constant.4.clone.basis_hbm), custom_call_target="tpu_custom_call" | custom-call | tf_op jit(solution)/shard_map/outbound/pallas_call | solution.py:454
  3.4 0.0 copy-start.2
  3.5 0.0 copy-start.3
  3.5 6.3 %all-to-all-start = ((bf16[16,400,128]{2,1,0:T(8,128)(2,1)}), bf16[16,400,128]{2,1,0:T(8,128)(2,1)S(1)}, u32[]{:S(2)}, u32[]{:S(2)}) async-start(bf16[16,400,128]{2,1,0:T(8,128)(2,1)} %outbound.1), calls=%async_computation | async-start | bytes 3276800 | tf_op jit(solution)/shard_map/all_to_all | solution.py:476
  9.8 0.0 copy-done.2
  9.8 0.0 copy-done.3
  9.8 1.9 %all-gather.1 = f32[2,2,384]{2,1,0:T(2,128)S(1)} all-gather(f32[1,2,384]{2,1,0:T(2,128)S(1)} %maximum_bitcast_fusion), channel_id=2, replica_groups=mesh['top'=2,'low'=8,'par'=2] {'par'}, dimensions={0}, use_global_device_ids=true | all-gather | bytes 9216 | tf_op jit(solution)/shard_map/all_gather | solution.py:479
  11.7 21.7 %all-to-all-done = bf16[16,400,128]{2,1,0:T(8,128)(2,1)S(1)} async-done(((bf16[16,400,128]{2,1,0:T(8,128)(2,1)}), bf16[16,400,128]{2,1,0:T(8,128)(2,1)S(1)}, u32[]{:S(2)}, u32[]{:S(2)}) %all-to-all-start) | async-done | bytes 1638432 | tf_op jit(solution)/shard_map/all_to_all | solution.py:476
  33.4 0.5 first_adjoint.1
  33.9 2.7 %collective-permute-start = (f32[2,32,384]{2,1,0:T(8,128)S(1)}, f32[2,32,384]{2,1,0:T(8,128)S(1)}, u32[]{:S(2)}, u32[]{:S(2)}) collective-permute-start(f32[2,32,384]{2,1,0:T(8,128)S(1)} %get-tuple-element.6.one_ref), channel_id=1, source_target_pairs={{0,16},{16,0},{1,17},{17,1},{2,18},{18,2},{3,19},{19,3},{4,20},{20... | collective-permute-start | bytes 294920 | tf_op jit(solution)/shard_map/ppermute | solution.py:483
  36.6 4.6 %collective-permute-done.other_ref = f32[2,32,384]{2,1,0:T(8,128)S(1)} collective-permute-done((f32[2,32,384]{2,1,0:T(8,128)S(1)}, f32[2,32,384]{2,1,0:T(8,128)S(1)}, u32[]{:S(2)}, u32[]{:S(2)}) %collective-permute-start) | collective-permute-done | bytes 98336 | tf_op jit(solution)/shard_map/ppermute | solution.py:483
  41.2 0.0 copy-start
  41.2 0.0 copy-start.1
  41.2 1.4 %forward_adjoint.1 = (f32[32,128]{1,0:T(8,128)S(1)}, f32[2,32,384]{2,1,0:T(8,128)S(1)}) custom-call(bf16[8,2,400,128]{3,2,1,0:T(8,128)(2,1)S(1)} %bitcast.13, f32[2,32,384]{2,1,0:T(8,128)S(1)} %get-tuple-element.6.one_ref, f32[2,32,384]{2,1,0:T(8,128)S(1)} %collective-permute-done.other_ref, f32[32,128]{1,0:T(8,128)S(1)} %get-tuple-element.7.spectra_ref, ...), custom_call_target="tpu_custom_call" | custom-call | tf_op jit(solution)/shard_map/forward_adjoint/pallas_call | solution.py:494
  42.6 1.0 %collective-permute-start.1 = (f32[2,32,384]{2,1,0:T(8,128)S(1)}, f32[2,32,384]{2,1,0:T(8,128)S(1)}, u32[]{:S(2)}, u32[]{:S(2)}) collective-permute-start(f32[2,32,384]{2,1,0:T(8,128)S(1)} %get-tuple-element.8.one_ref), channel_id=1, source_target_pairs={{0,16},{16,0},{1,17},{17,1},{2,18},{18,2},{3,19},{19,3},{4,20},{20... | collective-permute-start | bytes 294920 | tf_op jit(solution)/shard_map/ppermute | solution.py:483
  43.5 5.5 %collective-permute-done.1.other_ref = f32[2,32,384]{2,1,0:T(8,128)S(1)} collective-permute-done((f32[2,32,384]{2,1,0:T(8,128)S(1)}, f32[2,32,384]{2,1,0:T(8,128)S(1)}, u32[]{:S(2)}, u32[]{:S(2)}) %collective-permute-start.1) | collective-permute-done | bytes 98336 | tf_op jit(solution)/shard_map/ppermute | solution.py:483
  49.1 1.1 %last_forward.1 = f32[16,4,128]{2,1,0:T(4,128)S(1)} custom-call(bf16[8,2,400,128]{3,2,1,0:T(8,128)(2,1)S(1)} %bitcast.14, f32[2,32,384]{2,1,0:T(8,128)S(1)} %get-tuple-element.8.one_ref, f32[2,32,384]{2,1,0:T(8,128)S(1)} %collective-permute-done.1.other_ref, f32[32,128]{1,0:T(8,128)S(1)} %get-tuple-element.9.residual_ref, ...), custom_call_target="tpu_custom_call" | custom-call | tf_op jit(solution)/shard_map/last_forward/pallas_call | solution.py:500
  50.2 10.1 %all_to_all.10.got_ref = f32[16,4,128]{2,1,0:T(4,128)S(1)} all-to-all(f32[16,4,128]{2,1,0:T(4,128)S(1)} %last_forward.1), channel_id=1, replica_groups=mesh['top'=2,'low'=8,'par'=2] {'low','par'}, dimensions={0} | all-to-all | bytes 65536 | tf_op jit(solution)/shard_map/all_to_all | solution.py:506
  60.3 0.0 copy-done
  60.3 0.0 copy-done.1
  60.3 1.0 %to_time.1 = (f32[2,8,256]{2,1,0:T(8,128)}, f32[2,8,256]{2,1,0:T(8,128)}) custom-call(f32[16,4,128]{2,1,0:T(4,128)S(1)} %all_to_all.10.got_ref, f32[256,256]{1,0:T(8,128)S(1)} %copy-done, f32[1,8]{1,0:T(1,128)S(1)} %bitcast.16), custom_call_target="tpu_custom_call" | custom-call | tf_op jit(solution)/shard_map/to_time/pallas_call | solution.py:507
  (4 shorter events, 0.0 us)
Async XLA Ops:
  3.4 6.3 %copy-start.2 = (s32[1,384]{1,0:T(1,128)S(1)}, s32[1,384]{1,0:T(1,128)}, u32[]{:S(2)}) copy-start(s32[1,384]{1,0:T(1,128)} %param.13) | copy-start | bytes 4612
  3.5 6.3 %copy-start.3 = (f32[1,384]{1,0:T(1,128)S(1)}, f32[1,384]{1,0:T(1,128)}, u32[]{:S(2)}) copy-start(f32[1,384]{1,0:T(1,128)} %param.12) | copy-start | bytes 4612
  3.5 29.9 %all-to-all-start = ((bf16[16,400,128]{2,1,0:T(8,128)(2,1)}), bf16[16,400,128]{2,1,0:T(8,128)(2,1)S(1)}, u32[]{:S(2)}, u32[]{:S(2)}) async-start(bf16[16,400,128]{2,1,0:T(8,128)(2,1)} %outbound.1), calls=%async_computation | async-start | bytes 3276800 | tf_op jit(solution)/shard_map/all_to_all | solution.py:476
  33.9 7.3 %collective-permute-start = (f32[2,32,384]{2,1,0:T(8,128)S(1)}, f32[2,32,384]{2,1,0:T(8,128)S(1)}, u32[]{:S(2)}, u32[]{:S(2)}) collective-permute-start(f32[2,32,384]{2,1,0:T(8,128)S(1)} %get-tuple-element.6.one_ref), channel_id=1, source_target_pairs={{0,16},{16,0},{1,17},{17,1},{2,18},{18,2},{3,19},{19,3},{4,20},{20... | collective-permute-start | bytes 294920 | tf_op jit(solution)/shard_map/ppermute | solution.py:483
  41.2 19.2 %copy-start = (f32[256,256]{1,0:T(8,128)S(1)}, f32[256,256]{1,0:T(8,128)}, u32[]{:S(2)}) copy-start(f32[256,256]{1,0:T(8,128)} %constant.5.clone.basis_ref) | copy-start | bytes 786436
  41.2 19.2 %copy-start.1 = (f32[8]{0:T(128)S(1)}, f32[8]{0:T(128)}, u32[]{:S(2)}) copy-start(f32[8]{0:T(128)} %param.11) | copy-start | bytes 100
  42.6 6.5 %collective-permute-start.1 = (f32[2,32,384]{2,1,0:T(8,128)S(1)}, f32[2,32,384]{2,1,0:T(8,128)S(1)}, u32[]{:S(2)}, u32[]{:S(2)}) collective-permute-start(f32[2,32,384]{2,1,0:T(8,128)S(1)} %get-tuple-element.8.one_ref), channel_id=1, source_target_pairs={{0,16},{16,0},{1,17},{17,1},{2,18},{18,2},{3,19},{19,3},{4,20},{20... | collective-permute-start | bytes 294920 | tf_op jit(solution)/shard_map/ppermute | solution.py:483

commit v7 on v6

--- a/solution.py
+++ b/solution.py
@@ -377,28 +377,32 @@
                         out_ref[(h * per + i) * self.par + p, g : g + 1, :] = moved[i : i + 1, :]
 
 
-def first_kernel(share, got_ref, spectra_ref, sums_ref):
+def give(sums, own_ref, sent_ref):
+    for p, part in enumerate(sums):
+        own_ref[p] = part
+        sent_ref[p] = part.astype(sent_ref.dtype)
+
+
+def first_kernel(share, got_ref, spectra_ref, own_ref, sent_ref):
     share = share(got_ref)
     spectra = share.spectra()
     spectra_ref[...] = spectra
-    for p, part in enumerate(share.adjoint(spectra)):
-        sums_ref[p] = part
+    give(share.adjoint(spectra), own_ref, sent_ref)
 
 
 def summed(one_ref, other_ref):
-    return [one_ref[x] + other_ref[x] for x in range(one_ref.shape[0])]
+    return [one_ref[x] + other_ref[x].astype(jnp.float32) for x in range(one_ref.shape[0])]
 
 
 def middle_kernel(
-    share, got_ref, one_ref, other_ref, spectra_ref, coef_ref, link_ref, residual_ref, sums_ref
+    share, got_ref, one_ref, other_ref, spectra_ref, coef_ref, link_ref, residual_ref, own_ref, sent_ref
 ):
     share = share(got_ref)
     rest = roll(spectra_ref[...], -share.sensors, 1)
     field = share.smoothed(summed(one_ref, other_ref), coef_ref, link_ref)
     residual = rest - share.forward(field)
     residual_ref[...] = residual
-    for p, part in enumerate(share.adjoint(residual)):
-        sums_ref[p] = part
+    give(share.adjoint(residual), own_ref, sent_ref)
 
 
 def last_kernel(share, got_ref, one_ref, other_ref, residual_ref, coef_ref, link_ref, out_ref):
@@ -484,25 +488,25 @@
 
     share = functools.partial(Share, rows=rows, each=each, width=width)
     held, lanes = rows * 2 * each, low * pair
-    sums = f32(par, held, width)
-    spectra, one = pl.pallas_call(
+    sums = [f32(par, held, width), jax.ShapeDtypeStruct((par, held, width), jnp.bfloat16)]
+    spectra, one, sent = pl.pallas_call(
         functools.partial(first_kernel, share),
-        out_shape=[f32(held, lanes), sums],
+        out_shape=[f32(held, lanes)] + sums,
         compiler_params=room(32),
         name="first_adjoint",
     )(got)
-    residual, two = pl.pallas_call(
+    residual, two, sent_too = pl.pallas_call(
         functools.partial(middle_kernel, share),
-        out_shape=[f32(held, lanes), sums],
+        out_shape=[f32(held, lanes)] + sums,
         compiler_params=room(32),
         name="forward_adjoint",
-    )(got, one, across(one), spectra, coefs, links)
+    )(got, one, across(sent), spectra, coefs, links)
     message = pl.pallas_call(
         functools.partial(last_kernel, share),
         out_shape=f32(shares, held * pair // LANES, LANES),
         compiler_params=room(32),
         name="last_forward",
-    )(got, two, across(two), residual, coefs, links)
+    )(got, two, across(sent_too), residual, coefs, links)
     got = lax.all_to_all(message, axes, 0, 0, tiled=True)
     return pl.pallas_call(
         home_kernel,

time: 61.7 us -> 57.3 us (0.929)
  waiting for transfers between devices: 31.8 us -> 27.4 us
  starting transfers between devices: 9.93 us -> 11.2 us
  blocking collectives: 12 us -> 10.9 us
    ppermute x2, waiting for transfers between devices: 10.1 us -> 5.73 us  [across(): return lax.ppermute(sums, 'top', [(i, (i + 1) % top) for i in range(top)])]
    ppermute x2, starting transfers between devices: 3.63 us -> 4.87 us  [across(): return lax.ppermute(sums, 'top', [(i, (i + 1) % top) for i in range(top)])]
    all_to_all x1, blocking collectives: 10.1 us -> 8.98 us  [body_fast(): got = lax.all_to_all(message, axes, 0, 0, tiled=True)]
where the time goes in v7:
time: 57.3 us; the launch traced here: 57.1 us
  waiting for transfers between devices  27.4 us (48%)
  starting transfers between devices  11.2 us (20%)
  blocking collectives  10.9 us (19%)
  Pallas kernels  6.9 us (12%)
  between operations  0.72 us (1%)
    all_to_all x1, waiting for transfers between devices, body_fast(): lax.all_to_all(message, axes, 0, 0, tiled=True)  21.7 us
    all_to_all x1, blocking collectives, body_fast(): got = lax.all_to_all(message, axes, 0, 0, tiled=True)  8.98 us
    all_to_all x1, starting transfers between devices, body_fast(): lax.all_to_all(message, axes, 0, 0, tiled=True)  6.3 us
    ppermute x2, waiting for transfers between devices, across(): return lax.ppermute(sums, 'top', [(i, (i + 1) % top) for i in range(top)])  5.73 us
    ppermute x2, starting transfers between devices, across(): return lax.ppermute(sums, 'top', [(i, (i + 1) % top) for i in range(top)])  4.87 us
    pallas_call x1, Pallas kernels, body_fast(): pl.pallas_call(outbound_kernel, in_specs=[pl.BlockSpec(memory_space=pl.AN...  2.8 us
    all_gather x1, blocking collectives, body_fast(): grid = lax.all_gather(grid, 'par').transpose(1, 0, 2)  1.89 us
    pallas_call x1, Pallas kernels, body_fast(): pl.pallas_call(functools.partial(middle_kernel, share), out_shape=[f32(he...  1.37 us
  transfers between devices with their start and end apart: 3, of which 3 were waited for; matrix products, arithmetic and copies ran while one was open for 0% of the time, Pallas kernels for 0%

profile of v7, /device:TPU:0, one launch (start us, length us, event | category | flops | bytes accessed | tf_op | source)
XLA Modules:
  0.0 57.1 jit_solution(5461133455759999419)
XLA Ops:
  0.6 2.8 %outbound.1 = bf16[16,400,128]{2,1,0:T(8,128)(2,1)} custom-call(bf16[2,16,8,8,384]{4,3,2,1,0:T(8,128)(2,1)} %bitcast.17, f32[2,8,256]{2,1,0:T(8,128)} %vectors_hbm.1, f32[2,8,256]{2,1,0:T(8,128)} %observed_hbm.1, f32[1,8]{1,0:T(1,128)} %bitcast.15, f32[256,256]{1,0:T(8,128)} %constant.4.clone.basis_hbm), custom_call_target="tpu_custom_call" | custom-call | tf_op jit(solution)/shard_map/outbound/pallas_call | solution.py:458
  3.4 0.0 copy-start.2
  3.5 0.0 copy-start.3
  3.5 6.3 %all-to-all-start = ((bf16[16,400,128]{2,1,0:T(8,128)(2,1)}), bf16[16,400,128]{2,1,0:T(8,128)(2,1)S(1)}, u32[]{:S(2)}, u32[]{:S(2)}) async-start(bf16[16,400,128]{2,1,0:T(8,128)(2,1)} %outbound.1), calls=%async_computation | async-start | bytes 3276800 | tf_op jit(solution)/shard_map/all_to_all | solution.py:480
  9.8 0.0 copy-done.2
  9.8 0.0 copy-done.3
  9.8 1.9 %all-gather.1 = f32[2,2,384]{2,1,0:T(2,128)S(1)} all-gather(f32[1,2,384]{2,1,0:T(2,128)S(1)} %maximum_bitcast_fusion), channel_id=2, replica_groups=mesh['top'=2,'low'=8,'par'=2] {'par'}, dimensions={0}, use_global_device_ids=true | all-gather | bytes 9216 | tf_op jit(solution)/shard_map/all_gather | solution.py:483
  11.7 21.7 %all-to-all-done = bf16[16,400,128]{2,1,0:T(8,128)(2,1)S(1)} async-done(((bf16[16,400,128]{2,1,0:T(8,128)(2,1)}), bf16[16,400,128]{2,1,0:T(8,128)(2,1)S(1)}, u32[]{:S(2)}, u32[]{:S(2)}) %all-to-all-start) | async-done | bytes 1638432 | tf_op jit(solution)/shard_map/all_to_all | solution.py:480
  33.4 0.5 first_adjoint.1
  33.9 2.7 %collective-permute-start = (bf16[2,32,384]{2,1,0:T(8,128)(2,1)S(1)}, bf16[2,32,384]{2,1,0:T(8,128)(2,1)S(1)}, u32[]{:S(2)}, u32[]{:S(2)}) collective-permute-start(bf16[2,32,384]{2,1,0:T(8,128)(2,1)S(1)} %get-tuple-element.9), channel_id=1, source_target_pairs={{0,16},{16,0},{1,17},{17,1},{2,18},{18,2},{3,19},{19,3},{4,20},{20... | collective-permute-start | bytes 147464 | tf_op jit(solution)/shard_map/ppermute | solution.py:487
  36.6 2.8 %collective-permute-done.other_ref = bf16[2,32,384]{2,1,0:T(8,128)(2,1)S(1)} collective-permute-done((bf16[2,32,384]{2,1,0:T(8,128)(2,1)S(1)}, bf16[2,32,384]{2,1,0:T(8,128)(2,1)S(1)}, u32[]{:S(2)}, u32[]{:S(2)}) %collective-permute-start) | collective-permute-done | bytes 49184 | tf_op jit(solution)/shard_map/ppermute | solution.py:487
  39.4 0.0 copy-start
  39.4 0.0 copy-start.1
  39.4 1.4 %forward_adjoint.1 = (f32[32,128]{1,0:T(8,128)S(1)}, f32[2,32,384]{2,1,0:T(8,128)S(1)}, bf16[2,32,384]{2,1,0:T(8,128)(2,1)S(1)}) custom-call(bf16[8,2,400,128]{3,2,1,0:T(8,128)(2,1)S(1)} %bitcast.13, f32[2,32,384]{2,1,0:T(8,128)S(1)} %get-tuple-element.8.one_ref, bf16[2,32,384]{2,1,0:T(8,128)(2,1)S(1)} %collective-permute-done.other_ref, ...), custom_call_target="tpu_custom_call" | custom-call | tf_op jit(solution)/shard_map/forward_adjoint/pallas_call | solution.py:498
  40.8 2.2 %collective-permute-start.1 = (bf16[2,32,384]{2,1,0:T(8,128)(2,1)S(1)}, bf16[2,32,384]{2,1,0:T(8,128)(2,1)S(1)}, u32[]{:S(2)}, u32[]{:S(2)}) collective-permute-start(bf16[2,32,384]{2,1,0:T(8,128)(2,1)S(1)} %get-tuple-element.12), channel_id=1, source_target_pairs={{0,16},{16,0},{1,17},{17,1},{2,18},{18,2},{3,19},{19,3},{4,20},{20... | collective-permute-start | bytes 147464 | tf_op jit(solution)/shard_map/ppermute | solution.py:487
  43.0 2.9 %collective-permute-done.1.other_ref = bf16[2,32,384]{2,1,0:T(8,128)(2,1)S(1)} collective-permute-done((bf16[2,32,384]{2,1,0:T(8,128)(2,1)S(1)}, bf16[2,32,384]{2,1,0:T(8,128)(2,1)S(1)}, u32[]{:S(2)}, u32[]{:S(2)}) %collective-permute-start.1) | collective-permute-done | bytes 49184 | tf_op jit(solution)/shard_map/ppermute | solution.py:487
  45.9 1.2 %last_forward.1 = f32[16,4,128]{2,1,0:T(4,128)S(1)} custom-call(bf16[8,2,400,128]{3,2,1,0:T(8,128)(2,1)S(1)} %bitcast.14, f32[2,32,384]{2,1,0:T(8,128)S(1)} %get-tuple-element.11.one_ref, bf16[2,32,384]{2,1,0:T(8,128)(2,1)S(1)} %collective-permute-done.1.other_ref, f32[32,128]{1,0:T(8,128)S(1)} %get-tuple-element.13.residual_ref, ...), custom_call_target="tpu_custom_call" | custom-call | tf_op jit(solution)/shard_map/last_forward/pallas_call | solution.py:504
  47.1 9.0 %all_to_all.10.got_ref = f32[16,4,128]{2,1,0:T(4,128)S(1)} all-to-all(f32[16,4,128]{2,1,0:T(4,128)S(1)} %last_forward.1), channel_id=1, replica_groups=mesh['top'=2,'low'=8,'par'=2] {'low','par'}, dimensions={0} | all-to-all | bytes 65536 | tf_op jit(solution)/shard_map/all_to_all | solution.py:510
  56.0 0.0 copy-done
  56.0 0.0 copy-done.1
  56.0 1.0 %to_time.1 = (f32[2,8,256]{2,1,0:T(8,128)}, f32[2,8,256]{2,1,0:T(8,128)}) custom-call(f32[16,4,128]{2,1,0:T(4,128)S(1)} %all_to_all.10.got_ref, f32[256,256]{1,0:T(8,128)S(1)} %copy-done, f32[1,8]{1,0:T(1,128)S(1)} %bitcast.16), custom_call_target="tpu_custom_call" | custom-call | tf_op jit(solution)/shard_map/to_time/pallas_call | solution.py:511
  (4 shorter events, 0.0 us)
Async XLA Ops:
  3.4 6.3 %copy-start.2 = (s32[1,384]{1,0:T(1,128)S(1)}, s32[1,384]{1,0:T(1,128)}, u32[]{:S(2)}) copy-start(s32[1,384]{1,0:T(1,128)} %param.13) | copy-start | bytes 4612
  3.5 6.3 %copy-start.3 = (f32[1,384]{1,0:T(1,128)S(1)}, f32[1,384]{1,0:T(1,128)}, u32[]{:S(2)}) copy-start(f32[1,384]{1,0:T(1,128)} %param.12) | copy-start | bytes 4612
  3.5 29.9 %all-to-all-start = ((bf16[16,400,128]{2,1,0:T(8,128)(2,1)}), bf16[16,400,128]{2,1,0:T(8,128)(2,1)S(1)}, u32[]{:S(2)}, u32[]{:S(2)}) async-start(bf16[16,400,128]{2,1,0:T(8,128)(2,1)} %outbound.1), calls=%async_computation | async-start | bytes 3276800 | tf_op jit(solution)/shard_map/all_to_all | solution.py:480
  33.9 5.5 %collective-permute-start = (bf16[2,32,384]{2,1,0:T(8,128)(2,1)S(1)}, bf16[2,32,384]{2,1,0:T(8,128)(2,1)S(1)}, u32[]{:S(2)}, u32[]{:S(2)}) collective-permute-start(bf16[2,32,384]{2,1,0:T(8,128)(2,1)S(1)} %get-tuple-element.9), channel_id=1, source_target_pairs={{0,16},{16,0},{1,17},{17,1},{2,18},{18,2},{3,19},{19,3},{4,20},{20... | collective-permute-start | bytes 147464 | tf_op jit(solution)/shard_map/ppermute | solution.py:487
  39.4 16.6 %copy-start = (f32[256,256]{1,0:T(8,128)S(1)}, f32[256,256]{1,0:T(8,128)}, u32[]{:S(2)}) copy-start(f32[256,256]{1,0:T(8,128)} %constant.5.clone.basis_ref) | copy-start | bytes 786436
  39.4 16.6 %copy-start.1 = (f32[8]{0:T(128)S(1)}, f32[8]{0:T(128)}, u32[]{:S(2)}) copy-start(f32[8]{0:T(128)} %param.11) | copy-start | bytes 100
  40.8 5.1 %collective-permute-start.1 = (bf16[2,32,384]{2,1,0:T(8,128)(2,1)S(1)}, bf16[2,32,384]{2,1,0:T(8,128)(2,1)S(1)}, u32[]{:S(2)}, u32[]{:S(2)}) collective-permute-start(bf16[2,32,384]{2,1,0:T(8,128)(2,1)S(1)} %get-tuple-element.12), channel_id=1, source_target_pairs={{0,16},{16,0},{1,17},{17,1},{2,18},{18,2},{3,19},{19,3},{4,20},{20... | collective-permute-start | bytes 147464 | tf_op jit(solution)/shard_map/ppermute | solution.py:487

commit v8 on v7

--- a/solution.py
+++ b/solution.py
@@ -165,9 +165,21 @@
     return jnp.sum(square, axis=1, keepdims=True)
 
 
+def split(x):
+    high = x.astype(jnp.bfloat16).astype(jnp.float32)
+    middle = (x - high).astype(jnp.bfloat16).astype(jnp.float32)
+    return high, middle, (x - high - middle).astype(jnp.bfloat16).astype(jnp.float32)
+
+
+def tail_lanes(rows, pair):
+    start = 3 * rows * pair
+    return start, LANES // (LANES - start), LANES - start
+
+
 def outbound_kernel(
-    resp_hbm, vectors_hbm, observed_hbm, noise_hbm, basis_hbm, out_hbm,
-    resp_ref, vectors_ref, observed_ref, noise_ref, basis_ref, out_ref, small_sems, in_sems, out_sems,
+    resp_hbm, vectors_hbm, observed_hbm, noise_hbm, coef_hbm, link_hbm, basis_hbm, out_hbm,
+    resp_ref, vectors_ref, observed_ref, noise_ref, coef_ref, link_ref, basis_ref, out_ref,
+    small_sems, in_sems, out_sems,
 ):
     _, devices, each, sensors, width = resp_ref.shape
     pair, lines = 2 * sensors, 2 * each
@@ -183,6 +195,8 @@
                 (vectors_hbm, vectors_ref),
                 (observed_hbm, observed_ref),
                 (noise_hbm, noise_ref),
+                (coef_hbm, coef_ref),
+                (link_hbm, link_ref),
             ]
         )
     ]
@@ -227,12 +241,24 @@
         preferred_element_type=jnp.float32,
     )
     exact = iota(spectra.shape, 1) // sensors % 2 == 1
-    high = spectra.astype(jnp.bfloat16).astype(jnp.float32)
-    rest = jnp.where(exact, spectra - high, 0.0)
-    middle = rest.astype(jnp.bfloat16).astype(jnp.float32)
-    low = (rest - middle).astype(jnp.bfloat16).astype(jnp.float32)
-    packed = high + roll(middle, filled, 1) + roll(low, 2 * filled, 1)
-    packed = packed.reshape(devices, lines, LANES).astype(jnp.bfloat16)
+    high, middle, low = split(spectra)
+    packed = high + roll(jnp.where(exact, middle, 0.0), filled, 1)
+    packed = packed + roll(jnp.where(exact, low, 0.0), 2 * filled, 1)
+
+    start, chunks, free = tail_lanes(rows, pair)
+    turn = lax.axis_index("low") % tiles
+    coefs, links = (
+        sum(
+            jnp.where(turn == j, ref[:, j * LANES : (j + 1) * LANES].astype(jnp.float32), 0.0)
+            for j in range(tiles)
+        )
+        for ref in (coef_ref, link_ref)
+    )
+    grid = jnp.concatenate([*split(coefs), links], axis=0)
+    grid = jnp.concatenate([roll(grid, start - i * free, 1) for i in range(chunks)], axis=0)
+    grid = jnp.where(iota(grid.shape, 1) >= start, grid, 0.0)
+    packed = packed.reshape(devices, lines, LANES) + grid[None]
+    packed = packed.astype(jnp.bfloat16)
     out_ref[:, pl.ds(body, lines), :] = packed
     stores[-1].start()
     for copy in stores:
@@ -297,6 +323,27 @@
                 found[r][h] = jnp.where(at == place, moved, found[r][h])
         return jnp.concatenate([jnp.concatenate(line, axis=1) for line in found], axis=0)
 
+    def grid(self):
+        start, chunks, free = tail_lanes(self.rows, self.pair)
+        kinds = self.lines // chunks
+        chunk = iota((kinds, LANES), 1) // free
+        coefs, links = [], []
+        for p in range(self.par):
+            tail = self.got[
+                pl.ds(0, self.tiles), p, pl.ds(self.got.shape[2] - self.lines, self.lines), :
+            ].astype(jnp.float32)
+            found = []
+            for j in range(self.tiles):
+                line = jnp.zeros((kinds, LANES), jnp.float32)
+                for i in range(chunks):
+                    part = roll(tail[j, i * kinds : (i + 1) * kinds], i * free - start, 1)
+                    line = jnp.where(chunk == i, part, line)
+                found.append(line)
+            found = jnp.concatenate(found, axis=1)
+            coefs.append(found[0:1] + found[1:2] + found[2:3])
+            links.append(found[3:4])
+        return jnp.concatenate(coefs, axis=0), jnp.concatenate(links, axis=0)
+
     def adjoint(self, record):
         crossed = self.swapped(record)
         crossed = roll(jnp.where(self.real_row, crossed, -crossed), self.sensors, 1)
@@ -323,7 +370,7 @@
             masks = []
             for shift in range(-REACH, REACH + 1):
                 inside = (column + shift >= 0) & (column + shift < self.width)
-                mask = jnp.where((offset == shift) & inside, 1.0, 0.0)
+                mask = jnp.where((offset == float(shift)) & inside, 1.0, 0.0)
                 masks.append(jnp.broadcast_to(mask, shape))
             links.append(masks)
         after_first = jnp.broadcast_to(jnp.where(column > 0, 1.0, 0.0), shape)
@@ -383,8 +430,9 @@
         sent_ref[p] = part.astype(sent_ref.dtype)
 
 
-def first_kernel(share, got_ref, spectra_ref, own_ref, sent_ref):
+def first_kernel(share, got_ref, spectra_ref, coef_ref, link_ref, own_ref, sent_ref):
     share = share(got_ref)
+    coef_ref[...], link_ref[...] = share.grid()
     spectra = share.spectra()
     spectra_ref[...] = spectra
     give(share.adjoint(spectra), own_ref, sent_ref)
@@ -446,6 +494,7 @@
     axes = ("low", "par")
     basis = make_basis(length).reshape(length, 2, shares, each)
     noise = noise[None, :]
+    small = (vectors, observed, noise, coefficient, offsets)
     f32 = lambda *shape: jax.ShapeDtypeStruct(shape, jnp.float32)
     room = lambda mib: pltpu.CompilerParams(vmem_limit_bytes=mib * 2**20)
 
@@ -453,18 +502,18 @@
     tall = each * width // LANES * pair + 2 * each
     operator = operator.reshape(2, shares, each, sensors, width)
     scratch = [
-        pltpu.VMEM(array.shape, array.dtype) for array in (operator, vectors, observed, noise)
+        pltpu.VMEM(array.shape, array.dtype) for array in (operator, *small)
     ]
     message = pl.pallas_call(
         outbound_kernel,
-        in_specs=[pl.BlockSpec(memory_space=pl.ANY)] * 5,
+        in_specs=[pl.BlockSpec(memory_space=pl.ANY)] * 7,
         out_specs=pl.BlockSpec(memory_space=pl.ANY),
         out_shape=jax.ShapeDtypeStruct((shares, tall, LANES), jnp.bfloat16),
         scratch_shapes=scratch
         + [
             pltpu.VMEM((length, length), jnp.float32),
             pltpu.VMEM((shares, tall, LANES), jnp.bfloat16),
-            pltpu.SemaphoreType.DMA((4,)),
+            pltpu.SemaphoreType.DMA((6,)),
             pltpu.SemaphoreType.DMA((steps,)),
             pltpu.SemaphoreType.DMA((steps + 1,)),
         ],
@@ -472,26 +521,21 @@
         name="outbound",
     )(
         operator,
-        vectors,
-        observed,
-        noise,
+        *small,
         jnp.asarray(basis.transpose(2, 3, 1, 0).reshape(length, length)),
     )
     got = lax.all_to_all(message, axes, 0, 0, tiled=True).reshape(low, par, tall, LANES)
 
-    grid = jnp.concatenate([coefficient, offsets.astype(jnp.float32)])
-    grid = lax.all_gather(grid, "par").transpose(1, 0, 2)
-    coefs, links = grid[0], grid[1].astype(jnp.int32)
-
     def across(sums):
         return lax.ppermute(sums, "top", [(i, (i + 1) % top) for i in range(top)])
 
     share = functools.partial(Share, rows=rows, each=each, width=width)
     held, lanes = rows * 2 * each, low * pair
     sums = [f32(par, held, width), jax.ShapeDtypeStruct((par, held, width), jnp.bfloat16)]
-    spectra, one, sent = pl.pallas_call(
+    grid = [f32(par, width)] * 2
+    spectra, coefs, links, one, sent = pl.pallas_call(
         functools.partial(first_kernel, share),
-        out_shape=[f32(held, lanes)] + sums,
+        out_shape=[f32(held, lanes)] + grid + sums,
         compiler_params=room(32),
         name="first_adjoint",
     )(got)
@@ -526,8 +570,11 @@
     each, pair = half // (low * par), 2 * (sensors // sen)
     return (
         pair == 16
+        and 3 * rows * pair < LANES
         and each % 8 == 0
-        and 3 * rows * pair <= LANES
+        and LANES % (LANES - 3 * rows * pair) == 0
+        and 4 * tail_lanes(rows, pair)[1] == 2 * each
+        and low * LANES >= coefficient.shape[1]
         and low * pair % LANES == 0
         and coefficient.shape[1] % LANES == 0
     )

time: 57.3 us -> 55.5 us (0.969)
  blocking collectives: 10.9 us -> 37 us
  waiting for transfers between devices: 27.4 us -> 5.83 us
  starting transfers between devices: 11.2 us -> 4.8 us
    all_to_all x0 -> x1, blocking collectives: none -> 28.8 us  [body_fast(): lax.all_to_all(message, axes, 0, 0, tiled=True)]
    all_to_all x1 -> x0, waiting for transfers between devices: 21.7 us -> none  [body_fast(): lax.all_to_all(message, axes, 0, 0, tiled=True)]
    all_to_all x1 -> x0, starting transfers between devices: 6.3 us -> none  [body_fast(): lax.all_to_all(message, axes, 0, 0, tiled=True)]
    all_gather x1 -> x0, blocking collectives: 1.89 us -> none  [body_fast(): grid = lax.all_gather(grid, 'par').transpose(1, 0, 2)]
    all_to_all x1, blocking collectives: 8.98 us -> 8.22 us  [body_fast(): got = lax.all_to_all(message, axes, 0, 0, tiled=True)]
  transfers between devices with their start and end apart: 3 -> 2, of which waited for: 3 -> 2; matrix products, arithmetic and copies ran while one was open for 0% -> 0% of each run, Pallas kernels for 0% -> 0%
where the time goes in v8:
time: 55.5 us; the launch traced here: 55.3 us
  blocking collectives  37 us (67%)
  Pallas kernels  6.97 us (13%)
  waiting for transfers between devices  5.83 us (11%)
  starting transfers between devices  4.8 us (9%)
  between operations  0.66 us (1%)
    all_to_all x1, blocking collectives, body_fast(): lax.all_to_all(message, axes, 0, 0, tiled=True)  28.8 us
    all_to_all x1, blocking collectives, body_fast(): got = lax.all_to_all(message, axes, 0, 0, tiled=True)  8.22 us
    ppermute x2, waiting for transfers between devices, across(): return lax.ppermute(sums, 'top', [(i, (i + 1) % top) for i in range(top)])  5.83 us
    ppermute x2, starting transfers between devices, across(): return lax.ppermute(sums, 'top', [(i, (i + 1) % top) for i in range(top)])  4.8 us
    pallas_call x1, Pallas kernels, body_fast(): pl.pallas_call(outbound_kernel, in_specs=[pl.BlockSpec(memory_space=pl.AN...  2.87 us
    pallas_call x1, Pallas kernels, body_fast(): pl.pallas_call(functools.partial(middle_kernel, share), out_shape=[f32(he...  1.37 us
    pallas_call x1, Pallas kernels, body_fast(): pl.pallas_call(functools.partial(last_kernel, share), out_shape=f32(share...  1.15 us
  transfers between devices with their start and end apart: 2, of which 2 were waited for; matrix products, arithmetic and copies ran while one was open for 0% of the time, Pallas kernels for 0%

profile of v8, /device:TPU:0, one launch (start us, length us, event | category | flops | bytes accessed | tf_op | source)
XLA Modules:
  0.0 55.3 jit_solution(1535850970334574572)
XLA Ops:
  0.6 2.9 %outbound.1 = bf16[16,400,128]{2,1,0:T(8,128)(2,1)} custom-call(bf16[2,16,8,8,384]{4,3,2,1,0:T(8,128)(2,1)} %bitcast.8, f32[2,8,256]{2,1,0:T(8,128)} %vectors_hbm.1, f32[2,8,256]{2,1,0:T(8,128)} %observed_hbm.1, f32[1,8]{1,0:T(1,128)} %bitcast.6, f32[1,384]{1,0:T(1,128)} %coef_hbm.1, s32[1,384]{1,0:T(1,128)} %link_hbm.1, f32[256,256]{1,0:T(8,128)} %constant.4.clone.basis_hbm), custom_call_target="tpu_custom_call" | custom-call | tf_op jit(solution)/shard_map/outbound/pallas_call | solution.py:507
  3.5 28.8 %all_to_all.10 = bf16[16,400,128]{2,1,0:T(8,128)(2,1)S(1)} all-to-all(bf16[16,400,128]{2,1,0:T(8,128)(2,1)} %outbound.1), channel_id=1, replica_groups=mesh['top'=2,'low'=8,'par'=2] {'low','par'}, dimensions={0} | all-to-all | bytes 3276800 | tf_op jit(solution)/shard_map/all_to_all | solution.py:527
  32.3 0.5 first_adjoint.1
  32.8 2.7 %collective-permute-start = (bf16[2,32,384]{2,1,0:T(8,128)(2,1)S(1)}, bf16[2,32,384]{2,1,0:T(8,128)(2,1)S(1)}, u32[]{:S(2)}, u32[]{:S(2)}) collective-permute-start(bf16[2,32,384]{2,1,0:T(8,128)(2,1)S(1)} %get-tuple-element.11), channel_id=1, source_target_pairs={{0,16},{16,0},{1,17},{17,1},{2,18},{18,2},{3,19},{19,3},{4,20},{20... | collective-permute-start | bytes 147464 | tf_op jit(solution)/shard_map/ppermute | solution.py:530
  35.5 2.9 %collective-permute-done.other_ref = bf16[2,32,384]{2,1,0:T(8,128)(2,1)S(1)} collective-permute-done((bf16[2,32,384]{2,1,0:T(8,128)(2,1)S(1)}, bf16[2,32,384]{2,1,0:T(8,128)(2,1)S(1)}, u32[]{:S(2)}, u32[]{:S(2)}) %collective-permute-start) | collective-permute-done | bytes 49184 | tf_op jit(solution)/shard_map/ppermute | solution.py:530
  38.4 0.0 copy-start
  38.4 0.0 copy-start.1
  38.4 1.4 %forward_adjoint.1 = (f32[32,128]{1,0:T(8,128)S(1)}, f32[2,32,384]{2,1,0:T(8,128)S(1)}, bf16[2,32,384]{2,1,0:T(8,128)(2,1)S(1)}) custom-call(bf16[8,2,400,128]{3,2,1,0:T(8,128)(2,1)S(1)} %bitcast.4, f32[2,32,384]{2,1,0:T(8,128)S(1)} %get-tuple-element.10.one_ref, bf16[2,32,384]{2,1,0:T(8,128)(2,1)S(1)} %collective-permute-done.other_ref, ...), custom_call_target="tpu_custom_call" | custom-call | tf_op jit(solution)/shard_map/forward_adjoint/pallas_call | solution.py:542
  39.8 2.1 %collective-permute-start.1 = (bf16[2,32,384]{2,1,0:T(8,128)(2,1)S(1)}, bf16[2,32,384]{2,1,0:T(8,128)(2,1)S(1)}, u32[]{:S(2)}, u32[]{:S(2)}) collective-permute-start(bf16[2,32,384]{2,1,0:T(8,128)(2,1)S(1)} %get-tuple-element.16), channel_id=1, source_target_pairs={{0,16},{16,0},{1,17},{17,1},{2,18},{18,2},{3,19},{19,3},{4,20},{20... | collective-permute-start | bytes 147464 | tf_op jit(solution)/shard_map/ppermute | solution.py:530
  41.9 2.9 %collective-permute-done.1.other_ref = bf16[2,32,384]{2,1,0:T(8,128)(2,1)S(1)} collective-permute-done((bf16[2,32,384]{2,1,0:T(8,128)(2,1)S(1)}, bf16[2,32,384]{2,1,0:T(8,128)(2,1)S(1)}, u32[]{:S(2)}, u32[]{:S(2)}) %collective-permute-start.1) | collective-permute-done | bytes 49184 | tf_op jit(solution)/shard_map/ppermute | solution.py:530
  44.8 1.1 %last_forward.1 = f32[16,4,128]{2,1,0:T(4,128)S(1)} custom-call(bf16[8,2,400,128]{3,2,1,0:T(8,128)(2,1)S(1)} %bitcast.5, f32[2,32,384]{2,1,0:T(8,128)S(1)} %get-tuple-element.15.one_ref, bf16[2,32,384]{2,1,0:T(8,128)(2,1)S(1)} %collective-permute-done.1.other_ref, f32[32,128]{1,0:T(8,128)S(1)} %get-tuple-element.17.residual_ref, ...), custom_call_target="tpu_custom_call" | custom-call | tf_op jit(solution)/shard_map/last_forward/pallas_call | solution.py:548
  46.0 8.2 %all_to_all.11.got_ref = f32[16,4,128]{2,1,0:T(4,128)S(1)} all-to-all(f32[16,4,128]{2,1,0:T(4,128)S(1)} %last_forward.1), channel_id=1, replica_groups=mesh['top'=2,'low'=8,'par'=2] {'low','par'}, dimensions={0} | all-to-all | bytes 65536 | tf_op jit(solution)/shard_map/all_to_all | solution.py:554
  54.2 0.0 copy-done
  54.2 0.0 copy-done.1
  54.2 1.0 %to_time.1 = (f32[2,8,256]{2,1,0:T(8,128)}, f32[2,8,256]{2,1,0:T(8,128)}) custom-call(f32[16,4,128]{2,1,0:T(4,128)S(1)} %all_to_all.11.got_ref, f32[256,256]{1,0:T(8,128)S(1)} %copy-done, f32[1,8]{1,0:T(1,128)S(1)} %bitcast.7), custom_call_target="tpu_custom_call" | custom-call | tf_op jit(solution)/shard_map/to_time/pallas_call | solution.py:555
Async XLA Ops:
  32.8 5.6 %collective-permute-start = (bf16[2,32,384]{2,1,0:T(8,128)(2,1)S(1)}, bf16[2,32,384]{2,1,0:T(8,128)(2,1)S(1)}, u32[]{:S(2)}, u32[]{:S(2)}) collective-permute-start(bf16[2,32,384]{2,1,0:T(8,128)(2,1)S(1)} %get-tuple-element.11), channel_id=1, source_target_pairs={{0,16},{16,0},{1,17},{17,1},{2,18},{18,2},{3,19},{19,3},{4,20},{20... | collective-permute-start | bytes 147464 | tf_op jit(solution)/shard_map/ppermute | solution.py:530
  38.4 15.8 %copy-start = (f32[256,256]{1,0:T(8,128)S(1)}, f32[256,256]{1,0:T(8,128)}, u32[]{:S(2)}) copy-start(f32[256,256]{1,0:T(8,128)} %constant.5.clone.basis_ref) | copy-start | bytes 786436
  38.4 15.8 %copy-start.1 = (f32[8]{0:T(128)S(1)}, f32[8]{0:T(128)}, u32[]{:S(2)}) copy-start(f32[8]{0:T(128)} %param.11) | copy-start | bytes 100
  39.8 5.1 %collective-permute-start.1 = (bf16[2,32,384]{2,1,0:T(8,128)(2,1)S(1)}, bf16[2,32,384]{2,1,0:T(8,128)(2,1)S(1)}, u32[]{:S(2)}, u32[]{:S(2)}) collective-permute-start(bf16[2,32,384]{2,1,0:T(8,128)(2,1)S(1)} %get-tuple-element.16), channel_id=1, source_target_pairs={{0,16},{16,0},{1,17},{17,1},{2,18},{18,2},{3,19},{19,3},{4,20},{20... | collective-permute-start | bytes 147464 | tf_op jit(solution)/shard_map/ppermute | solution.py:530

commit v9 on v8

--- a/solution.py
+++ b/solution.py
@@ -177,9 +177,9 @@
 
 
 def outbound_kernel(
-    resp_hbm, vectors_hbm, observed_hbm, noise_hbm, coef_hbm, link_hbm, basis_hbm, out_hbm,
-    resp_ref, vectors_ref, observed_ref, noise_ref, coef_ref, link_ref, basis_ref, out_ref,
-    small_sems, in_sems, out_sems,
+    resp_hbm, vectors_hbm, observed_hbm, noise_hbm, coef_hbm, link_hbm, basis_hbm, out_ref,
+    resp_ref, vectors_ref, observed_ref, noise_ref, coef_ref, link_ref, basis_ref,
+    small_sems, in_sems,
 ):
     _, devices, each, sensors, width = resp_ref.shape
     pair, lines = 2 * sensors, 2 * each
@@ -205,23 +205,8 @@
         for i, piece in enumerate(pieces)
     ]
     body = each * tiles * pair
-    parts = [(piece, pl.ds(0, body)) for piece in pieces] + [(pl.ds(0, devices), pl.ds(body, lines))]
-    stores = [
-        pltpu.make_async_copy(out_ref.at[part], out_hbm.at[part], out_sems.at[i])
-        for i, part in enumerate(parts)
-    ]
-    for copy in loads + small:
+    for copy in small + loads:
         copy.start()
-
-    for i, piece in enumerate(pieces):
-        loads[i].wait()
-        for f in range(each):
-            for j in range(tiles):
-                lanes = pl.ds(j * LANES, LANES)
-                both = [resp_ref[c, piece, f, :, lanes] for c in range(2)]
-                lane_rows = pl.ds((f * tiles + j) * pair, pair)
-                out_ref[piece, lane_rows, :] = jnp.concatenate(both, axis=1)
-        stores[i].start()
 
     for copy in small:
         copy.wait()
@@ -260,9 +245,15 @@
     packed = packed.reshape(devices, lines, LANES) + grid[None]
     packed = packed.astype(jnp.bfloat16)
     out_ref[:, pl.ds(body, lines), :] = packed
-    stores[-1].start()
-    for copy in stores:
-        copy.wait()
+
+    for i, piece in enumerate(pieces):
+        loads[i].wait()
+        for f in range(each):
+            for j in range(tiles):
+                lanes = pl.ds(j * LANES, LANES)
+                both = [resp_ref[c, piece, f, :, lanes] for c in range(2)]
+                lane_rows = pl.ds((f * tiles + j) * pair, pair)
+                out_ref[piece, lane_rows, :] = jnp.concatenate(both, axis=1)
 
 
 class Share:
@@ -498,7 +489,7 @@
     f32 = lambda *shape: jax.ShapeDtypeStruct(shape, jnp.float32)
     room = lambda mib: pltpu.CompilerParams(vmem_limit_bytes=mib * 2**20)
 
-    steps = 4 if shares % 4 == 0 else 1
+    steps = 2 if shares % 2 == 0 else 1
     tall = each * width // LANES * pair + 2 * each
     operator = operator.reshape(2, shares, each, sensors, width)
     scratch = [
@@ -507,22 +498,25 @@
     message = pl.pallas_call(
         outbound_kernel,
         in_specs=[pl.BlockSpec(memory_space=pl.ANY)] * 7,
-        out_specs=pl.BlockSpec(memory_space=pl.ANY),
+        out_specs=pl.BlockSpec(memory_space=pltpu.VMEM),
         out_shape=jax.ShapeDtypeStruct((shares, tall, LANES), jnp.bfloat16),
         scratch_shapes=scratch
         + [
             pltpu.VMEM((length, length), jnp.float32),
-            pltpu.VMEM((shares, tall, LANES), jnp.bfloat16),
             pltpu.SemaphoreType.DMA((6,)),
             pltpu.SemaphoreType.DMA((steps,)),
-            pltpu.SemaphoreType.DMA((steps + 1,)),
         ],
-        compiler_params=room(60),
+        compiler_params=room(50),
         name="outbound",
     )(
-        operator,
-        *small,
-        jnp.asarray(basis.transpose(2, 3, 1, 0).reshape(length, length)),
+        *(
+            pltpu.with_memory_space_constraint(x, pltpu.HBM)
+            for x in (
+                operator,
+                *small,
+                jnp.asarray(basis.transpose(2, 3, 1, 0).reshape(length, length)),
+            )
+        )
     )
     got = lax.all_to_all(message, axes, 0, 0, tiled=True).reshape(low, par, tall, LANES)
 

time: 55.5 us -> 54.4 us (0.980)
  Pallas kernels: 6.97 us -> 6.06 us
    pallas_call x1, Pallas kernels: 2.87 us -> 1.93 us  [body_fast(): pl.pallas_call(outbound_kernel, in_specs=[pl.BlockSpec(memory_space=pl.AN...]
where the time goes in v9:
time: 54.4 us; the launch traced here: 54.2 us
  blocking collectives  36.8 us (68%)
  Pallas kernels  6.06 us (11%)
  waiting for transfers between devices  5.85 us (11%)
  starting transfers between devices  4.78 us (9%)
  between operations  0.66 us (1%)
    all_to_all x1, blocking collectives, body_fast(): lax.all_to_all(message, axes, 0, 0, tiled=True)  28.6 us
    all_to_all x1, blocking collectives, body_fast(): got = lax.all_to_all(message, axes, 0, 0, tiled=True)  8.22 us
    ppermute x2, waiting for transfers between devices, across(): return lax.ppermute(sums, 'top', [(i, (i + 1) % top) for i in range(top)])  5.85 us
    ppermute x2, starting transfers between devices, across(): return lax.ppermute(sums, 'top', [(i, (i + 1) % top) for i in range(top)])  4.78 us
    pallas_call x1, Pallas kernels, body_fast(): pl.pallas_call(outbound_kernel, in_specs=[pl.BlockSpec(memory_space=pl.AN...  1.93 us
    pallas_call x1, Pallas kernels, body_fast(): pl.pallas_call(functools.partial(middle_kernel, share), out_shape=[f32(he...  1.38 us
    pallas_call x1, Pallas kernels, body_fast(): pl.pallas_call(functools.partial(last_kernel, share), out_shape=f32(share...  1.16 us
  transfers between devices with their start and end apart: 2, of which 2 were waited for; matrix products, arithmetic and copies ran while one was open for 0% of the time, Pallas kernels for 0%

profile of v9, /device:TPU:0, one launch (start us, length us, event | category | flops | bytes accessed | tf_op | source)
XLA Modules:
  0.0 54.2 jit_solution(877996065231180744)
XLA Ops:
  0.6 1.9 %outbound.1 = bf16[16,400,128]{2,1,0:T(8,128)(2,1)S(1)} custom-call(bf16[2,16,8,8,384]{4,3,2,1,0:T(8,128)(2,1)} %bitcast.8, f32[2,8,256]{2,1,0:T(8,128)} %vectors_hbm.1, f32[2,8,256]{2,1,0:T(8,128)} %observed_hbm.1, f32[1,8]{1,0:T(1,128)} %bitcast.6, f32[1,384]{1,0:T(1,128)} %coef_hbm.1, s32[1,384]{1,0:T(1,128)} %link_hbm.1, f32[256,256]{1,0:T(8,128)} %constant.4.clone.basis_hbm), custom_call_target="tpu_custom_call" | custom-call | tf_op jit(solution)/shard_map/outbound/pallas_call | solution.py:498
  2.6 28.6 %all_to_all.10 = bf16[16,400,128]{2,1,0:T(8,128)(2,1)S(1)} all-to-all(bf16[16,400,128]{2,1,0:T(8,128)(2,1)S(1)} %outbound.1), channel_id=1, replica_groups=mesh['top'=2,'low'=8,'par'=2] {'low','par'}, dimensions={0} | all-to-all | bytes 3276800 | tf_op jit(solution)/shard_map/all_to_all | solution.py:521
  31.1 0.5 %first_adjoint.1 = (f32[32,128]{1,0:T(8,128)S(1)}, f32[2,384]{1,0:T(2,128)S(1)}, f32[2,384]{1,0:T(2,128)S(1)}, f32[2,32,384]{2,1,0:T(8,128)S(1)}, bf16[2,32,384]{2,1,0:T(8,128)(2,1)S(1)}) custom-call(bf16[8,2,400,128]{3,2,1,0:T(8,128)(2,1)S(1)} %bitcast.3), custom_call_target="tpu_custom_call" | custom-call | tf_op jit(solution)/shard_map/first_adjoint/pallas_call | solution.py:530
  31.7 2.7 %collective-permute-start = (bf16[2,32,384]{2,1,0:T(8,128)(2,1)S(1)}, bf16[2,32,384]{2,1,0:T(8,128)(2,1)S(1)}, u32[]{:S(2)}, u32[]{:S(2)}) collective-permute-start(bf16[2,32,384]{2,1,0:T(8,128)(2,1)S(1)} %get-tuple-element.11), channel_id=1, source_target_pairs={{0,16},{16,0},{1,17},{17,1},{2,18},{18,2},{3,19},{19,3},{4,20},{20... | collective-permute-start | bytes 147464 | tf_op jit(solution)/shard_map/ppermute | solution.py:524
  34.3 2.9 %collective-permute-done.other_ref = bf16[2,32,384]{2,1,0:T(8,128)(2,1)S(1)} collective-permute-done((bf16[2,32,384]{2,1,0:T(8,128)(2,1)S(1)}, bf16[2,32,384]{2,1,0:T(8,128)(2,1)S(1)}, u32[]{:S(2)}, u32[]{:S(2)}) %collective-permute-start) | collective-permute-done | bytes 49184 | tf_op jit(solution)/shard_map/ppermute | solution.py:524
  37.3 0.0 copy-start
  37.3 0.0 copy-start.1
  37.3 1.4 %forward_adjoint.1 = (f32[32,128]{1,0:T(8,128)S(1)}, f32[2,32,384]{2,1,0:T(8,128)S(1)}, bf16[2,32,384]{2,1,0:T(8,128)(2,1)S(1)}) custom-call(bf16[8,2,400,128]{3,2,1,0:T(8,128)(2,1)S(1)} %bitcast.4, f32[2,32,384]{2,1,0:T(8,128)S(1)} %get-tuple-element.10.one_ref, bf16[2,32,384]{2,1,0:T(8,128)(2,1)S(1)} %collective-permute-done.other_ref, ...), custom_call_target="tpu_custom_call" | custom-call | tf_op jit(solution)/shard_map/forward_adjoint/pallas_call | solution.py:536
  38.7 2.1 %collective-permute-start.1 = (bf16[2,32,384]{2,1,0:T(8,128)(2,1)S(1)}, bf16[2,32,384]{2,1,0:T(8,128)(2,1)S(1)}, u32[]{:S(2)}, u32[]{:S(2)}) collective-permute-start(bf16[2,32,384]{2,1,0:T(8,128)(2,1)S(1)} %get-tuple-element.16), channel_id=1, source_target_pairs={{0,16},{16,0},{1,17},{17,1},{2,18},{18,2},{3,19},{19,3},{4,20},{20... | collective-permute-start | bytes 147464 | tf_op jit(solution)/shard_map/ppermute | solution.py:524
  40.8 2.9 %collective-permute-done.1.other_ref = bf16[2,32,384]{2,1,0:T(8,128)(2,1)S(1)} collective-permute-done((bf16[2,32,384]{2,1,0:T(8,128)(2,1)S(1)}, bf16[2,32,384]{2,1,0:T(8,128)(2,1)S(1)}, u32[]{:S(2)}, u32[]{:S(2)}) %collective-permute-start.1) | collective-permute-done | bytes 49184 | tf_op jit(solution)/shard_map/ppermute | solution.py:524
  43.7 1.2 %last_forward.1 = f32[16,4,128]{2,1,0:T(4,128)S(1)} custom-call(bf16[8,2,400,128]{3,2,1,0:T(8,128)(2,1)S(1)} %bitcast.5, f32[2,32,384]{2,1,0:T(8,128)S(1)} %get-tuple-element.15.one_ref, bf16[2,32,384]{2,1,0:T(8,128)(2,1)S(1)} %collective-permute-done.1.other_ref, f32[32,128]{1,0:T(8,128)S(1)} %get-tuple-element.17.residual_ref, ...), custom_call_target="tpu_custom_call" | custom-call | tf_op jit(solution)/shard_map/last_forward/pallas_call | solution.py:542
  44.9 8.2 %all_to_all.11.got_ref = f32[16,4,128]{2,1,0:T(4,128)S(1)} all-to-all(f32[16,4,128]{2,1,0:T(4,128)S(1)} %last_forward.1), channel_id=1, replica_groups=mesh['top'=2,'low'=8,'par'=2] {'low','par'}, dimensions={0} | all-to-all | bytes 65536 | tf_op jit(solution)/shard_map/all_to_all | solution.py:548
  53.1 0.0 copy-done
  53.1 0.0 copy-done.1
  53.1 1.0 %to_time.1 = (f32[2,8,256]{2,1,0:T(8,128)}, f32[2,8,256]{2,1,0:T(8,128)}) custom-call(f32[16,4,128]{2,1,0:T(4,128)S(1)} %all_to_all.11.got_ref, f32[256,256]{1,0:T(8,128)S(1)} %copy-done, f32[1,8]{1,0:T(1,128)S(1)} %bitcast.7), custom_call_target="tpu_custom_call" | custom-call | tf_op jit(solution)/shard_map/to_time/pallas_call | solution.py:549
Async XLA Ops:
  31.7 5.6 %collective-permute-start = (bf16[2,32,384]{2,1,0:T(8,128)(2,1)S(1)}, bf16[2,32,384]{2,1,0:T(8,128)(2,1)S(1)}, u32[]{:S(2)}, u32[]{:S(2)}) collective-permute-start(bf16[2,32,384]{2,1,0:T(8,128)(2,1)S(1)} %get-tuple-element.11), channel_id=1, source_target_pairs={{0,16},{16,0},{1,17},{17,1},{2,18},{18,2},{3,19},{19,3},{4,20},{20... | collective-permute-start | bytes 147464 | tf_op jit(solution)/shard_map/ppermute | solution.py:524
  37.3 15.8 %copy-start = (f32[256,256]{1,0:T(8,128)S(1)}, f32[256,256]{1,0:T(8,128)}, u32[]{:S(2)}) copy-start(f32[256,256]{1,0:T(8,128)} %constant.5.clone.basis_ref) | copy-start | bytes 786436
  37.3 15.8 %copy-start.1 = (f32[8]{0:T(128)S(1)}, f32[8]{0:T(128)}, u32[]{:S(2)}) copy-start(f32[8]{0:T(128)} %param.11) | copy-start | bytes 100
  38.7 5.1 %collective-permute-start.1 = (bf16[2,32,384]{2,1,0:T(8,128)(2,1)S(1)}, bf16[2,32,384]{2,1,0:T(8,128)(2,1)S(1)}, u32[]{:S(2)}, u32[]{:S(2)}) collective-permute-start(bf16[2,32,384]{2,1,0:T(8,128)(2,1)S(1)} %get-tuple-element.16), channel_id=1, source_target_pairs={{0,16},{16,0},{1,17},{17,1},{2,18},{18,2},{3,19},{19,3},{4,20},{20... | collective-permute-start | bytes 147464 | tf_op jit(solution)/shard_map/ppermute | solution.py:524

commit v10 on v9

--- a/solution.py
+++ b/solution.py
@@ -266,18 +266,19 @@
         self.pair = (got_ref.shape[2] - self.lines) // (each * self.tiles)
         self.sensors = self.pair // 2
         self.lanes = self.low * self.pair
-        self.held = rows * self.lines
+        self.joint = joint_of(each, self.lanes)
+        self.groups = each // self.joint
+        self.held = rows * 2 * self.joint
         shape = (self.held, self.lanes)
         row = iota(shape, 0)
         self.real_row = row % 2 == 0
         self.real_lane = iota(shape, 1) // self.sensors % 2 == 0
-        self.freq = row // 2 % each
-        self.joint = max(1, min(each, DEPTH // self.lanes))
+        self.place = row // 2 % self.joint
 
     def swapped(self, x):
         return jnp.where(self.real_row, roll(x, -1, 0), roll(x, 1, 0))
 
-    def block(self, first, p):
+    def block(self, group, p):
         return jnp.concatenate(
             [
                 jnp.concatenate(
@@ -289,7 +290,7 @@
                     ],
                     axis=1,
                 )
-                for f in range(first, first + self.joint)
+                for f in range(group * self.joint, (group + 1) * self.joint)
             ],
             axis=0,
         )
@@ -312,7 +313,12 @@
             for r in range(self.rows):
                 moved = roll(packed, (place - r) * self.pair, 1)
                 found[r][h] = jnp.where(at == place, moved, found[r][h])
-        return jnp.concatenate([jnp.concatenate(line, axis=1) for line in found], axis=0)
+        found = [jnp.concatenate(line, axis=1) for line in found]
+        few = 2 * self.joint
+        return [
+            jnp.concatenate([line[g * few : (g + 1) * few] for line in found], axis=0)
+            for g in range(self.groups)
+        ]
 
     def grid(self):
         start, chunks, free = tail_lanes(self.rows, self.pair)
@@ -335,37 +341,35 @@
             links.append(found[3:4])
         return jnp.concatenate(coefs, axis=0), jnp.concatenate(links, axis=0)
 
-    def adjoint(self, record):
+    def adjoint(self, group, record):
         crossed = self.swapped(record)
         crossed = roll(jnp.where(self.real_row, crossed, -crossed), self.sensors, 1)
         left = jnp.where(self.real_lane, record, crossed)
-        sums = [jnp.zeros((self.held, self.width), jnp.float32) for _ in range(self.par)]
-        for first in range(0, self.each, self.joint):
-            part = [
-                jnp.where(self.freq == f, left, 0.0) for f in range(first, first + self.joint)
-            ]
-            part = jnp.concatenate(part, axis=1).astype(jnp.bfloat16)
-            for p in range(self.par):
-                sums[p] += jnp.dot(
-                    part, self.block(first, p), preferred_element_type=jnp.float32
-                )
-        return sums
-
-    def smoothed(self, field, coef_ref, link_ref):
+        left = [jnp.where(self.place == i, left, 0.0) for i in range(self.joint)]
+        left = jnp.concatenate(left, axis=1).astype(jnp.bfloat16)
+        return [
+            jnp.dot(left, self.block(group, p), preferred_element_type=jnp.float32)
+            for p in range(self.par)
+        ]
+
+    def masks(self, coef_ref, link_ref):
         shape = (self.held, self.width)
         column = iota((1, self.width), 1)
+        wide = lambda mask: jnp.broadcast_to(jnp.where(mask, 1.0, 0.0), shape)
         coefs, links = [], []
         for x in range(self.par):
             coefs.append(jnp.broadcast_to(coef_ref[x : x + 1, :], shape))
             offset = link_ref[x : x + 1, :]
-            masks = []
-            for shift in range(-REACH, REACH + 1):
-                inside = (column + shift >= 0) & (column + shift < self.width)
-                mask = jnp.where((offset == float(shift)) & inside, 1.0, 0.0)
-                masks.append(jnp.broadcast_to(mask, shape))
-            links.append(masks)
-        after_first = jnp.broadcast_to(jnp.where(column > 0, 1.0, 0.0), shape)
-        before_last = jnp.broadcast_to(jnp.where(column < self.width - 1, 1.0, 0.0), shape)
+            links.append(
+                [
+                    wide((offset == float(k)) & (column + k >= 0) & (column + k < self.width))
+                    for k in range(-REACH, REACH + 1)
+                ]
+            )
+        return coefs, links, wide(column > 0), wide(column < self.width - 1)
+
+    def smoothed(self, field, masks):
+        coefs, links, after_first, before_last = masks
         for _ in range(SWEEPS):
             after = []
             for x, u in enumerate(field):
@@ -373,7 +377,7 @@
                 if x > 0:
                     around += field[x - 1]
                 if x < self.par - 1:
-                    linked = jnp.zeros(shape, jnp.float32)
+                    linked = jnp.zeros(u.shape, jnp.float32)
                     for mask, shift in zip(links[x], range(-REACH, REACH + 1)):
                         linked += mask * roll(field[x + 1], -shift, 1)
                     around += linked
@@ -381,73 +385,86 @@
             field = after
         return field
 
-    def forward(self, field):
-        prior = [u.astype(jnp.bfloat16) for u in field]
-        out = jnp.zeros((self.held, self.lanes), jnp.float32)
-        for first in range(0, self.each, self.joint):
-            part = jnp.zeros((self.held, self.joint * self.lanes), jnp.float32)
-            for p in range(self.par):
-                part += lax.dot_general(
-                    prior[p],
-                    self.block(first, p),
-                    (((1,), (1,)), ((), ())),
-                    preferred_element_type=jnp.float32,
-                )
-            for i in range(self.joint):
-                own = part[:, i * self.lanes : (i + 1) * self.lanes]
-                out = jnp.where(self.freq == first + i, own, out)
+    def forward(self, group, field):
+        part = jnp.zeros((self.held, self.joint * self.lanes), jnp.float32)
+        for p in range(self.par):
+            part += lax.dot_general(
+                field[p].astype(jnp.bfloat16),
+                self.block(group, p),
+                (((1,), (1,)), ((), ())),
+                preferred_element_type=jnp.float32,
+            )
+        out = part[:, : self.lanes]
+        for i in range(1, self.joint):
+            out = jnp.where(self.place == i, part[:, i * self.lanes : (i + 1) * self.lanes], out)
         crossed = self.swapped(roll(out, -self.sensors, 1))
         return out + jnp.where(self.real_row, -crossed, crossed)
 
-    def messages(self, residual, applied, out_ref):
+    def message(self, group, residual, applied, out_ref):
         both = jnp.where(self.real_lane, residual, roll(applied, self.sensors, 1))
-        per = LANES // self.pair
-        to, group = iota((per, LANES), 0), iota((per, LANES), 1) // self.pair
-        for g in range(self.held // per):
-            for h in range(self.lanes // LANES):
-                tile = both[g * per : (g + 1) * per, h * LANES : (h + 1) * LANES]
-                moved = tile
-                for turn in range(1, per):
-                    turned = roll(roll(tile, -turn, 0), turn * self.pair, 1)
-                    moved = jnp.where((group - to + per) % per == turn, turned, moved)
-                for i in range(per):
-                    for p in range(self.par):
-                        out_ref[(h * per + i) * self.par + p, g : g + 1, :] = moved[i : i + 1, :]
-
-
-def give(sums, own_ref, sent_ref):
-    for p, part in enumerate(sums):
-        own_ref[p] = part
-        sent_ref[p] = part.astype(sent_ref.dtype)
+        per = self.held
+        to, lane_group = iota((per, LANES), 0), iota((per, LANES), 1) // self.pair
+        for h in range(self.lanes // LANES):
+            tile = both[:, h * LANES : (h + 1) * LANES]
+            moved = tile
+            for turn in range(1, per):
+                turned = roll(roll(tile, -turn, 0), turn * self.pair, 1)
+                moved = jnp.where((lane_group - to + per) % per == turn, turned, moved)
+            for i in range(per):
+                for p in range(self.par):
+                    place = (h * per + i) * self.par + p
+                    out_ref[place, group : group + 1, :] = moved[i : i + 1, :]
+
+    def rows_of(self, group):
+        return pl.ds(group * self.held, self.held)
+
+    def give(self, sums, own_ref, sent_ref):
+        for p in range(self.par):
+            part = jnp.concatenate([line[p] for line in sums], axis=0)
+            own_ref[p] = part
+            sent_ref[p] = part.astype(sent_ref.dtype)
+
+    def summed(self, own_ref, other_ref):
+        whole = [own_ref[p] + other_ref[p].astype(jnp.float32) for p in range(self.par)]
+        return [
+            [part[g * self.held : (g + 1) * self.held] for part in whole]
+            for g in range(self.groups)
+        ]
+
+
+def joint_of(each, lanes):
+    return max(1, min(each, DEPTH // lanes))
 
 
 def first_kernel(share, got_ref, spectra_ref, coef_ref, link_ref, own_ref, sent_ref):
     share = share(got_ref)
     coef_ref[...], link_ref[...] = share.grid()
-    spectra = share.spectra()
-    spectra_ref[...] = spectra
-    give(share.adjoint(spectra), own_ref, sent_ref)
-
-
-def summed(one_ref, other_ref):
-    return [one_ref[x] + other_ref[x].astype(jnp.float32) for x in range(one_ref.shape[0])]
+    sums = []
+    for g, spectra in enumerate(share.spectra()):
+        spectra_ref[share.rows_of(g), :] = spectra
+        sums.append(share.adjoint(g, spectra))
+    share.give(sums, own_ref, sent_ref)
 
 
 def middle_kernel(
     share, got_ref, one_ref, other_ref, spectra_ref, coef_ref, link_ref, residual_ref, own_ref, sent_ref
 ):
     share = share(got_ref)
-    rest = roll(spectra_ref[...], -share.sensors, 1)
-    field = share.smoothed(summed(one_ref, other_ref), coef_ref, link_ref)
-    residual = rest - share.forward(field)
-    residual_ref[...] = residual
-    give(share.adjoint(residual), own_ref, sent_ref)
+    masks = share.masks(coef_ref, link_ref)
+    residuals = []
+    for g, field in enumerate(share.summed(one_ref, other_ref)):
+        rest = roll(spectra_ref[share.rows_of(g), :], -share.sensors, 1)
+        residuals.append(rest - share.forward(g, share.smoothed(field, masks)))
+        residual_ref[share.rows_of(g), :] = residuals[g]
+    share.give([share.adjoint(g, x) for g, x in enumerate(residuals)], own_ref, sent_ref)
 
 
 def last_kernel(share, got_ref, one_ref, other_ref, residual_ref, coef_ref, link_ref, out_ref):
     share = share(got_ref)
-    field = share.smoothed(summed(one_ref, other_ref), coef_ref, link_ref)
-    share.messages(residual_ref[...], share.forward(field), out_ref)
+    masks = share.masks(coef_ref, link_ref)
+    for g, field in enumerate(share.summed(one_ref, other_ref)):
+        applied = share.forward(g, share.smoothed(field, masks))
+        share.message(g, residual_ref[share.rows_of(g), :], applied, out_ref)
 
 
 def home_kernel(got_ref, basis_ref, noise_ref, residual_ref, applied_ref):
@@ -455,16 +472,14 @@
     rows = residual_ref.shape[0]
     pair = 2 * sensors
     noise = upright(noise_ref[...])
-    groups = got_ref.shape[1] // rows
-    lines = []
-    for r in range(rows):
-        parts = []
-        for g in range(groups):
-            turned = got_ref[:, r * groups + g, :].T
-            parts += [turned[i : i + pair, :] for i in range(0, LANES, pair)]
-        lines.append(jnp.concatenate(parts, axis=1))
+    lines = [[] for _ in range(rows)]
+    for g in range(got_ref.shape[1]):
+        turned = got_ref[:, g, :].T
+        for r in range(rows):
+            first, last = r * LANES // rows, (r + 1) * LANES // rows
+            lines[r] += [turned[i : i + pair, :] for i in range(first, last, pair)]
     back = jnp.dot(
-        jnp.concatenate(lines, axis=0),
+        jnp.concatenate([jnp.concatenate(line, axis=1) for line in lines], axis=0),
         basis_ref[...],
         precision=lax.Precision.HIGHEST,
         preferred_element_type=jnp.float32,
@@ -541,7 +556,7 @@
     )(got, one, across(sent), spectra, coefs, links)
     message = pl.pallas_call(
         functools.partial(last_kernel, share),
-        out_shape=f32(shares, held * pair // LANES, LANES),
+        out_shape=f32(shares, each // joint_of(each, lanes), LANES),
         compiler_params=room(32),
         name="last_forward",
     )(got, two, across(sent_too), residual, coefs, links)
@@ -563,12 +578,13 @@
         return False
     each, pair = half // (low * par), 2 * (sensors // sen)
     return (
-        pair == 16
+        2 * rows * joint_of(each, low * pair) * pair == LANES
         and 3 * rows * pair < LANES
-        and each % 8 == 0
+        and each % joint_of(each, low * pair) == 0
         and LANES % (LANES - 3 * rows * pair) == 0
         and 4 * tail_lanes(rows, pair)[1] == 2 * each
         and low * LANES >= coefficient.shape[1]
+        and pair == 16
         and low * pair % LANES == 0
         and coefficient.shape[1] % LANES == 0
     )

time: 54.4 us -> 54.2 us (level)
  no operation moved by 1% of the time
where the time goes in v10:
time: 54.2 us; the launch traced here: 54 us
  blocking collectives  36.8 us (68%)
  Pallas kernels  5.93 us (11%)
  waiting for transfers between devices  5.85 us (11%)
  starting transfers between devices  4.73 us (9%)
  between operations  0.65 us (1%)
    all_to_all x1, blocking collectives, body_fast(): lax.all_to_all(message, axes, 0, 0, tiled=True)  28.6 us
    all_to_all x1, blocking collectives, body_fast(): got = lax.all_to_all(message, axes, 0, 0, tiled=True)  8.22 us
    ppermute x2, waiting for transfers between devices, across(): return lax.ppermute(sums, 'top', [(i, (i + 1) % top) for i in range(top)])  5.85 us
    ppermute x2, starting transfers between devices, across(): return lax.ppermute(sums, 'top', [(i, (i + 1) % top) for i in range(top)])  4.73 us
    pallas_call x1, Pallas kernels, body_fast(): pl.pallas_call(outbound_kernel, in_specs=[pl.BlockSpec(memory_space=pl.AN...  1.93 us
    pallas_call x1, Pallas kernels, body_fast(): pl.pallas_call(functools.partial(middle_kernel, share), out_shape=[f32(he...  1.3 us
    pallas_call x1, Pallas kernels, body_fast(): pl.pallas_call(functools.partial(last_kernel, share), out_shape=f32(share...  1.11 us
  transfers between devices with their start and end apart: 2, of which 2 were waited for; matrix products, arithmetic and copies ran while one was open for 0% of the time, Pallas kernels for 0%

profile of v10, /device:TPU:0, one launch (start us, length us, event | category | flops | bytes accessed | tf_op | source)
XLA Modules:
  0.0 54.0 jit_solution(14411930721009145158)
XLA Ops:
  0.6 1.9 %outbound.1 = bf16[16,400,128]{2,1,0:T(8,128)(2,1)S(1)} custom-call(bf16[2,16,8,8,384]{4,3,2,1,0:T(8,128)(2,1)} %bitcast.8, f32[2,8,256]{2,1,0:T(8,128)} %vectors_hbm.1, f32[2,8,256]{2,1,0:T(8,128)} %observed_hbm.1, f32[1,8]{1,0:T(1,128)} %bitcast.6, f32[1,384]{1,0:T(1,128)} %coef_hbm.1, s32[1,384]{1,0:T(1,128)} %link_hbm.1, f32[256,256]{1,0:T(8,128)} %constant.4.clone.basis_hbm), custom_call_target="tpu_custom_call" | custom-call | tf_op jit(solution)/shard_map/outbound/pallas_call | solution.py:513
  2.6 28.6 %all_to_all.10 = bf16[16,400,128]{2,1,0:T(8,128)(2,1)S(1)} all-to-all(bf16[16,400,128]{2,1,0:T(8,128)(2,1)S(1)} %outbound.1), channel_id=1, replica_groups=mesh['top'=2,'low'=8,'par'=2] {'low','par'}, dimensions={0} | all-to-all | bytes 3276800 | tf_op jit(solution)/shard_map/all_to_all | solution.py:536
  31.1 0.6 %first_adjoint.1 = (f32[32,128]{1,0:T(8,128)S(1)}, f32[2,384]{1,0:T(2,128)S(1)}, f32[2,384]{1,0:T(2,128)S(1)}, f32[2,32,384]{2,1,0:T(8,128)S(1)}, bf16[2,32,384]{2,1,0:T(8,128)(2,1)S(1)}) custom-call(bf16[8,2,400,128]{3,2,1,0:T(8,128)(2,1)S(1)} %bitcast.3), custom_call_target="tpu_custom_call" | custom-call | tf_op jit(solution)/shard_map/first_adjoint/pallas_call | solution.py:545
  31.7 2.6 %collective-permute-start = (bf16[2,32,384]{2,1,0:T(8,128)(2,1)S(1)}, bf16[2,32,384]{2,1,0:T(8,128)(2,1)S(1)}, u32[]{:S(2)}, u32[]{:S(2)}) collective-permute-start(bf16[2,32,384]{2,1,0:T(8,128)(2,1)S(1)} %get-tuple-element.11), channel_id=1, source_target_pairs={{0,16},{16,0},{1,17},{17,1},{2,18},{18,2},{3,19},{19,3},{4,20},{20... | collective-permute-start | bytes 147464 | tf_op jit(solution)/shard_map/ppermute | solution.py:539
  34.4 2.9 %collective-permute-done.other_ref = bf16[2,32,384]{2,1,0:T(8,128)(2,1)S(1)} collective-permute-done((bf16[2,32,384]{2,1,0:T(8,128)(2,1)S(1)}, bf16[2,32,384]{2,1,0:T(8,128)(2,1)S(1)}, u32[]{:S(2)}, u32[]{:S(2)}) %collective-permute-start) | collective-permute-done | bytes 49184 | tf_op jit(solution)/shard_map/ppermute | solution.py:539
  37.3 0.0 copy-start
  37.3 0.0 copy-start.1
  37.3 1.3 %forward_adjoint.1 = (f32[32,128]{1,0:T(8,128)S(1)}, f32[2,32,384]{2,1,0:T(8,128)S(1)}, bf16[2,32,384]{2,1,0:T(8,128)(2,1)S(1)}) custom-call(bf16[8,2,400,128]{3,2,1,0:T(8,128)(2,1)S(1)} %bitcast.4, f32[2,32,384]{2,1,0:T(8,128)S(1)} %get-tuple-element.10.one_ref, bf16[2,32,384]{2,1,0:T(8,128)(2,1)S(1)} %collective-permute-done.other_ref, ...), custom_call_target="tpu_custom_call" | custom-call | tf_op jit(solution)/shard_map/forward_adjoint/pallas_call | solution.py:551
  38.6 2.1 %collective-permute-start.1 = (bf16[2,32,384]{2,1,0:T(8,128)(2,1)S(1)}, bf16[2,32,384]{2,1,0:T(8,128)(2,1)S(1)}, u32[]{:S(2)}, u32[]{:S(2)}) collective-permute-start(bf16[2,32,384]{2,1,0:T(8,128)(2,1)S(1)} %get-tuple-element.16), channel_id=1, source_target_pairs={{0,16},{16,0},{1,17},{17,1},{2,18},{18,2},{3,19},{19,3},{4,20},{20... | collective-permute-start | bytes 147464 | tf_op jit(solution)/shard_map/ppermute | solution.py:539
  40.7 2.9 %collective-permute-done.1.other_ref = bf16[2,32,384]{2,1,0:T(8,128)(2,1)S(1)} collective-permute-done((bf16[2,32,384]{2,1,0:T(8,128)(2,1)S(1)}, bf16[2,32,384]{2,1,0:T(8,128)(2,1)S(1)}, u32[]{:S(2)}, u32[]{:S(2)}) %collective-permute-start.1) | collective-permute-done | bytes 49184 | tf_op jit(solution)/shard_map/ppermute | solution.py:539
  43.6 1.1 %last_forward.1 = f32[16,4,128]{2,1,0:T(4,128)S(1)} custom-call(bf16[8,2,400,128]{3,2,1,0:T(8,128)(2,1)S(1)} %bitcast.5, f32[2,32,384]{2,1,0:T(8,128)S(1)} %get-tuple-element.15.one_ref, bf16[2,32,384]{2,1,0:T(8,128)(2,1)S(1)} %collective-permute-done.1.other_ref, f32[32,128]{1,0:T(8,128)S(1)} %get-tuple-element.17.residual_ref, ...), custom_call_target="tpu_custom_call" | custom-call | tf_op jit(solution)/shard_map/last_forward/pallas_call | solution.py:557
  44.7 8.2 %all_to_all.11.got_ref = f32[16,4,128]{2,1,0:T(4,128)S(1)} all-to-all(f32[16,4,128]{2,1,0:T(4,128)S(1)} %last_forward.1), channel_id=1, replica_groups=mesh['top'=2,'low'=8,'par'=2] {'low','par'}, dimensions={0} | all-to-all | bytes 65536 | tf_op jit(solution)/shard_map/all_to_all | solution.py:563
  52.9 0.0 copy-done
  52.9 0.0 copy-done.1
  52.9 1.0 %to_time.1 = (f32[2,8,256]{2,1,0:T(8,128)}, f32[2,8,256]{2,1,0:T(8,128)}) custom-call(f32[16,4,128]{2,1,0:T(4,128)S(1)} %all_to_all.11.got_ref, f32[256,256]{1,0:T(8,128)S(1)} %copy-done, f32[1,8]{1,0:T(1,128)S(1)} %bitcast.7), custom_call_target="tpu_custom_call" | custom-call | tf_op jit(solution)/shard_map/to_time/pallas_call | solution.py:564
Async XLA Ops:
  31.7 5.5 %collective-permute-start = (bf16[2,32,384]{2,1,0:T(8,128)(2,1)S(1)}, bf16[2,32,384]{2,1,0:T(8,128)(2,1)S(1)}, u32[]{:S(2)}, u32[]{:S(2)}) collective-permute-start(bf16[2,32,384]{2,1,0:T(8,128)(2,1)S(1)} %get-tuple-element.11), channel_id=1, source_target_pairs={{0,16},{16,0},{1,17},{17,1},{2,18},{18,2},{3,19},{19,3},{4,20},{20... | collective-permute-start | bytes 147464 | tf_op jit(solution)/shard_map/ppermute | solution.py:539
  37.3 15.7 %copy-start = (f32[256,256]{1,0:T(8,128)S(1)}, f32[256,256]{1,0:T(8,128)}, u32[]{:S(2)}) copy-start(f32[256,256]{1,0:T(8,128)} %constant.5.clone.basis_ref) | copy-start | bytes 786436
  37.3 15.7 %copy-start.1 = (f32[8]{0:T(128)S(1)}, f32[8]{0:T(128)}, u32[]{:S(2)}) copy-start(f32[8]{0:T(128)} %param.11) | copy-start | bytes 100
  38.6 5.0 %collective-permute-start.1 = (bf16[2,32,384]{2,1,0:T(8,128)(2,1)S(1)}, bf16[2,32,384]{2,1,0:T(8,128)(2,1)S(1)}, u32[]{:S(2)}, u32[]{:S(2)}) collective-permute-start(bf16[2,32,384]{2,1,0:T(8,128)(2,1)S(1)} %get-tuple-element.16), channel_id=1, source_target_pairs={{0,16},{16,0},{1,17},{17,1},{2,18},{18,2},{3,19},{19,3},{4,20},{20... | collective-permute-start | bytes 147464 | tf_op jit(solution)/shard_map/ppermute | solution.py:539

commit v11 on v10

--- a/solution.py
+++ b/solution.py
@@ -418,11 +418,11 @@
     def rows_of(self, group):
         return pl.ds(group * self.held, self.held)
 
-    def give(self, sums, own_ref, sent_ref):
+    def give(self, sums, *refs):
         for p in range(self.par):
             part = jnp.concatenate([line[p] for line in sums], axis=0)
-            own_ref[p] = part
-            sent_ref[p] = part.astype(sent_ref.dtype)
+            for ref in refs:
+                ref[p] = part.astype(ref.dtype)
 
     def summed(self, own_ref, other_ref):
         whole = [own_ref[p] + other_ref[p].astype(jnp.float32) for p in range(self.par)]
@@ -436,14 +436,14 @@
     return max(1, min(each, DEPTH // lanes))
 
 
-def first_kernel(share, got_ref, spectra_ref, coef_ref, link_ref, own_ref, sent_ref):
+def first_kernel(share, got_ref, spectra_ref, coef_ref, link_ref, own_ref):
     share = share(got_ref)
     coef_ref[...], link_ref[...] = share.grid()
     sums = []
     for g, spectra in enumerate(share.spectra()):
         spectra_ref[share.rows_of(g), :] = spectra
         sums.append(share.adjoint(g, spectra))
-    share.give(sums, own_ref, sent_ref)
+    share.give(sums, own_ref)
 
 
 def middle_kernel(
@@ -540,26 +540,27 @@
 
     share = functools.partial(Share, rows=rows, each=each, width=width)
     held, lanes = rows * 2 * each, low * pair
-    sums = [f32(par, held, width), jax.ShapeDtypeStruct((par, held, width), jnp.bfloat16)]
+    sums = f32(par, held, width)
+    rounded = jax.ShapeDtypeStruct(sums.shape, jnp.bfloat16)
     grid = [f32(par, width)] * 2
-    spectra, coefs, links, one, sent = pl.pallas_call(
+    spectra, coefs, links, one = pl.pallas_call(
         functools.partial(first_kernel, share),
-        out_shape=[f32(held, lanes)] + grid + sums,
+        out_shape=[f32(held, lanes)] + grid + [sums],
         compiler_params=room(32),
         name="first_adjoint",
     )(got)
-    residual, two, sent_too = pl.pallas_call(
+    residual, two, sent = pl.pallas_call(
         functools.partial(middle_kernel, share),
-        out_shape=[f32(held, lanes)] + sums,
+        out_shape=[f32(held, lanes), sums, rounded],
         compiler_params=room(32),
         name="forward_adjoint",
-    )(got, one, across(sent), spectra, coefs, links)
+    )(got, one, across(one), spectra, coefs, links)
     message = pl.pallas_call(
         functools.partial(last_kernel, share),
         out_shape=f32(shares, each // joint_of(each, lanes), LANES),
         compiler_params=room(32),
         name="last_forward",
-    )(got, two, across(sent_too), residual, coefs, links)
+    )(got, two, across(sent), residual, coefs, links)
     got = lax.all_to_all(message, axes, 0, 0, tiled=True)
     return pl.pallas_call(
         home_kernel,

time: 54.2 us -> 56.6 us (1.044)
  waiting for transfers between devices: 5.85 us -> 9.7 us
  starting transfers between devices: 4.73 us -> 3.29 us
    ppermute x2, waiting for transfers between devices: 5.85 us -> 9.7 us  [across(): return lax.ppermute(sums, 'top', [(i, (i + 1) % top) for i in range(top)])]
    ppermute x2, starting transfers between devices: 4.73 us -> 3.29 us  [across(): return lax.ppermute(sums, 'top', [(i, (i + 1) % top) for i in range(top)])]
where the time goes in v11:
time: 56.6 us; the launch traced here: 56.4 us
  blocking collectives  36.8 us (65%)
  waiting for transfers between devices  9.7 us (17%)
  Pallas kernels  5.93 us (10%)
  starting transfers between devices  3.29 us (6%)
  between operations  0.65 us (1%)
    all_to_all x1, blocking collectives, body_fast(): lax.all_to_all(message, axes, 0, 0, tiled=True)  28.6 us
    ppermute x2, waiting for transfers between devices, across(): return lax.ppermute(sums, 'top', [(i, (i + 1) % top) for i in range(top)])  9.7 us
    all_to_all x1, blocking collectives, body_fast(): got = lax.all_to_all(message, axes, 0, 0, tiled=True)  8.22 us
    ppermute x2, starting transfers between devices, across(): return lax.ppermute(sums, 'top', [(i, (i + 1) % top) for i in range(top)])  3.29 us
    pallas_call x1, Pallas kernels, body_fast(): pl.pallas_call(outbound_kernel, in_specs=[pl.BlockSpec(memory_space=pl.AN...  1.93 us
    pallas_call x1, Pallas kernels, body_fast(): pl.pallas_call(functools.partial(middle_kernel, share), out_shape=[f32(he...  1.3 us
  transfers between devices with their start and end apart: 2, of which 2 were waited for; matrix products, arithmetic and copies ran while one was open for 0% of the time, Pallas kernels for 0%

profile of v11, /device:TPU:0, one launch (start us, length us, event | category | flops | bytes accessed | tf_op | source)
XLA Modules:
  0.0 56.4 jit_solution(6800817915927481765)
XLA Ops:
  0.6 1.9 %outbound.1 = bf16[16,400,128]{2,1,0:T(8,128)(2,1)S(1)} custom-call(bf16[2,16,8,8,384]{4,3,2,1,0:T(8,128)(2,1)} %bitcast.8, f32[2,8,256]{2,1,0:T(8,128)} %vectors_hbm.1, f32[2,8,256]{2,1,0:T(8,128)} %observed_hbm.1, f32[1,8]{1,0:T(1,128)} %bitcast.6, f32[1,384]{1,0:T(1,128)} %coef_hbm.1, s32[1,384]{1,0:T(1,128)} %link_hbm.1, f32[256,256]{1,0:T(8,128)} %constant.4.clone.basis_hbm), custom_call_target="tpu_custom_call" | custom-call | tf_op jit(solution)/shard_map/outbound/pallas_call | solution.py:513
  2.6 28.6 %all_to_all.10 = bf16[16,400,128]{2,1,0:T(8,128)(2,1)S(1)} all-to-all(bf16[16,400,128]{2,1,0:T(8,128)(2,1)S(1)} %outbound.1), channel_id=1, replica_groups=mesh['top'=2,'low'=8,'par'=2] {'low','par'}, dimensions={0} | all-to-all | bytes 3276800 | tf_op jit(solution)/shard_map/all_to_all | solution.py:536
  31.1 0.6 %first_adjoint.1 = (f32[32,128]{1,0:T(8,128)S(1)}, f32[2,384]{1,0:T(2,128)S(1)}, f32[2,384]{1,0:T(2,128)S(1)}, f32[2,32,384]{2,1,0:T(8,128)S(1)}) custom-call(bf16[8,2,400,128]{3,2,1,0:T(8,128)(2,1)S(1)} %bitcast.3), custom_call_target="tpu_custom_call" | custom-call | tf_op jit(solution)/shard_map/first_adjoint/pallas_call | solution.py:546
  31.7 2.6 %collective-permute-start = (f32[2,32,384]{2,1,0:T(8,128)S(1)}, f32[2,32,384]{2,1,0:T(8,128)S(1)}, u32[]{:S(2)}, u32[]{:S(2)}) collective-permute-start(f32[2,32,384]{2,1,0:T(8,128)S(1)} %get-tuple-element.9.one_ref), channel_id=1, source_target_pairs={{0,16},{16,0},{1,17},{17,1},{2,18},{18,2},{3,19},{19,3},{4,20},{20... | collective-permute-start | bytes 294920 | tf_op jit(solution)/shard_map/ppermute | solution.py:539
  34.3 4.9 %collective-permute-done.other_ref = f32[2,32,384]{2,1,0:T(8,128)S(1)} collective-permute-done((f32[2,32,384]{2,1,0:T(8,128)S(1)}, f32[2,32,384]{2,1,0:T(8,128)S(1)}, u32[]{:S(2)}, u32[]{:S(2)}) %collective-permute-start) | collective-permute-done | bytes 98336 | tf_op jit(solution)/shard_map/ppermute | solution.py:539
  39.2 0.0 copy-start
  39.2 0.0 copy-start.1
  39.2 1.3 %forward_adjoint.1 = (f32[32,128]{1,0:T(8,128)S(1)}, f32[2,32,384]{2,1,0:T(8,128)S(1)}, bf16[2,32,384]{2,1,0:T(8,128)(2,1)S(1)}) custom-call(bf16[8,2,400,128]{3,2,1,0:T(8,128)(2,1)S(1)} %bitcast.4, f32[2,32,384]{2,1,0:T(8,128)S(1)} %get-tuple-element.9.one_ref, f32[2,32,384]{2,1,0:T(8,128)S(1)} %collective-permute-done.other_ref, ...), custom_call_target="tpu_custom_call" | custom-call | tf_op jit(solution)/shard_map/forward_adjoint/pallas_call | solution.py:552
  40.5 0.7 %collective-permute-start.1 = (bf16[2,32,384]{2,1,0:T(8,128)(2,1)S(1)}, bf16[2,32,384]{2,1,0:T(8,128)(2,1)S(1)}, u32[]{:S(2)}, u32[]{:S(2)}) collective-permute-start(bf16[2,32,384]{2,1,0:T(8,128)(2,1)S(1)} %get-tuple-element.14), channel_id=1, source_target_pairs={{0,16},{16,0},{1,17},{17,1},{2,18},{18,2},{3,19},{19,3},{4,20},{20... | collective-permute-start | bytes 147464 | tf_op jit(solution)/shard_map/ppermute | solution.py:539
  41.2 4.8 %collective-permute-done.1.other_ref = bf16[2,32,384]{2,1,0:T(8,128)(2,1)S(1)} collective-permute-done((bf16[2,32,384]{2,1,0:T(8,128)(2,1)S(1)}, bf16[2,32,384]{2,1,0:T(8,128)(2,1)S(1)}, u32[]{:S(2)}, u32[]{:S(2)}) %collective-permute-start.1) | collective-permute-done | bytes 49184 | tf_op jit(solution)/shard_map/ppermute | solution.py:539
  46.0 1.1 %last_forward.1 = f32[16,4,128]{2,1,0:T(4,128)S(1)} custom-call(bf16[8,2,400,128]{3,2,1,0:T(8,128)(2,1)S(1)} %bitcast.5, f32[2,32,384]{2,1,0:T(8,128)S(1)} %get-tuple-element.13.one_ref, bf16[2,32,384]{2,1,0:T(8,128)(2,1)S(1)} %collective-permute-done.1.other_ref, f32[32,128]{1,0:T(8,128)S(1)} %get-tuple-element.15.residual_ref, ...), custom_call_target="tpu_custom_call" | custom-call | tf_op jit(solution)/shard_map/last_forward/pallas_call | solution.py:558
  47.1 8.2 %all_to_all.11.got_ref = f32[16,4,128]{2,1,0:T(4,128)S(1)} all-to-all(f32[16,4,128]{2,1,0:T(4,128)S(1)} %last_forward.1), channel_id=1, replica_groups=mesh['top'=2,'low'=8,'par'=2] {'low','par'}, dimensions={0} | all-to-all | bytes 65536 | tf_op jit(solution)/shard_map/all_to_all | solution.py:564
  55.3 0.0 copy-done
  55.3 0.0 copy-done.1
  55.3 1.0 %to_time.1 = (f32[2,8,256]{2,1,0:T(8,128)}, f32[2,8,256]{2,1,0:T(8,128)}) custom-call(f32[16,4,128]{2,1,0:T(4,128)S(1)} %all_to_all.11.got_ref, f32[256,256]{1,0:T(8,128)S(1)} %copy-done, f32[1,8]{1,0:T(1,128)S(1)} %bitcast.7), custom_call_target="tpu_custom_call" | custom-call | tf_op jit(solution)/shard_map/to_time/pallas_call | solution.py:565
Async XLA Ops:
  31.7 7.5 %collective-permute-start = (f32[2,32,384]{2,1,0:T(8,128)S(1)}, f32[2,32,384]{2,1,0:T(8,128)S(1)}, u32[]{:S(2)}, u32[]{:S(2)}) collective-permute-start(f32[2,32,384]{2,1,0:T(8,128)S(1)} %get-tuple-element.9.one_ref), channel_id=1, source_target_pairs={{0,16},{16,0},{1,17},{17,1},{2,18},{18,2},{3,19},{19,3},{4,20},{20... | collective-permute-start | bytes 294920 | tf_op jit(solution)/shard_map/ppermute | solution.py:539
  39.2 16.1 %copy-start = (f32[256,256]{1,0:T(8,128)S(1)}, f32[256,256]{1,0:T(8,128)}, u32[]{:S(2)}) copy-start(f32[256,256]{1,0:T(8,128)} %constant.5.clone.basis_ref) | copy-start | bytes 786436
  39.2 16.1 %copy-start.1 = (f32[8]{0:T(128)S(1)}, f32[8]{0:T(128)}, u32[]{:S(2)}) copy-start(f32[8]{0:T(128)} %param.11) | copy-start | bytes 100
  40.5 5.5 %collective-permute-start.1 = (bf16[2,32,384]{2,1,0:T(8,128)(2,1)S(1)}, bf16[2,32,384]{2,1,0:T(8,128)(2,1)S(1)}, u32[]{:S(2)}, u32[]{:S(2)}) collective-permute-start(bf16[2,32,384]{2,1,0:T(8,128)(2,1)S(1)} %get-tuple-element.14), channel_id=1, source_target_pairs={{0,16},{16,0},{1,17},{17,1},{2,18},{18,2},{3,19},{19,3},{4,20},{20... | collective-permute-start | bytes 147464 | tf_op jit(solution)/shard_map/ppermute | solution.py:539

commit v12 on v11

--- a/solution.py
+++ b/solution.py
@@ -14,6 +14,7 @@
 REACH = 3
 LANES = 128
 DEPTH = 256
+KINDS = 4
 
 
 def make_basis(length):
@@ -171,9 +172,9 @@
     return high, middle, (x - high - middle).astype(jnp.bfloat16).astype(jnp.float32)
 
 
-def tail_lanes(rows, pair):
-    start = 3 * rows * pair
-    return start, LANES // (LANES - start), LANES - start
+def tail_lanes(each, pair):
+    start = 2 * 3 * pair
+    return start, LANES - start, each // KINDS
 
 
 def outbound_kernel(
@@ -182,8 +183,7 @@
     small_sems, in_sems,
 ):
     _, devices, each, sensors, width = resp_ref.shape
-    pair, lines = 2 * sensors, 2 * each
-    tiles = width // LANES
+    pair, tiles = 2 * sensors, width // LANES
     steps = in_sems.shape[0]
     some = devices // steps
     pieces = [pl.ds(i * some, some) for i in range(steps)]
@@ -210,14 +210,11 @@
 
     for copy in small:
         copy.wait()
-    rows = vectors_ref.shape[0]
     noise = upright(noise_ref[...])
-    records = []
-    for r in range(rows):
-        record = vectors_ref[r]
-        records += [record, observed_ref[r] - noise * record]
-    filled = rows * pair
-    records.append(jnp.zeros((LANES - filled, records[0].shape[1]), jnp.float32))
+    core = lax.axis_index("par")
+    record = vectors_ref[core]
+    records = [record, observed_ref[core] - noise * record]
+    records.append(jnp.zeros((LANES - pair, record.shape[1]), jnp.float32))
     spectra = lax.dot_general(
         basis_ref[...],
         jnp.concatenate(records, axis=0),
@@ -227,24 +224,30 @@
     )
     exact = iota(spectra.shape, 1) // sensors % 2 == 1
     high, middle, low = split(spectra)
-    packed = high + roll(jnp.where(exact, middle, 0.0), filled, 1)
-    packed = packed + roll(jnp.where(exact, low, 0.0), 2 * filled, 1)
-
-    start, chunks, free = tail_lanes(rows, pair)
-    turn = lax.axis_index("low") % tiles
+    packed = high + roll(jnp.where(exact, middle, 0.0), pair, 1)
+    packed = packed + roll(jnp.where(exact, low, 0.0), 2 * pair, 1)
+    packed = packed[: devices * each] + roll(packed[devices * each :], 3 * pair, 1)
+
+    start, free, chunks = tail_lanes(each, pair)
+    piece = chunks * free
+    per = LANES // piece
+    turn = lax.axis_index("low") % (width // piece)
     coefs, links = (
         sum(
-            jnp.where(turn == j, ref[:, j * LANES : (j + 1) * LANES].astype(jnp.float32), 0.0)
+            jnp.where(turn // per == j, ref[:, j * LANES : (j + 1) * LANES].astype(jnp.float32), 0.0)
             for j in range(tiles)
         )
         for ref in (coef_ref, link_ref)
     )
-    grid = jnp.concatenate([*split(coefs), links], axis=0)
+    whole = jnp.concatenate([*split(coefs), links], axis=0)
+    grid = whole
+    for i in range(1, per):
+        grid = jnp.where(turn % per == i, roll(whole, -i * piece, 1), grid)
     grid = jnp.concatenate([roll(grid, start - i * free, 1) for i in range(chunks)], axis=0)
     grid = jnp.where(iota(grid.shape, 1) >= start, grid, 0.0)
-    packed = packed.reshape(devices, lines, LANES) + grid[None]
+    packed = packed.reshape(devices, each, LANES) + grid[None]
     packed = packed.astype(jnp.bfloat16)
-    out_ref[:, pl.ds(body, lines), :] = packed
+    out_ref[:, pl.ds(body, each), :] = packed
 
     for i, piece in enumerate(pieces):
         loads[i].wait()
@@ -261,9 +264,8 @@
         self.got = got_ref
         self.low, self.par = got_ref.shape[:2]
         self.rows, self.each, self.width = rows, each, width
-        self.lines = 2 * each
         self.tiles = width // LANES
-        self.pair = (got_ref.shape[2] - self.lines) // (each * self.tiles)
+        self.pair = (got_ref.shape[2] - each) // (each * self.tiles)
         self.sensors = self.pair // 2
         self.lanes = self.low * self.pair
         self.joint = joint_of(each, self.lanes)
@@ -271,12 +273,12 @@
         self.held = rows * 2 * self.joint
         shape = (self.held, self.lanes)
         row = iota(shape, 0)
-        self.real_row = row % 2 == 0
+        self.real_row = row // self.joint % 2 == 0
         self.real_lane = iota(shape, 1) // self.sensors % 2 == 0
-        self.place = row // 2 % self.joint
+        self.place = row % self.joint
 
     def swapped(self, x):
-        return jnp.where(self.real_row, roll(x, -1, 0), roll(x, 1, 0))
+        return jnp.where(self.real_row, roll(x, -self.joint, 0), roll(x, self.joint, 0))
 
     def block(self, group, p):
         return jnp.concatenate(
@@ -295,47 +297,46 @@
             axis=0,
         )
 
+    def tail(self, count):
+        rows = pl.ds(self.got.shape[2] - self.each, self.each)
+        return self.got[pl.ds(0, count), :, rows, :].astype(jnp.float32)
+
     def spectra(self):
-        tail = self.got[:, 0, pl.ds(self.got.shape[2] - self.lines, self.lines), :]
-        tail = tail.astype(jnp.float32)
-        filled = self.rows * self.pair
-        shape = (self.lines, LANES)
+        tail = self.tail(self.low)
+        shape = (self.each, LANES)
         at = iota(shape, 1) // self.pair
         per = LANES // self.pair
         found = [
             [jnp.zeros(shape, jnp.float32) for _ in range(self.lanes // LANES)]
-            for _ in range(self.rows)
+            for _ in range(2 * self.rows)
         ]
         for i in range(self.low):
-            packed = tail[i]
-            packed = packed + roll(packed, -filled, 1) + roll(packed, -2 * filled, 1)
             h, place = divmod(i, per)
             for r in range(self.rows):
-                moved = roll(packed, (place - r) * self.pair, 1)
-                found[r][h] = jnp.where(at == place, moved, found[r][h])
+                packed = tail[i, r]
+                packed = packed + roll(packed, -self.pair, 1) + roll(packed, -2 * self.pair, 1)
+                for c in range(2):
+                    moved = roll(packed, (place - 3 * c) * self.pair, 1)
+                    line = found[2 * r + c]
+                    line[h] = jnp.where(at == place, moved, line[h])
         found = [jnp.concatenate(line, axis=1) for line in found]
-        few = 2 * self.joint
         return [
-            jnp.concatenate([line[g * few : (g + 1) * few] for line in found], axis=0)
+            jnp.concatenate([line[g * self.joint : (g + 1) * self.joint] for line in found], axis=0)
             for g in range(self.groups)
         ]
 
     def grid(self):
-        start, chunks, free = tail_lanes(self.rows, self.pair)
-        kinds = self.lines // chunks
-        chunk = iota((kinds, LANES), 1) // free
+        start, free, chunks = tail_lanes(self.each, self.pair)
+        count = self.width // (chunks * free)
+        tail = self.tail(count)
+        chunk = iota((KINDS, LANES), 1) // free
         coefs, links = [], []
         for p in range(self.par):
-            tail = self.got[
-                pl.ds(0, self.tiles), p, pl.ds(self.got.shape[2] - self.lines, self.lines), :
-            ].astype(jnp.float32)
-            found = []
-            for j in range(self.tiles):
-                line = jnp.zeros((kinds, LANES), jnp.float32)
-                for i in range(chunks):
-                    part = roll(tail[j, i * kinds : (i + 1) * kinds], i * free - start, 1)
-                    line = jnp.where(chunk == i, part, line)
-                found.append(line)
+            found = [jnp.zeros((KINDS, LANES), jnp.float32) for _ in range(self.tiles)]
+            for i in range(count * chunks):
+                part = tail[i // chunks, p, i % chunks * KINDS : (i % chunks + 1) * KINDS]
+                j, at = divmod(i * free, LANES)
+                found[j] = jnp.where(chunk == at // free, roll(part, at - start, 1), found[j])
             found = jnp.concatenate(found, axis=1)
             coefs.append(found[0:1] + found[1:2] + found[2:3])
             links.append(found[3:4])
@@ -505,7 +506,7 @@
     room = lambda mib: pltpu.CompilerParams(vmem_limit_bytes=mib * 2**20)
 
     steps = 2 if shares % 2 == 0 else 1
-    tall = each * width // LANES * pair + 2 * each
+    tall = each * width // LANES * pair + each
     operator = operator.reshape(2, shares, each, sensors, width)
     scratch = [
         pltpu.VMEM(array.shape, array.dtype) for array in (operator, *small)
@@ -529,7 +530,7 @@
             for x in (
                 operator,
                 *small,
-                jnp.asarray(basis.transpose(2, 3, 1, 0).reshape(length, length)),
+                jnp.asarray(basis.transpose(1, 2, 3, 0).reshape(length, length)),
             )
         )
     )
@@ -540,6 +541,7 @@
 
     share = functools.partial(Share, rows=rows, each=each, width=width)
     held, lanes = rows * 2 * each, low * pair
+    joint = joint_of(each, lanes)
     sums = f32(par, held, width)
     rounded = jax.ShapeDtypeStruct(sums.shape, jnp.bfloat16)
     grid = [f32(par, width)] * 2
@@ -557,17 +559,18 @@
     )(got, one, across(one), spectra, coefs, links)
     message = pl.pallas_call(
         functools.partial(last_kernel, share),
-        out_shape=f32(shares, each // joint_of(each, lanes), LANES),
+        out_shape=f32(shares, each // joint, LANES),
         compiler_params=room(32),
         name="last_forward",
     )(got, two, across(sent), residual, coefs, links)
     got = lax.all_to_all(message, axes, 0, 0, tiled=True)
+    turned = basis.reshape(length, 2, shares, each // joint, joint)
     return pl.pallas_call(
         home_kernel,
         out_shape=[f32(rows, sensors, length)] * 2,
         compiler_params=room(16),
         name="to_time",
-    )(got, jnp.asarray(basis.transpose(3, 1, 2, 0).reshape(length, length)), noise)
+    )(got, jnp.asarray(turned.transpose(3, 1, 4, 2, 0).reshape(length, length)), noise)
 
 
 def fits(mesh, args):
@@ -578,16 +581,19 @@
     if sen % 2 or half % (low * par) or sensors % sen or coefficient.shape[0] != par:
         return False
     each, pair = half // (low * par), 2 * (sensors // sen)
+    start, free, chunks = tail_lanes(each, pair)
+    piece = chunks * free
     return (
-        2 * rows * joint_of(each, low * pair) * pair == LANES
-        and 3 * rows * pair < LANES
+        rows == par
+        and pair == 16
+        and each % KINDS == 0
         and each % joint_of(each, low * pair) == 0
-        and LANES % (LANES - 3 * rows * pair) == 0
-        and 4 * tail_lanes(rows, pair)[1] == 2 * each
-        and low * LANES >= coefficient.shape[1]
-        and pair == 16
+        and 2 * rows * joint_of(each, low * pair) * pair == LANES
         and low * pair % LANES == 0
         and coefficient.shape[1] % LANES == 0
+        and start < LANES
+        and LANES % piece == 0
+        and low * piece >= coefficient.shape[1]
     )
 
 

time: 56.6 us -> 56.3 us (level)
  no operation moved by 1% of the time
where the time goes in v12:
time: 56.3 us; the launch traced here: 56.1 us
  blocking collectives  36.4 us (65%)
  waiting for transfers between devices  9.79 us (17%)
  Pallas kernels  5.95 us (11%)
  starting transfers between devices  3.24 us (6%)
  between operations  0.65 us (1%)
    all_to_all x1, blocking collectives, body_fast(): lax.all_to_all(message, axes, 0, 0, tiled=True)  28.2 us
    ppermute x2, waiting for transfers between devices, across(): return lax.ppermute(sums, 'top', [(i, (i + 1) % top) for i in range(top)])  9.79 us
    all_to_all x1, blocking collectives, body_fast(): got = lax.all_to_all(message, axes, 0, 0, tiled=True)  8.22 us
    ppermute x2, starting transfers between devices, across(): return lax.ppermute(sums, 'top', [(i, (i + 1) % top) for i in range(top)])  3.24 us
    pallas_call x1, Pallas kernels, body_fast(): pl.pallas_call(outbound_kernel, in_specs=[pl.BlockSpec(memory_space=pl.AN...  2 us
    pallas_call x1, Pallas kernels, body_fast(): pl.pallas_call(functools.partial(middle_kernel, share), out_shape=[f32(he...  1.3 us
  transfers between devices with their start and end apart: 2, of which 2 were waited for; matrix products, arithmetic and copies ran while one was open for 0% of the time, Pallas kernels for 0%

profile of v12, /device:TPU:0, one launch (start us, length us, event | category | flops | bytes accessed | tf_op | source)
XLA Modules:
  0.0 56.1 jit_solution(11622116042202616350)
XLA Ops:
  0.6 2.0 %outbound.1 = bf16[16,392,128]{2,1,0:T(8,128)(2,1)S(1)} custom-call(bf16[2,16,8,8,384]{4,3,2,1,0:T(8,128)(2,1)} %bitcast.8, f32[2,8,256]{2,1,0:T(8,128)} %vectors_hbm.1, f32[2,8,256]{2,1,0:T(8,128)} %observed_hbm.1, f32[1,8]{1,0:T(1,128)} %bitcast.6, f32[1,384]{1,0:T(1,128)} %coef_hbm.1, s32[1,384]{1,0:T(1,128)} %link_hbm.1, f32[256,256]{1,0:T(8,128)} %constant.4.clone.basis_hbm), custom_call_target="tpu_custom_call" | custom-call | tf_op jit(solution)/shard_map/outbound/pallas_call | solution.py:514
  2.6 28.2 %all_to_all.10 = bf16[16,392,128]{2,1,0:T(8,128)(2,1)S(1)} all-to-all(bf16[16,392,128]{2,1,0:T(8,128)(2,1)S(1)} %outbound.1), channel_id=1, replica_groups=mesh['top'=2,'low'=8,'par'=2] {'low','par'}, dimensions={0} | all-to-all | bytes 3211264 | tf_op jit(solution)/shard_map/all_to_all | solution.py:537
  30.9 0.5 first_adjoint.1
  31.4 2.6 %collective-permute-start = (f32[2,32,384]{2,1,0:T(8,128)S(1)}, f32[2,32,384]{2,1,0:T(8,128)S(1)}, u32[]{:S(2)}, u32[]{:S(2)}) collective-permute-start(f32[2,32,384]{2,1,0:T(8,128)S(1)} %get-tuple-element.9.one_ref), channel_id=1, source_target_pairs={{0,16},{16,0},{1,17},{17,1},{2,18},{18,2},{3,19},{19,3},{4,20},{20... | collective-permute-start | bytes 294920 | tf_op jit(solution)/shard_map/ppermute | solution.py:540
  34.0 5.1 %collective-permute-done.other_ref = f32[2,32,384]{2,1,0:T(8,128)S(1)} collective-permute-done((f32[2,32,384]{2,1,0:T(8,128)S(1)}, f32[2,32,384]{2,1,0:T(8,128)S(1)}, u32[]{:S(2)}, u32[]{:S(2)}) %collective-permute-start) | collective-permute-done | bytes 98336 | tf_op jit(solution)/shard_map/ppermute | solution.py:540
  39.1 0.0 copy-start
  39.1 0.0 copy-start.1
  39.1 1.3 %forward_adjoint.1 = (f32[32,128]{1,0:T(8,128)S(1)}, f32[2,32,384]{2,1,0:T(8,128)S(1)}, bf16[2,32,384]{2,1,0:T(8,128)(2,1)S(1)}) custom-call(bf16[8,2,392,128]{3,2,1,0:T(8,128)(2,1)S(1)} %bitcast.4, f32[2,32,384]{2,1,0:T(8,128)S(1)} %get-tuple-element.9.one_ref, f32[2,32,384]{2,1,0:T(8,128)S(1)} %collective-permute-done.other_ref, ...), custom_call_target="tpu_custom_call" | custom-call | tf_op jit(solution)/shard_map/forward_adjoint/pallas_call | solution.py:554
  40.4 0.6 %collective-permute-start.1 = (bf16[2,32,384]{2,1,0:T(8,128)(2,1)S(1)}, bf16[2,32,384]{2,1,0:T(8,128)(2,1)S(1)}, u32[]{:S(2)}, u32[]{:S(2)}) collective-permute-start(bf16[2,32,384]{2,1,0:T(8,128)(2,1)S(1)} %get-tuple-element.14), channel_id=1, source_target_pairs={{0,16},{16,0},{1,17},{17,1},{2,18},{18,2},{3,19},{19,3},{4,20},{20... | collective-permute-start | bytes 147464 | tf_op jit(solution)/shard_map/ppermute | solution.py:540
  41.0 4.7 %collective-permute-done.1.other_ref = bf16[2,32,384]{2,1,0:T(8,128)(2,1)S(1)} collective-permute-done((bf16[2,32,384]{2,1,0:T(8,128)(2,1)S(1)}, bf16[2,32,384]{2,1,0:T(8,128)(2,1)S(1)}, u32[]{:S(2)}, u32[]{:S(2)}) %collective-permute-start.1) | collective-permute-done | bytes 49184 | tf_op jit(solution)/shard_map/ppermute | solution.py:540
  45.7 1.1 %last_forward.1 = f32[16,4,128]{2,1,0:T(4,128)S(1)} custom-call(bf16[8,2,392,128]{3,2,1,0:T(8,128)(2,1)S(1)} %bitcast.5, f32[2,32,384]{2,1,0:T(8,128)S(1)} %get-tuple-element.13.one_ref, bf16[2,32,384]{2,1,0:T(8,128)(2,1)S(1)} %collective-permute-done.1.other_ref, f32[32,128]{1,0:T(8,128)S(1)} %get-tuple-element.15.residual_ref, ...), custom_call_target="tpu_custom_call" | custom-call | tf_op jit(solution)/shard_map/last_forward/pallas_call | solution.py:560
  46.8 8.2 %all_to_all.11.got_ref = f32[16,4,128]{2,1,0:T(4,128)S(1)} all-to-all(f32[16,4,128]{2,1,0:T(4,128)S(1)} %last_forward.1), channel_id=1, replica_groups=mesh['top'=2,'low'=8,'par'=2] {'low','par'}, dimensions={0} | all-to-all | bytes 65536 | tf_op jit(solution)/shard_map/all_to_all | solution.py:566
  55.1 0.0 copy-done
  55.1 0.0 copy-done.1
  55.1 1.0 %to_time.1 = (f32[2,8,256]{2,1,0:T(8,128)}, f32[2,8,256]{2,1,0:T(8,128)}) custom-call(f32[16,4,128]{2,1,0:T(4,128)S(1)} %all_to_all.11.got_ref, f32[256,256]{1,0:T(8,128)S(1)} %copy-done, f32[1,8]{1,0:T(1,128)S(1)} %bitcast.7), custom_call_target="tpu_custom_call" | custom-call | tf_op jit(solution)/shard_map/to_time/pallas_call | solution.py:568
Async XLA Ops:
  31.4 7.7 %collective-permute-start = (f32[2,32,384]{2,1,0:T(8,128)S(1)}, f32[2,32,384]{2,1,0:T(8,128)S(1)}, u32[]{:S(2)}, u32[]{:S(2)}) collective-permute-start(f32[2,32,384]{2,1,0:T(8,128)S(1)} %get-tuple-element.9.one_ref), channel_id=1, source_target_pairs={{0,16},{16,0},{1,17},{17,1},{2,18},{18,2},{3,19},{19,3},{4,20},{20... | collective-permute-start | bytes 294920 | tf_op jit(solution)/shard_map/ppermute | solution.py:540
  39.1 16.0 %copy-start = (f32[256,256]{1,0:T(8,128)S(1)}, f32[256,256]{1,0:T(8,128)}, u32[]{:S(2)}) copy-start(f32[256,256]{1,0:T(8,128)} %constant.5.clone.basis_ref) | copy-start | bytes 786436
  39.1 16.0 %copy-start.1 = (f32[8]{0:T(128)S(1)}, f32[8]{0:T(128)}, u32[]{:S(2)}) copy-start(f32[8]{0:T(128)} %param.11) | copy-start | bytes 100
  40.4 5.4 %collective-permute-start.1 = (bf16[2,32,384]{2,1,0:T(8,128)(2,1)S(1)}, bf16[2,32,384]{2,1,0:T(8,128)(2,1)S(1)}, u32[]{:S(2)}, u32[]{:S(2)}) collective-permute-start(bf16[2,32,384]{2,1,0:T(8,128)(2,1)S(1)} %get-tuple-element.14), channel_id=1, source_target_pairs={{0,16},{16,0},{1,17},{17,1},{2,18},{18,2},{3,19},{19,3},{4,20},{20... | collective-permute-start | bytes 147464 | tf_op jit(solution)/shard_map/ppermute | solution.py:540

commit v13 on v12

--- a/solution.py
+++ b/solution.py
@@ -14,6 +14,7 @@
 REACH = 3
 LANES = 128
 DEPTH = 256
+PARTS = 2
 KINDS = 4
 
 
@@ -25,6 +26,14 @@
     angle = phase.astype(np.float64) * (math.pi / length)
     scale = math.sqrt(2.0 / length)
     return (np.concatenate([np.cos(angle), np.sin(angle)], axis=1) * scale).astype(np.float32)
+
+
+def thirds(x):
+    parts = []
+    for _ in range(3):
+        parts.append(x.astype(jnp.bfloat16))
+        x = x - parts[-1].astype(np.float32)
+    return np.stack(parts)
 
 
 def halo(field, axis, dim):
@@ -428,8 +437,8 @@
     def summed(self, own_ref, other_ref):
         whole = [own_ref[p] + other_ref[p].astype(jnp.float32) for p in range(self.par)]
         return [
-            [part[g * self.held : (g + 1) * self.held] for part in whole]
-            for g in range(self.groups)
+            [part[i : i + self.held] for part in whole]
+            for i in range(0, own_ref.shape[1], self.held)
         ]
 
 
@@ -443,21 +452,34 @@
     sums = []
     for g, spectra in enumerate(share.spectra()):
         spectra_ref[share.rows_of(g), :] = spectra
-        sums.append(share.adjoint(g, spectra))
+        if g * share.held < own_ref.shape[1]:
+            sums.append(share.adjoint(g, spectra))
     share.give(sums, own_ref)
 
 
-def middle_kernel(
-    share, got_ref, one_ref, other_ref, spectra_ref, coef_ref, link_ref, residual_ref, own_ref, sent_ref
-):
+def more_kernel(share, first, got_ref, spectra_ref, own_ref):
+    share = share(got_ref)
+    groups = range(first, first + own_ref.shape[1] // share.held)
+    share.give([share.adjoint(g, spectra_ref[share.rows_of(g), :]) for g in groups], own_ref)
+
+
+def middle_kernel(share, first, got_ref, one_ref, other_ref, spectra_ref, coef_ref, link_ref, *refs):
+    *before, residual_ref, own_ref, sent_ref = refs
     share = share(got_ref)
     masks = share.masks(coef_ref, link_ref)
     residuals = []
-    for g, field in enumerate(share.summed(one_ref, other_ref)):
-        rest = roll(spectra_ref[share.rows_of(g), :], -share.sensors, 1)
-        residuals.append(rest - share.forward(g, share.smoothed(field, masks)))
-        residual_ref[share.rows_of(g), :] = residuals[g]
-    share.give([share.adjoint(g, x) for g, x in enumerate(residuals)], own_ref, sent_ref)
+    for i, field in enumerate(share.summed(one_ref, other_ref)):
+        rest = roll(spectra_ref[share.rows_of(first + i), :], -share.sensors, 1)
+        residuals.append(rest - share.forward(first + i, share.smoothed(field, masks)))
+        residual_ref[share.rows_of(first + i), :] = residuals[i]
+    sums = [share.adjoint(first + i, x) for i, x in enumerate(residuals)]
+    done = first * share.held
+    for old, new in zip(before, (residual_ref, own_ref, sent_ref)):
+        new[..., :done, :] = old[...]
+    for p in range(share.par):
+        part = jnp.concatenate([line[p] for line in sums], axis=0)
+        own_ref[p, done:, :] = part
+        sent_ref[p, done:, :] = part.astype(sent_ref.dtype)
 
 
 def last_kernel(share, got_ref, one_ref, other_ref, residual_ref, coef_ref, link_ref, out_ref):
@@ -479,12 +501,14 @@
         for r in range(rows):
             first, last = r * LANES // rows, (r + 1) * LANES // rows
             lines[r] += [turned[i : i + pair, :] for i in range(first, last, pair)]
-    back = jnp.dot(
-        jnp.concatenate([jnp.concatenate(line, axis=1) for line in lines], axis=0),
-        basis_ref[...],
-        precision=lax.Precision.HIGHEST,
-        preferred_element_type=jnp.float32,
-    )
+    spectra = jnp.concatenate([jnp.concatenate(line, axis=1) for line in lines], axis=0)
+    parts = [part.astype(jnp.bfloat16) for part in split(spectra)]
+    back = jnp.zeros((spectra.shape[0], basis_ref.shape[2]), jnp.float32)
+    for i in reversed(range(len(parts))):
+        left = jnp.concatenate(parts[: len(parts) - i], axis=0)
+        product = jnp.dot(left, basis_ref[i], preferred_element_type=jnp.float32)
+        for k in reversed(range(len(parts) - i)):
+            back += product[k * spectra.shape[0] : (k + 1) * spectra.shape[0]]
     for r in range(rows):
         residual = back[r * pair : r * pair + sensors]
         residual_ref[r] = residual
@@ -542,24 +566,41 @@
     share = functools.partial(Share, rows=rows, each=each, width=width)
     held, lanes = rows * 2 * each, low * pair
     joint = joint_of(each, lanes)
-    sums = f32(par, held, width)
-    rounded = jax.ShapeDtypeStruct(sums.shape, jnp.bfloat16)
+    groups = each // joint_of(each, lanes)
+    parts = PARTS if groups % PARTS == 0 else 1
+    some = groups // parts
     grid = [f32(par, width)] * 2
+    part = f32(par, held // parts, width)
     spectra, coefs, links, one = pl.pallas_call(
         functools.partial(first_kernel, share),
-        out_shape=[f32(held, lanes)] + grid + [sums],
+        out_shape=[f32(held, lanes)] + grid + [part],
         compiler_params=room(32),
         name="first_adjoint",
     )(got)
-    residual, two, sent = pl.pallas_call(
-        functools.partial(middle_kernel, share),
-        out_shape=[f32(held, lanes), sums, rounded],
-        compiler_params=room(32),
-        name="forward_adjoint",
-    )(got, one, across(one), spectra, coefs, links)
+    ones = [one] + [
+        pl.pallas_call(
+            functools.partial(more_kernel, share, i * some),
+            out_shape=part,
+            compiler_params=room(32),
+            name="more_adjoint",
+        )(got, spectra)
+        for i in range(1, parts)
+    ]
+    others = [across(one) for one in ones]
+    middle = []
+    for i in range(parts):
+        done = held * (i + 1) // parts
+        sent = jax.ShapeDtypeStruct((par, done, width), jnp.bfloat16)
+        middle = pl.pallas_call(
+            functools.partial(middle_kernel, share, i * some),
+            out_shape=[f32(done, lanes), f32(par, done, width), sent],
+            compiler_params=room(32),
+            name="forward_adjoint",
+        )(got, ones[i], others[i], spectra, coefs, links, *middle)
+    residual, two, sent = middle
     message = pl.pallas_call(
         functools.partial(last_kernel, share),
-        out_shape=f32(shares, each // joint, LANES),
+        out_shape=f32(shares, groups, LANES),
         compiler_params=room(32),
         name="last_forward",
     )(got, two, across(sent), residual, coefs, links)
@@ -570,7 +611,7 @@
         out_shape=[f32(rows, sensors, length)] * 2,
         compiler_params=room(16),
         name="to_time",
-    )(got, jnp.asarray(turned.transpose(3, 1, 4, 2, 0).reshape(length, length)), noise)
+    )(got, jnp.asarray(thirds(turned.transpose(3, 1, 4, 2, 0).reshape(length, length))), noise)
 
 
 def fits(mesh, args):

time: 56.3 us -> 56.3 us (level)
  waiting for transfers between devices: 9.79 us -> 9.02 us
  Pallas kernels: 5.95 us -> 6.65 us
    pallas_call x1 -> x3, Pallas kernels: 1.3 us -> 2.14 us  [the longest x2 1.88 us: body_fast(): pl.pallas_call(functools.partial(middle_kernel, share, i * some), out_sha...]
    ppermute x2 -> x3, waiting for transfers between devices: 9.79 us -> 9.02 us  [across(): return lax.ppermute(sums, 'top', [(i, (i + 1) % top) for i in range(top)])]
    ppermute x2 -> x3, starting transfers between devices: 3.24 us -> 3.29 us  [across(): return lax.ppermute(sums, 'top', [(i, (i + 1) % top) for i in range(top)])]
  transfers between devices with their start and end apart: 2 -> 3, of which waited for: 2 -> 3; matrix products, arithmetic and copies ran while one was open for 0% -> 0% of each run, Pallas kernels for 0% -> 2%
where the time goes in v13:
time: 56.3 us; the launch traced here: 56.1 us
  blocking collectives  36.4 us (65%)
  waiting for transfers between devices  9.02 us (16%)
  Pallas kernels  6.65 us (12%)
  starting transfers between devices  3.29 us (6%)
  between operations  0.66 us (1%)
    all_to_all x1, blocking collectives, body_fast(): lax.all_to_all(message, axes, 0, 0, tiled=True)  28.2 us
    ppermute x3, waiting for transfers between devices, across(): return lax.ppermute(sums, 'top', [(i, (i + 1) % top) for i in range(top)])  9.02 us
    all_to_all x1, blocking collectives, body_fast(): got = lax.all_to_all(message, axes, 0, 0, tiled=True)  8.22 us
    ppermute x3, starting transfers between devices, across(): return lax.ppermute(sums, 'top', [(i, (i + 1) % top) for i in range(top)])  3.29 us
    pallas_call x1, Pallas kernels, body_fast(): pl.pallas_call(outbound_kernel, in_specs=[pl.BlockSpec(memory_space=pl.AN...  2 us
    pallas_call x2, Pallas kernels, body_fast(): pl.pallas_call(functools.partial(middle_kernel, share, i * some), out_sha...  1.88 us
  transfers between devices with their start and end apart: 3, of which 3 were waited for; matrix products, arithmetic and copies ran while one was open for 0% of the time, Pallas kernels for 2%

profile of v13, /device:TPU:0, one launch (start us, length us, event | category | flops | bytes accessed | tf_op | source)
XLA Modules:
  0.0 56.1 jit_solution(17745191992648098684)
XLA Ops:
  0.6 2.0 %outbound.1 = bf16[16,392,128]{2,1,0:T(8,128)(2,1)S(1)} custom-call(bf16[2,16,8,8,384]{4,3,2,1,0:T(8,128)(2,1)} %bitcast.10, f32[2,8,256]{2,1,0:T(8,128)} %vectors_hbm.1, f32[2,8,256]{2,1,0:T(8,128)} %observed_hbm.1, f32[1,8]{1,0:T(1,128)} %bitcast.8, f32[1,384]{1,0:T(1,128)} %coef_hbm.1, s32[1,384]{1,0:T(1,128)} %link_hbm.1, f32[256,256]{1,0:T(8,128)} %constant.4.clone.basis_hbm), custom_call_target="tpu_custom_call" | custom-call | tf_op jit(solution)/shard_map/outbound/pallas_call | solution.py:538
  2.6 28.2 %all_to_all.10 = bf16[16,392,128]{2,1,0:T(8,128)(2,1)S(1)} all-to-all(bf16[16,392,128]{2,1,0:T(8,128)(2,1)S(1)} %outbound.1), channel_id=1, replica_groups=mesh['top'=2,'low'=8,'par'=2] {'low','par'}, dimensions={0} | all-to-all | bytes 3211264 | tf_op jit(solution)/shard_map/all_to_all | solution.py:561
  30.9 0.4 first_adjoint.1
  31.3 2.6 %collective-permute-start.1 = (f32[2,16,384]{2,1,0:T(8,128)S(1)}, f32[2,16,384]{2,1,0:T(8,128)S(1)}, u32[]{:S(2)}, u32[]{:S(2)}) collective-permute-start(f32[2,16,384]{2,1,0:T(8,128)S(1)} %get-tuple-element.15.one_ref), channel_id=1, source_target_pairs={{0,16},{16,0},{1,17},{17,1},{2,18},{18,2},{3,19},{19,3},{4,20},{20... | collective-permute-start | bytes 147464 | tf_op jit(solution)/shard_map/ppermute | solution.py:564
  33.9 0.3 more_adjoint.1.one_ref
  34.2 0.4 collective-permute-start
  34.5 2.3 %collective-permute-done.1.other_ref = f32[2,16,384]{2,1,0:T(8,128)S(1)} collective-permute-done((f32[2,16,384]{2,1,0:T(8,128)S(1)}, f32[2,16,384]{2,1,0:T(8,128)S(1)}, u32[]{:S(2)}, u32[]{:S(2)}) %collective-permute-start.1) | collective-permute-done | bytes 49184 | tf_op jit(solution)/shard_map/ppermute | solution.py:564
  36.9 0.9 %forward_adjoint.2 = (f32[16,128]{1,0:T(8,128)S(1)}, f32[2,16,384]{2,1,0:T(8,128)S(1)}, bf16[2,16,384]{2,1,0:T(8,128)(2,1)S(1)}) custom-call(bf16[8,2,392,128]{3,2,1,0:T(8,128)(2,1)S(1)} %bitcast.5, f32[2,16,384]{2,1,0:T(8,128)S(1)} %get-tuple-element.15.one_ref, f32[2,16,384]{2,1,0:T(8,128)S(1)} %collective-permute-done.1.other_ref, ...), custom_call_target="tpu_custom_call" | custom-call | tf_op jit(solution)/shard_map/forward_adjoint/pallas_call | solution.py:594
  37.8 1.9 %collective-permute-done.other_ref = f32[2,16,384]{2,1,0:T(8,128)S(1)} collective-permute-done((f32[2,16,384]{2,1,0:T(8,128)S(1)}, f32[2,16,384]{2,1,0:T(8,128)S(1)}, u32[]{:S(2)}, u32[]{:S(2)}) %collective-permute-start) | collective-permute-done | bytes 49184 | tf_op jit(solution)/shard_map/ppermute | solution.py:564
  39.7 0.0 copy-start
  39.7 0.0 copy-start.1
  39.7 0.9 %forward_adjoint.3 = (f32[32,128]{1,0:T(8,128)S(1)}, f32[2,32,384]{2,1,0:T(8,128)S(1)}, bf16[2,32,384]{2,1,0:T(8,128)(2,1)S(1)}) custom-call(bf16[8,2,392,128]{3,2,1,0:T(8,128)(2,1)S(1)} %bitcast.6, f32[2,16,384]{2,1,0:T(8,128)S(1)} %more_adjoint.1.one_ref, f32[2,16,384]{2,1,0:T(8,128)S(1)} %collective-permute-done.other_ref, ...), custom_call_target="tpu_custom_call" | custom-call | tf_op jit(solution)/shard_map/forward_adjoint/pallas_call | solution.py:594
  40.7 0.3 collective-permute-start.2
  41.0 4.8 %collective-permute-done.2.other_ref = bf16[2,32,384]{2,1,0:T(8,128)(2,1)S(1)} collective-permute-done((bf16[2,32,384]{2,1,0:T(8,128)(2,1)S(1)}, bf16[2,32,384]{2,1,0:T(8,128)(2,1)S(1)}, u32[]{:S(2)}, u32[]{:S(2)}) %collective-permute-start.2) | collective-permute-done | bytes 49184 | tf_op jit(solution)/shard_map/ppermute | solution.py:564
  45.7 1.1 %last_forward.1 = f32[16,4,128]{2,1,0:T(4,128)S(1)} custom-call(bf16[8,2,392,128]{3,2,1,0:T(8,128)(2,1)S(1)} %bitcast.7, f32[2,32,384]{2,1,0:T(8,128)S(1)} %get-tuple-element.19.one_ref, bf16[2,32,384]{2,1,0:T(8,128)(2,1)S(1)} %collective-permute-done.2.other_ref, f32[32,128]{1,0:T(8,128)S(1)} %get-tuple-element.21.residual_ref, ...), custom_call_target="tpu_custom_call" | custom-call | tf_op jit(solution)/shard_map/last_forward/pallas_call | solution.py:601
  46.9 8.2 %all_to_all.11.got_ref = f32[16,4,128]{2,1,0:T(4,128)S(1)} all-to-all(f32[16,4,128]{2,1,0:T(4,128)S(1)} %last_forward.1), channel_id=1, replica_groups=mesh['top'=2,'low'=8,'par'=2] {'low','par'}, dimensions={0} | all-to-all | bytes 65536 | tf_op jit(solution)/shard_map/all_to_all | solution.py:607
  55.1 0.0 copy-done
  55.1 0.0 copy-done.1
  55.1 1.0 %to_time.1 = (f32[2,8,256]{2,1,0:T(8,128)}, f32[2,8,256]{2,1,0:T(8,128)}) custom-call(f32[16,4,128]{2,1,0:T(4,128)S(1)} %all_to_all.11.got_ref, bf16[3,256,256]{2,1,0:T(8,128)(2,1)S(1)} %copy-done, f32[1,8]{1,0:T(1,128)S(1)} %bitcast.9), custom_call_target="tpu_custom_call" | custom-call | tf_op jit(solution)/shard_map/to_time/pallas_call | solution.py:609
Async XLA Ops:
  31.3 5.6 %collective-permute-start.1 = (f32[2,16,384]{2,1,0:T(8,128)S(1)}, f32[2,16,384]{2,1,0:T(8,128)S(1)}, u32[]{:S(2)}, u32[]{:S(2)}) collective-permute-start(f32[2,16,384]{2,1,0:T(8,128)S(1)} %get-tuple-element.15.one_ref), channel_id=1, source_target_pairs={{0,16},{16,0},{1,17},{17,1},{2,18},{18,2},{3,19},{19,3},{4,20},{20... | collective-permute-start | bytes 147464 | tf_op jit(solution)/shard_map/ppermute | solution.py:564
  34.2 5.5 %collective-permute-start = (f32[2,16,384]{2,1,0:T(8,128)S(1)}, f32[2,16,384]{2,1,0:T(8,128)S(1)}, u32[]{:S(2)}, u32[]{:S(2)}) collective-permute-start(f32[2,16,384]{2,1,0:T(8,128)S(1)} %more_adjoint.1.one_ref), channel_id=1, source_target_pairs={{0,16},{16,0},{1,17},{17,1},{2,18},{18,2},{3,19},{19,3},{4,20},{20... | collective-permute-start | bytes 147464 | tf_op jit(solution)/shard_map/ppermute | solution.py:564
  39.7 15.4 %copy-start = (bf16[3,256,256]{2,1,0:T(8,128)(2,1)S(1)}, bf16[3,256,256]{2,1,0:T(8,128)(2,1)}, u32[]{:S(2)}) copy-start(bf16[3,256,256]{2,1,0:T(8,128)(2,1)} %constant.5.clone.basis_ref) | copy-start | bytes 1179652
  39.7 15.4 %copy-start.1 = (f32[8]{0:T(128)S(1)}, f32[8]{0:T(128)}, u32[]{:S(2)}) copy-start(f32[8]{0:T(128)} %param.11) | copy-start | bytes 100
  40.7 5.1 %collective-permute-start.2 = (bf16[2,32,384]{2,1,0:T(8,128)(2,1)S(1)}, bf16[2,32,384]{2,1,0:T(8,128)(2,1)S(1)}, u32[]{:S(2)}, u32[]{:S(2)}) collective-permute-start(bf16[2,32,384]{2,1,0:T(8,128)(2,1)S(1)} %get-tuple-element.20), channel_id=1, source_target_pairs={{0,16},{16,0},{1,17},{17,1},{2,18},{18,2},{3,19},{19,3},{4,20},{20... | collective-permute-start | bytes 147464 | tf_op jit(solution)/shard_map/ppermute | solution.py:564
